TPU v7x, 32 devices: a whole 2x2x4 slice. The times are simulated.
32 devices in a mesh: dp: 4 (over y, core), fsdp: 8 (over z, x).
Axes of the slice: x: 2, y: 2, z: 4, core: 2. Of those that a mesh axis runs over, the one named last changes fastest.
Arguments:
- latents: bfloat16 [32, 384, 1536], P(('dp', 'fsdp')), may hold values from -6 to 6
- context: bfloat16 [32, 128, 768], P(('dp', 'fsdp')), may hold values from -6 to 6
- timestep: bfloat16 [32, 1536], P(('dp', 'fsdp')), may hold values from -6 to 6
- lengths: int32 [32], P(('dp', 'fsdp')), may hold values from 21 to 384, as said below
- cotangent: bfloat16 [32, 384, 1536], P(('dp', 'fsdp')), may hold values from -6 to 6
- mod_matrix: float32 [1536, 9216], P(('dp', 'fsdp')), may hold values from -0.25515518 to 0.25515518
- mod_first: float32 [1536, 9216], P(('dp', 'fsdp')), may hold values from -16 to 16
- mod_second: float32 [1536, 9216], P(('dp', 'fsdp')), may hold values from 0.73728 to 2.94912
- qkv_matrix: float32 [1536, 4608], P(('dp', 'fsdp')), may hold values from -0.09021098 to 0.09021098
- qkv_first: float32 [1536, 4608], P(('dp', 'fsdp')), may hold values from -16 to 16
- qkv_second: float32 [1536, 4608], P(('dp', 'fsdp')), may hold values from 0.73728 to 2.94912
- square_set: float32 [3, 1536, 1536], P(None, ('dp', 'fsdp')), may hold values from -2.8867513 to 2.8867513
- square_first: float32 [3, 1536, 1536], P(None, ('dp', 'fsdp')), may hold values from -16 to 16
- square_second: float32 [3, 1536, 1536], P(None, ('dp', 'fsdp')), may hold values from 0.73728 to 2.94912
- ctx_matrix: float32 [768, 3072], P(('dp', 'fsdp')), may hold values from -0.12757759 to 0.12757759
- ctx_first: float32 [768, 3072], P(('dp', 'fsdp')), may hold values from -16 to 16
- ctx_second: float32 [768, 3072], P(('dp', 'fsdp')), may hold values from 0.73728 to 2.94912
- ff_in: float32 [1536, 12288], P(('dp', 'fsdp')), may hold values from -0.25515518 to 0.25515518
- in_first: float32 [1536, 12288], P(('dp', 'fsdp')), may hold values from -16 to 16
- in_second: float32 [1536, 12288], P(('dp', 'fsdp')), may hold values from 0.73728 to 2.94912
- ff_down: float32 [6144, 1536], P(('dp', 'fsdp')), may hold values from -0.12757759 to 0.12757759
- down_first: float32 [6144, 1536], P(('dp', 'fsdp')), may hold values from -16 to 16
- down_second: float32 [6144, 1536], P(('dp', 'fsdp')), may hold values from 0.73728 to 2.94912
- norm_gains: float32 [3, 1536], P(None, ('dp', 'fsdp')), may hold values from 0.25 to 3.2
- gains_first: float32 [3, 1536], P(None, ('dp', 'fsdp')), may hold values from -16 to 16
- gains_second: float32 [3, 1536], P(None, ('dp', 'fsdp')), may hold values from 0.73728 to 2.94912
Outputs:
- block_out: bfloat16 [32, 384, 1536], P(('dp', 'fsdp'))
- latents_grad: bfloat16 [32, 384, 1536], P(('dp', 'fsdp'))
- mod_matrix_new: float32 [1536, 9216], P(('dp', 'fsdp'))
- mod_first_new: float32 [1536, 9216], P(('dp', 'fsdp'))
- mod_second_new: float32 [1536, 9216], P(('dp', 'fsdp'))
- qkv_matrix_new: float32 [1536, 4608], P(('dp', 'fsdp'))
- qkv_first_new: float32 [1536, 4608], P(('dp', 'fsdp'))
- qkv_second_new: float32 [1536, 4608], P(('dp', 'fsdp'))
- square_set_new: float32 [3, 1536, 1536], P(None, ('dp', 'fsdp'))
- square_first_new: float32 [3, 1536, 1536], P(None, ('dp', 'fsdp'))
- square_second_new: float32 [3, 1536, 1536], P(None, ('dp', 'fsdp'))
- ctx_matrix_new: float32 [768, 3072], P(('dp', 'fsdp'))
- ctx_first_new: float32 [768, 3072], P(('dp', 'fsdp'))
- ctx_second_new: float32 [768, 3072], P(('dp', 'fsdp'))
- ff_in_new: float32 [1536, 12288], P(('dp', 'fsdp'))
- in_first_new: float32 [1536, 12288], P(('dp', 'fsdp'))
- in_second_new: float32 [1536, 12288], P(('dp', 'fsdp'))
- ff_down_new: float32 [6144, 1536], P(('dp', 'fsdp'))
- down_first_new: float32 [6144, 1536], P(('dp', 'fsdp'))
- down_second_new: float32 [6144, 1536], P(('dp', 'fsdp'))
- norm_gains_new: float32 [3, 1536], P(None, ('dp', 'fsdp'))
- gains_first_new: float32 [3, 1536], P(None, ('dp', 'fsdp'))
- gains_second_new: float32 [3, 1536], P(None, ('dp', 'fsdp'))
- weight_norms: float32 [9], replicated
- update_norms: float32 [9], replicated
- stream_rms: float32 [4], replicated
Inputs may be any that keep to these rules, and one draw needn't show every extreme that they name: `lengths`: the last clip is full.
All inputs are finite; a program needn't handle non-finite values.
Results may differ from a plain program's by a relative error of at most 0.018.
The roundings to bfloat16 on the way count: a program that leaves them out, or rounds other values in their place, can miss the bound.
Values may be sent and summed in bfloat16 or wider, within the bound.
A program may use at most 512 MiB of HBM per device.

v0:
```python
import jax
import jax.numpy as jnp
from jax import lax
from jax.sharding import PartitionSpec as P

D = 1536
HEAD_DIM = 64
FF = 6144
STEP = 10


NORM_EPS = 1e-05
BETA_ONE = 0.9
BETA_TWO = 0.999
ADAM_EPS = 1e-06
DECAY = 0.01
RATE = 0.5
SCALE = 0.125


def norm_rows(matrix):
    centred = matrix - jnp.mean(matrix, axis=-1, keepdims=True)
    inverse = lax.rsqrt(jnp.mean(centred * centred, axis=-1, keepdims=True) + NORM_EPS)
    return (centred * inverse, inverse)


def norm_back(gradient, normed, inverse):
    return inverse * (
        gradient
        - jnp.mean(gradient, axis=-1, keepdims=True)
        - normed * jnp.mean(gradient * normed, axis=-1, keepdims=True)
    )


def score_block(queries, key_rows, usable):
    scores = (
        jnp.einsum("qhe,khe->hqk", queries, key_rows, preferred_element_type=jnp.float32) * SCALE
    )
    return jnp.where(usable[None, None, :], scores, -1e30)


def attend_forward(queries, key_rows, values, usable):
    scores = score_block(queries, key_rows, usable)
    ceiling = jnp.max(scores, axis=-1, keepdims=True)
    powers = jnp.exp(scores - ceiling)
    totals = jnp.sum(powers, axis=-1, keepdims=True)
    chances = (powers / totals).astype(jnp.bfloat16)
    mixture = jnp.einsum("hqk,khe->qhe", chances, values, preferred_element_type=jnp.float32)
    return (mixture.reshape(mixture.shape[0], -1).astype(jnp.bfloat16), ceiling + jnp.log(totals))


def attend_backward(queries, key_rows, values, usable, log_total, d_mixture):
    scores = score_block(queries, key_rows, usable)
    chances = jnp.exp(scores - log_total)
    d_heads = d_mixture.reshape(queries.shape)
    d_values = jnp.einsum(
        "hqk,qhe->khe", chances.astype(jnp.bfloat16), d_heads, preferred_element_type=jnp.float32
    )
    d_chances = jnp.einsum("qhe,khe->hqk", d_heads, values, preferred_element_type=jnp.float32)
    d_scores = (
        chances * (d_chances - jnp.sum(chances * d_chances, axis=-1, keepdims=True))
    ).astype(jnp.bfloat16)
    d_queries = (
        jnp.einsum("hqk,khe->qhe", d_scores, key_rows, preferred_element_type=jnp.float32) * SCALE
    )
    d_key_rows = (
        jnp.einsum("hqk,qhe->khe", d_scores, queries, preferred_element_type=jnp.float32) * SCALE
    )
    return (d_queries, d_key_rows, d_values)


def forward_clip(stream_row, context_row, timestep_row, valid_count, weights):
    mod_matrix, qkv_matrix, square_set, ctx_matrix, ff_in, ff_down, norm_gains = weights
    frame_count = stream_row.shape[0]
    head_count = qkv_matrix.shape[1] // (3 * HEAD_DIM)
    gain_rows = norm_gains.astype(jnp.float32)
    lifted = jax.nn.silu(timestep_row.astype(jnp.float32)).astype(jnp.bfloat16)
    shifts = jnp.dot(lifted[None, :], mod_matrix, preferred_element_type=jnp.float32).reshape(6, -1)
    usable = jnp.arange(frame_count) < valid_count
    stream = stream_row.astype(jnp.float32)
    normed_one, inverse_one = norm_rows(stream)
    entry_attn = (normed_one * gain_rows[0] * (1.0 + shifts[1]) + shifts[0]).astype(jnp.bfloat16)
    qkv = (
        jnp.dot(entry_attn, qkv_matrix, preferred_element_type=jnp.float32)
        .astype(jnp.bfloat16)
        .reshape(frame_count, 3, head_count, HEAD_DIM)
    )
    mixture_attn, log_attn = attend_forward(qkv[:, 0], qkv[:, 1], qkv[:, 2], usable)
    branch_attn = jnp.dot(mixture_attn, square_set[0], preferred_element_type=jnp.float32)
    after_attn = stream + shifts[2] * branch_attn
    normed_two, inverse_two = norm_rows(after_attn)
    entry_cross = (normed_two * gain_rows[1]).astype(jnp.bfloat16)
    query_cross = (
        jnp.dot(entry_cross, square_set[1], preferred_element_type=jnp.float32)
        .astype(jnp.bfloat16)
        .reshape(frame_count, head_count, HEAD_DIM)
    )
    kv_cross = (
        jnp.dot(context_row, ctx_matrix, preferred_element_type=jnp.float32)
        .astype(jnp.bfloat16)
        .reshape(context_row.shape[0], 2, head_count, HEAD_DIM)
    )
    everywhere = jnp.arange(context_row.shape[0]) >= 0
    mixture_cross, log_cross = attend_forward(
        query_cross, kv_cross[:, 0], kv_cross[:, 1], everywhere
    )
    branch_cross = jnp.dot(mixture_cross, square_set[2], preferred_element_type=jnp.float32)
    after_cross = after_attn + branch_cross
    normed_three, inverse_three = norm_rows(after_cross)
    entry_ffn = (normed_three * gain_rows[2] * (1.0 + shifts[4]) + shifts[3]).astype(jnp.bfloat16)
    gate_up = jnp.dot(entry_ffn, ff_in, preferred_element_type=jnp.float32)
    gate_part = gate_up[:, :FF]
    up_part = gate_up[:, FF:]
    hidden = (jax.nn.silu(gate_part) * up_part).astype(jnp.bfloat16)
    branch_ffn = jnp.dot(hidden, ff_down, preferred_element_type=jnp.float32)
    result = after_cross + shifts[5] * branch_ffn
    keep_rows = usable.astype(jnp.float32)[:, None]
    branches = (result, shifts[2] * branch_attn, branch_cross, shifts[5] * branch_ffn)
    stream_terms = jnp.stack([jnp.sum(keep_rows * branch * branch) for branch in branches])
    kept_state = (
        lifted,
        shifts,
        usable,
        normed_one,
        inverse_one,
        entry_attn,
        qkv,
        mixture_attn,
        log_attn,
        branch_attn,
        normed_two,
        inverse_two,
        entry_cross,
        query_cross,
        kv_cross,
        everywhere,
        mixture_cross,
        log_cross,
        normed_three,
        inverse_three,
        entry_ffn,
        gate_part,
        up_part,
        hidden,
        branch_ffn,
        gain_rows,
        context_row,
    )
    return (result, stream_terms, kept_state)


def backward_clip(kept_state, weights, d_result):
    (
        lifted,
        shifts,
        usable,
        normed_one,
        inverse_one,
        entry_attn,
        qkv,
        mixture_attn,
        log_attn,
        branch_attn,
        normed_two,
        inverse_two,
        entry_cross,
        query_cross,
        kv_cross,
        everywhere,
        mixture_cross,
        log_cross,
        normed_three,
        inverse_three,
        entry_ffn,
        gate_part,
        up_part,
        hidden,
        branch_ffn,
        gain_rows,
        context_row,
    ) = kept_state
    mod_matrix, qkv_matrix, square_set, ctx_matrix, ff_in, ff_down, norm_gains = weights
    frame_count = d_result.shape[0]
    d_branch_ffn = (d_result * shifts[5]).astype(jnp.bfloat16)
    d_gate_ffn = jnp.sum(d_result * branch_ffn, axis=0)
    grad_down = jnp.einsum("lf,ld->fd", hidden, d_branch_ffn, preferred_element_type=jnp.float32)
    d_hidden = jnp.einsum("ld,fd->lf", d_branch_ffn, ff_down, preferred_element_type=jnp.float32)
    logistic = jax.nn.sigmoid(gate_part)
    d_gate_up = jnp.concatenate(
        [
            d_hidden * up_part * logistic * (1.0 + gate_part * (1.0 - logistic)),
            d_hidden * gate_part * logistic,
        ],
        axis=1,
    ).astype(jnp.bfloat16)
    grad_in = jnp.einsum("ld,lf->df", entry_ffn, d_gate_up, preferred_element_type=jnp.float32)
    d_entry_ffn = jnp.einsum("lf,df->ld", d_gate_up, ff_in, preferred_element_type=jnp.float32)
    d_gain_ffn = jnp.sum(d_entry_ffn * normed_three * (1.0 + shifts[4]), axis=0)
    d_scale_ffn = jnp.sum(d_entry_ffn * normed_three * gain_rows[2], axis=0)
    d_shift_ffn = jnp.sum(d_entry_ffn, axis=0)
    d_after_cross = d_result + norm_back(
        d_entry_ffn * gain_rows[2] * (1.0 + shifts[4]), normed_three, inverse_three
    )
    d_branch_cross = d_after_cross.astype(jnp.bfloat16)
    grad_cross = jnp.einsum(
        "ld,le->de", mixture_cross, d_branch_cross, preferred_element_type=jnp.float32
    )
    d_mixture_cross = jnp.einsum(
        "le,de->ld", d_branch_cross, square_set[2], preferred_element_type=jnp.float32
    ).astype(jnp.bfloat16)
    d_query_cross, d_key_cross, d_value_cross = attend_backward(
        query_cross, kv_cross[:, 0], kv_cross[:, 1], everywhere, log_cross, d_mixture_cross
    )
    d_kv_cross = (
        jnp.stack([d_key_cross, d_value_cross], axis=1)
        .reshape(kv_cross.shape[0], -1)
        .astype(jnp.bfloat16)
    )
    grad_ctx = jnp.einsum("ce,cf->ef", context_row, d_kv_cross, preferred_element_type=jnp.float32)
    d_query_rows = d_query_cross.reshape(frame_count, -1).astype(jnp.bfloat16)
    grad_query = jnp.einsum(
        "ld,le->de", entry_cross, d_query_rows, preferred_element_type=jnp.float32
    )
    d_entry_cross = jnp.einsum(
        "le,de->ld", d_query_rows, square_set[1], preferred_element_type=jnp.float32
    )
    d_gain_cross = jnp.sum(d_entry_cross * normed_two, axis=0)
    d_after_attn = d_after_cross + norm_back(d_entry_cross * gain_rows[1], normed_two, inverse_two)
    d_branch_attn = (d_after_attn * shifts[2]).astype(jnp.bfloat16)
    d_gate_attn = jnp.sum(d_after_attn * branch_attn, axis=0)
    grad_out = jnp.einsum(
        "ld,le->de", mixture_attn, d_branch_attn, preferred_element_type=jnp.float32
    )
    d_mixture_attn = jnp.einsum(
        "le,de->ld", d_branch_attn, square_set[0], preferred_element_type=jnp.float32
    ).astype(jnp.bfloat16)
    d_queries, d_key_rows, d_values = attend_backward(
        qkv[:, 0], qkv[:, 1], qkv[:, 2], usable, log_attn, d_mixture_attn
    )
    d_qkv = (
        jnp.stack([d_queries, d_key_rows, d_values], axis=1)
        .reshape(frame_count, -1)
        .astype(jnp.bfloat16)
    )
    grad_qkv = jnp.einsum("ld,lf->df", entry_attn, d_qkv, preferred_element_type=jnp.float32)
    d_entry_attn = jnp.einsum("lf,df->ld", d_qkv, qkv_matrix, preferred_element_type=jnp.float32)
    d_gain_attn = jnp.sum(d_entry_attn * normed_one * (1.0 + shifts[1]), axis=0)
    d_scale_attn = jnp.sum(d_entry_attn * normed_one * gain_rows[0], axis=0)
    d_shift_attn = jnp.sum(d_entry_attn, axis=0)
    d_latents = d_after_attn + norm_back(
        d_entry_attn * gain_rows[0] * (1.0 + shifts[1]), normed_one, inverse_one
    )
    d_shifts = jnp.concatenate(
        [d_shift_attn, d_scale_attn, d_gate_attn, d_shift_ffn, d_scale_ffn, d_gate_ffn]
    ).astype(jnp.bfloat16)
    grad_mod = jnp.einsum("d,m->dm", lifted, d_shifts, preferred_element_type=jnp.float32)
    grad_square = jnp.stack([grad_out, grad_query, grad_cross])
    grad_gains = jnp.stack([d_gain_attn, d_gain_cross, d_gain_ffn])
    return (d_latents, (grad_mod, grad_qkv, grad_square, grad_ctx, grad_in, grad_down, grad_gains))


def shards(
    latents,
    context,
    timestep,
    lengths,
    cotangent,
    mod_matrix,
    mod_first,
    mod_second,
    qkv_matrix,
    qkv_first,
    qkv_second,
    square_set,
    square_first,
    square_second,
    ctx_matrix,
    ctx_first,
    ctx_second,
    ff_in,
    in_first,
    in_second,
    ff_down,
    down_first,
    down_second,
    norm_gains,
    gains_first,
    gains_second,
):
    masters = (mod_matrix, qkv_matrix, square_set, ctx_matrix, ff_in, ff_down, norm_gains)
    firsts = (mod_first, qkv_first, square_first, ctx_first, in_first, down_first, gains_first)
    seconds = (
        mod_second,
        qkv_second,
        square_second,
        ctx_second,
        in_second,
        down_second,
        gains_second,
    )
    gathered = (
        lax.all_gather(mod_matrix.astype(jnp.bfloat16), ("dp", "fsdp"), axis=0, tiled=True),
        lax.all_gather(qkv_matrix.astype(jnp.bfloat16), ("dp", "fsdp"), axis=0, tiled=True),
        lax.all_gather(square_set.astype(jnp.bfloat16), ("dp", "fsdp"), axis=1, tiled=True),
        lax.all_gather(ctx_matrix.astype(jnp.bfloat16), ("dp", "fsdp"), axis=0, tiled=True),
        lax.all_gather(ff_in.astype(jnp.bfloat16), ("dp", "fsdp"), axis=0, tiled=True),
        lax.all_gather(ff_down.astype(jnp.bfloat16), ("dp", "fsdp"), axis=0, tiled=True),
        lax.all_gather(norm_gains.astype(jnp.bfloat16), ("dp", "fsdp"), axis=1, tiled=True),
    )
    position = 0
    result, clip_terms, kept_state = forward_clip(
        latents[position], context[position], timestep[position], lengths[position], gathered
    )
    results = [result.astype(jnp.bfloat16)]
    states = [kept_state]
    count_term = jnp.sum(lengths).astype(jnp.float32)
    stream_total, count_total = lax.psum((clip_terms, count_term), ("dp", "fsdp"))
    back_weights = (
        lax.all_gather(mod_matrix.astype(jnp.bfloat16), ("dp", "fsdp"), axis=0, tiled=True),
        lax.all_gather(qkv_matrix.astype(jnp.bfloat16), ("dp", "fsdp"), axis=0, tiled=True),
        lax.all_gather(square_set.astype(jnp.bfloat16), ("dp", "fsdp"), axis=1, tiled=True),
        lax.all_gather(ctx_matrix.astype(jnp.bfloat16), ("dp", "fsdp"), axis=0, tiled=True),
        lax.all_gather(ff_in.astype(jnp.bfloat16), ("dp", "fsdp"), axis=0, tiled=True),
        lax.all_gather(ff_down.astype(jnp.bfloat16), ("dp", "fsdp"), axis=0, tiled=True),
        lax.all_gather(norm_gains.astype(jnp.bfloat16), ("dp", "fsdp"), axis=1, tiled=True),
    )
    position = 0
    frame_count = latents.shape[1]
    live_rows = (jnp.arange(frame_count) < lengths[position]).astype(jnp.float32)[:, None]
    d_latents, own_grads = backward_clip(
        states[position], back_weights, cotangent[position].astype(jnp.float32) * live_rows
    )
    d_rows = [d_latents.astype(jnp.bfloat16)]
    summed = (
        lax.psum_scatter(own_grads[0], ("dp", "fsdp"), scatter_dimension=0, tiled=True),
        lax.psum_scatter(own_grads[1], ("dp", "fsdp"), scatter_dimension=0, tiled=True),
        lax.psum_scatter(own_grads[2], ("dp", "fsdp"), scatter_dimension=1, tiled=True),
        lax.psum_scatter(own_grads[3], ("dp", "fsdp"), scatter_dimension=0, tiled=True),
        lax.psum_scatter(own_grads[4], ("dp", "fsdp"), scatter_dimension=0, tiled=True),
        lax.psum_scatter(own_grads[5], ("dp", "fsdp"), scatter_dimension=0, tiled=True),
        lax.psum_scatter(own_grads[6], ("dp", "fsdp"), scatter_dimension=1, tiled=True),
    )
    pending = []
    weight_parts = []
    update_parts = []
    for weight, first_moment, second_moment, gradient in zip(masters, firsts, seconds, summed):
        first_new = BETA_ONE * first_moment + (1.0 - BETA_ONE) * gradient
        second_new = BETA_TWO * second_moment + (1.0 - BETA_TWO) * gradient * gradient
        direction = (
            first_new
            / (1.0 - BETA_ONE**STEP)
            / (jnp.sqrt(second_new / (1.0 - BETA_TWO**STEP)) + ADAM_EPS)
            + DECAY * weight
        )
        reduce_axes = (1, 2) if weight.ndim == 3 else None
        weight_parts.append(jnp.sum(weight * weight, axis=reduce_axes).reshape(-1))
        update_parts.append(jnp.sum(direction * direction, axis=reduce_axes).reshape(-1))
        pending.append((weight, direction, first_new, second_new))
    weight_squares = jnp.concatenate(weight_parts)
    update_squares = jnp.concatenate(update_parts)
    weight_total, update_total = lax.psum((weight_squares, update_squares), ("dp", "fsdp"))
    weight_norms = jnp.sqrt(weight_total)
    update_norms = jnp.sqrt(update_total)
    ratios = weight_norms / update_norms
    outputs = [jnp.stack(results), jnp.stack(d_rows)]
    cursor = 0
    for weight, direction, first_new, second_new in pending:
        if weight.ndim == 3:
            factor = ratios[cursor : cursor + weight.shape[0]].reshape(-1, 1, 1)
            cursor = cursor + weight.shape[0]
        else:
            factor = ratios[cursor]
            cursor = cursor + 1
        outputs.append(weight - RATE * factor * direction)
        outputs.append(first_new)
        outputs.append(second_new)
    stream_rms = jnp.sqrt(stream_total / (count_total * D))
    outputs.append(weight_norms)
    outputs.append(update_norms)
    outputs.append(stream_rms)
    return tuple(outputs)


def solution(mesh):
    in_specs = (
        P(("dp", "fsdp"), None, None),
        P(("dp", "fsdp"), None, None),
        P(("dp", "fsdp"), None),
        P(("dp", "fsdp")),
        P(("dp", "fsdp"), None, None),
        P(("dp", "fsdp"), None),
        P(("dp", "fsdp"), None),
        P(("dp", "fsdp"), None),
        P(("dp", "fsdp"), None),
        P(("dp", "fsdp"), None),
        P(("dp", "fsdp"), None),
        P(None, ("dp", "fsdp"), None),
        P(None, ("dp", "fsdp"), None),
        P(None, ("dp", "fsdp"), None),
        P(("dp", "fsdp"), None),
        P(("dp", "fsdp"), None),
        P(("dp", "fsdp"), None),
        P(("dp", "fsdp"), None),
        P(("dp", "fsdp"), None),
        P(("dp", "fsdp"), None),
        P(("dp", "fsdp"), None),
        P(("dp", "fsdp"), None),
        P(("dp", "fsdp"), None),
        P(None, ("dp", "fsdp")),
        P(None, ("dp", "fsdp")),
        P(None, ("dp", "fsdp")),
    )
    out_specs = (
        P(("dp", "fsdp"), None, None),
        P(("dp", "fsdp"), None, None),
        P(("dp", "fsdp"), None),
        P(("dp", "fsdp"), None),
        P(("dp", "fsdp"), None),
        P(("dp", "fsdp"), None),
        P(("dp", "fsdp"), None),
        P(("dp", "fsdp"), None),
        P(None, ("dp", "fsdp"), None),
        P(None, ("dp", "fsdp"), None),
        P(None, ("dp", "fsdp"), None),
        P(("dp", "fsdp"), None),
        P(("dp", "fsdp"), None),
        P(("dp", "fsdp"), None),
        P(("dp", "fsdp"), None),
        P(("dp", "fsdp"), None),
        P(("dp", "fsdp"), None),
        P(("dp", "fsdp"), None),
        P(("dp", "fsdp"), None),
        P(("dp", "fsdp"), None),
        P(None, ("dp", "fsdp")),
        P(None, ("dp", "fsdp")),
        P(None, ("dp", "fsdp")),
        P(),
        P(),
        P(),
    )
    return jax.shard_map(shards, mesh=mesh, in_specs=in_specs, out_specs=out_specs, check_vma=False)
```

profile of v0, /device:TPU:0, one launch (start us, length us, event | category | flops | bytes accessed | tf_op | source)
XLA Modules:
  0.0 3324.9 jit_solution(11234631549501804248)
XLA Ops:
  19.4 69.8 %all-gather = bf16[32,48,3]{1,2,0:T(4,128)(2,1)S(1)} all-gather(bf16[1,48,3]{1,2,0:T(4,128)(2,1)S(1)} %convert_bitcast_fusion.2), channel_id=1, replica_groups=mesh['dp'=4,'fsdp'=8] {'dp','fsdp'}, dimensions={0}, use_global_device_ids=true | all-gather | bytes 9504 | tf_op jit(solution)/shard_map/all_gather | solution.py:308
  93.9 156.4 %all-gather.8.cloned.1.call-done = bf16[1536,9216]{1,0:T(8,128)(2,1)} async-done(((bf16[48,9216]{1,0:T(8,128)(2,1)}), bf16[1536,9216]{1,0:T(8,128)(2,1)}) %all-gather.8.cloned.1.call-update) | async-done | bytes 28311568 | tf_op jit(solution)/shard_map/all_gather | solution.py:302
  250.3 11.0 fusion.125
  261.3 93.9 %all-gather.10.cloned.1.call-done = bf16[1536,4608]{1,0:T(8,128)(2,1)} async-done(((bf16[48,4608]{1,0:T(8,128)(2,1)}), bf16[1536,4608]{1,0:T(8,128)(2,1)}) %all-gather.10.cloned.1.call-update) | async-done | bytes 14155792 | tf_op jit(solution)/shard_map/all_gather | solution.py:303
  355.3 12.3 convolution_convert_fusion
  373.6 10.1 fusion.124
  383.6 7.8 fusion
  391.4 9.1 fusion.62
  400.6 59.7 %all-gather.12.cloned.1.call-done = bf16[3,1536,1536]{2,1,0:T(8,128)(2,1)} async-done(((bf16[3,48,1536]{2,1,0:T(8,128)(2,1)}), bf16[3,1536,1536]{2,1,0:T(8,128)(2,1)}) %all-gather.12.cloned.1.call-update) | async-done | bytes 14155792 | tf_op jit(solution)/shard_map/all_gather | solution.py:304
  488.9 187.9 %all-gather.16.cloned.1.call-done = bf16[1536,12288]{1,0:T(8,128)(2,1)} async-done(((bf16[48,12288]{1,0:T(8,128)(2,1)}), bf16[1536,12288]{1,0:T(8,128)(2,1)}) %all-gather.16.cloned.1.call-update) | async-done | bytes 37748752 | tf_op jit(solution)/shard_map/all_gather | solution.py:306
  676.8 26.9 fusion.109
  703.7 99.4 %all-gather.18.cloned.1.call-done = bf16[6144,1536]{1,0:T(8,128)(2,1)} async-done(((bf16[192,1536]{1,0:T(8,128)(2,1)}), bf16[6144,1536]{1,0:T(8,128)(2,1)}) %all-gather.18.cloned.1.call-update) | async-done | bytes 18874384 | tf_op jit(solution)/shard_map/all_gather | solution.py:307
  803.1 23.1 multiply_convert_fusion.2
  826.2 27.7 fusion.7
  853.9 17.8 fusion.44
  911.8 9.2 fusion.59
  921.0 14.1 multiply_reduce_fusion
  949.9 12.1 multiply_reduce_fusion.5
  968.4 9.6 copy.145
  988.7 9.6 pad_maximum_fusion
  999.6 15.0 fusion.75
  1015.9 18.7 fusion.96
  1036.4 18.3 broadcast_multiply_fusion
  1056.4 37.3 %fusion.6 = f32[1536,12288]{1,0:T(8,128)} fusion(bf16[384,6144]{1,0:T(8,128)(2,1)} %get-tuple-element.173, bf16[384,6144]{1,0:T(8,128)(2,1)} %get-tuple-element.172, f32[384,1536]{1,0:T(8,128)S(1)} %copy-done.5, f32[1536]{0:T(1024)S(1)} %copy-done.57, f32[1536]{0:T(1024)S(1)} %copy-done.49, f32[1536]{0:T(1024)S(1)} %copy-done.51, f32[384]{0:T(512)S(1)} %copy-done.55, ...), kind=kOutput, calls=%fused_computation.23 | convolution fusion | flops 14517927936 | bytes 87315456 | tf_op jit(solution)/shard_map/ld,lf->df/dot_general | solution.py:196
  1098.8 98.9 %reduce-scatter.22.cloned.1.call-done = f32[24,3072]{1,0:T(8,128)} async-done(((f32[768,3072]{1,0:T(8,128)}), f32[24,3072]{1,0:T(8,128)}) %reduce-scatter.22.cloned.1.call-update) | async-done | bytes 294928 | tf_op jit(solution)/shard_map/reduce_scatter | solution.py:338
  1200.3 265.9 %reduce-scatter.16.cloned.1.call-done = f32[3,48,1536]{2,1,0:T(8,128)} async-done(((f32[3,1536,1536]{2,1,0:T(8,128)}), f32[3,48,1536]{2,1,0:T(8,128)}) %reduce-scatter.16.cloned.1.call-update) | async-done | bytes 884752 | tf_op jit(solution)/shard_map/reduce_scatter | solution.py:337
  1469.6 267.6 %reduce-scatter.14.cloned.1.call-done = f32[48,4608]{1,0:T(8,128)} async-done(((f32[1536,4608]{1,0:T(8,128)}), f32[48,4608]{1,0:T(8,128)}) %reduce-scatter.14.cloned.1.call-update) | async-done | bytes 884752 | tf_op jit(solution)/shard_map/reduce_scatter | solution.py:336
  1741.4 351.8 %reduce-scatter.20.cloned.1.call-done = f32[192,1536]{1,0:T(8,128)} async-done(((f32[6144,1536]{1,0:T(8,128)}), f32[192,1536]{1,0:T(8,128)}) %reduce-scatter.20.cloned.1.call-update) | async-done | bytes 1179664 | tf_op jit(solution)/shard_map/reduce_scatter | solution.py:340
  2097.8 474.5 %reduce-scatter.12.cloned.1.call-done = f32[48,9216]{1,0:T(8,128)} async-done(((f32[1536,9216]{1,0:T(8,128)}), f32[48,9216]{1,0:T(8,128)}) %reduce-scatter.12.cloned.1.call-update) | async-done | bytes 1769488 | tf_op jit(solution)/shard_map/reduce_scatter | solution.py:335
  2579.2 656.7 %reduce-scatter.18.cloned.1.call-done = f32[48,12288]{1,0:T(8,128)} async-done(((f32[1536,12288]{1,0:T(8,128)}), f32[48,12288]{1,0:T(8,128)}) %reduce-scatter.18.cloned.1.call-update) | async-done | bytes 2359312 | tf_op jit(solution)/shard_map/reduce_scatter | solution.py:339
  3235.8 7.8 multiply_reduce_fusion.6
  3256.1 39.7 %all-reduce = (f32[9]{0:T(128)S(1)}, f32[9]{0:T(128)S(1)}, f32[4]{0:T(128)S(1)}, f32[]{:T(128)}) all-reduce(f32[9]{0:T(128)S(1)} %concatenate.15, f32[9]{0:T(128)S(1)} %concatenate.17, f32[4]{0:T(128)S(1)} %pad_maximum_fusion.6, f32[]{:T(128)S(6)} %convert_element_type.236), channel_id=1, replica_groups=mesh['dp'=4,'fsdp'=8] {'dp','fsdp'}, use_global_device_ids=true, to_apply=%region_25.26 | all-reduce | flops 23 | bytes 184 | tf_op jit(solution)/shard_map/psum | solution.py:361
  (307 shorter events, 184.5 us)
Async XLA Ops:
  7.2 83.0 %all-gather.14.cloned.1.call-start = ((), (), s32[]{:S(2)}) async-start(), calls=%async_computation.10 | async-start | bytes 4866048 | tf_op jit(solution)/shard_map/all_gather | solution.py:305
  9.0 241.2 %all-gather.8.cloned.1.call-start = ((), (), s32[]{:S(2)}) async-start(), calls=%async_computation.7 | async-start | bytes 29196288 | tf_op jit(solution)/shard_map/all_gather | solution.py:302
  11.6 343.7 %all-gather.10.cloned.1.call-start = ((), (), s32[]{:S(2)}) async-start(), calls=%async_computation.8 | async-start | bytes 14598144 | tf_op jit(solution)/shard_map/all_gather | solution.py:303
  12.5 447.8 %all-gather.12.cloned.1.call-start = ((), (), s32[]{:S(2)}) async-start(), calls=%async_computation.9 | async-start | bytes 14598144 | tf_op jit(solution)/shard_map/all_gather | solution.py:304
  14.5 662.3 %all-gather.16.cloned.1.call-start = ((), (), s32[]{:S(2)}) async-start(), calls=%async_computation.11 | async-start | bytes 38928384 | tf_op jit(solution)/shard_map/all_gather | solution.py:306
  15.7 787.4 %all-gather.18.cloned.1.call-start = ((), (), s32[]{:S(2)}) async-start(), calls=%async_computation.12 | async-start | bytes 19464192 | tf_op jit(solution)/shard_map/all_gather | solution.py:307
  18.0 1078.8 %reduce-scatter.24.cloned.1.call-start = ((), (), s32[]{:S(2)}) async-start(), calls=%async_computation.19 | async-start | bytes 811008
  89.4 265.8 %copy-start.62 = (f32[1536]{0:T(1024)}, f32[1536]{0:T(1024)S(1)}, u32[]{:S(2)}) copy-start(f32[1536]{0:T(1024)S(1)} %get-tuple-element.140) | copy-start | bytes 18436
  89.4 782.3 %copy-start.50 = (f32[1536]{0:T(1024)}, f32[1536]{0:T(1024)S(1)}, u32[]{:S(2)}) copy-start(f32[1536]{0:T(1024)S(1)} %get-tuple-element.138) | copy-start | bytes 18436
  89.7 265.6 %copy-start.68 = (f32[384]{0:T(512)}, f32[384]{0:T(512)S(1)}, u32[]{:S(2)}) copy-start(f32[384]{0:T(512)S(1)} %broadcast_multiply_fusion.9) | copy-start | bytes 4612
  90.2 265.1 %copy-start.70 = (f32[384]{0:T(512)}, f32[384]{0:T(512)S(1)}, u32[]{:S(2)}) copy-start(f32[384]{0:T(512)S(1)} %add_rsqrt_fusion.2) | copy-start | bytes 4612
  261.3 106.3 %copy-start.60 = (f32[1536]{0:T(1024)}, f32[1536]{0:T(1024)S(1)}, u32[]{:S(2)}) copy-start(f32[1536]{0:T(1024)S(1)} %get-tuple-element.180) | copy-start | bytes 18436
  261.3 106.3 %copy-start.64 = (f32[1536]{0:T(1024)}, f32[1536]{0:T(1024)S(1)}, u32[]{:S(2)}) copy-start(f32[1536]{0:T(1024)S(1)} %get-tuple-element.179) | copy-start | bytes 18436
  261.3 198.9 %copy-start.66 = (f32[1536]{0:T(1024)}, f32[1536]{0:T(1024)S(1)}, u32[]{:S(2)}) copy-start(f32[1536]{0:T(1024)S(1)} %get-tuple-element.181) | copy-start | bytes 18436
  261.3 415.5 %copy-start.56 = (f32[1536]{0:T(1024)}, f32[1536]{0:T(1024)S(1)}, u32[]{:S(2)}) copy-start(f32[1536]{0:T(1024)S(1)} %get-tuple-element.177) | copy-start | bytes 18436
  261.3 610.4 %copy-start.48 = (f32[1536]{0:T(1024)}, f32[1536]{0:T(1024)S(1)}, u32[]{:S(2)}) copy-start(f32[1536]{0:T(1024)S(1)} %get-tuple-element.178) | copy-start | bytes 18436
  487.1 384.7 %copy-start.52 = (f32[384]{0:T(512)}, f32[384]{0:T(512)S(1)}, u32[]{:S(2)}) copy-start(f32[384]{0:T(512)S(1)} %broadcast_multiply_fusion.7) | copy-start | bytes 4612
  488.9 382.9 %copy-start.54 = (f32[384]{0:T(512)}, f32[384]{0:T(512)S(1)}, u32[]{:S(2)}) copy-start(f32[384]{0:T(512)S(1)} %add_rsqrt_fusion) | copy-start | bytes 4612
  963.3 234.5 %reduce-scatter.22.cloned.1.call-start = ((), (), s32[]{:S(2)}) async-start(), calls=%async_computation.18 | async-start | bytes 9732096 | tf_op jit(solution)/shard_map/reduce_scatter | solution.py:338
  978.1 488.1 %reduce-scatter.16.cloned.1.call-start = ((), (), s32[]{:S(2)}) async-start(), calls=%async_computation.15 | async-start | bytes 29196288 | tf_op jit(solution)/shard_map/reduce_scatter | solution.py:337
  998.3 738.9 %reduce-scatter.14.cloned.1.call-start = ((), (), s32[]{:S(2)}) async-start(), calls=%async_computation.14 | async-start | bytes 29196288 | tf_op jit(solution)/shard_map/reduce_scatter | solution.py:336
  1014.6 1078.6 %reduce-scatter.20.cloned.1.call-start = ((), (), s32[]{:S(2)}) async-start(), calls=%async_computation.17 | async-start | bytes 38928384 | tf_op jit(solution)/shard_map/reduce_scatter | solution.py:340
  1034.7 1537.6 %reduce-scatter.12.cloned.1.call-start = ((), (), s32[]{:S(2)}) async-start(), calls=%async_computation.13 | async-start | bytes 58392576 | tf_op jit(solution)/shard_map/reduce_scatter | solution.py:335
  1054.8 2181.0 %reduce-scatter.18.cloned.1.call-start = ((), (), s32[]{:S(2)}) async-start(), calls=%async_computation.16 | async-start | bytes 77856768 | tf_op jit(solution)/shard_map/reduce_scatter | solution.py:339
  1093.8 103.9 %copy-start.39 = (f32[24,3072]{1,0:T(8,128)S(1)}, f32[24,3072]{1,0:T(8,128)}, u32[]{:S(2)}) copy-start(f32[24,3072]{1,0:T(8,128)} %param.40) | copy-start | bytes 884740
  1093.8 103.9 %copy-start.58 = (f32[24,3072]{1,0:T(8,128)S(1)}, f32[24,3072]{1,0:T(8,128)}, u32[]{:S(2)}) copy-start(f32[24,3072]{1,0:T(8,128)} %param.41) | copy-start | bytes 884740
  1093.8 372.4 %copy-start.26 = (f32[3,48,1536]{2,1,0:T(8,128)S(1)}, f32[3,48,1536]{2,1,0:T(8,128)}, u32[]{:S(2)}) copy-start(f32[3,48,1536]{2,1,0:T(8,128)} %param.37) | copy-start | bytes 2654212
  1093.9 372.4 %copy-start.47 = (f32[3,48,1536]{2,1,0:T(8,128)S(1)}, f32[3,48,1536]{2,1,0:T(8,128)}, u32[]{:S(2)}) copy-start(f32[3,48,1536]{2,1,0:T(8,128)} %param.38) | copy-start | bytes 2654212
  1200.3 536.9 %copy-start.25 = (f32[48,4608]{1,0:T(8,128)S(1)}, f32[48,4608]{1,0:T(8,128)}, u32[]{:S(2)}) copy-start(f32[48,4608]{1,0:T(8,128)} %param.34) | copy-start | bytes 2654212
  1469.6 623.7 %copy-start.19 = (f32[192,1536]{1,0:T(8,128)S(1)}, f32[192,1536]{1,0:T(8,128)}, u32[]{:S(2)}) copy-start(f32[192,1536]{1,0:T(8,128)} %param.46) | copy-start | bytes 3538948
  1469.6 623.7 %copy-start.46 = (f32[192,1536]{1,0:T(8,128)S(1)}, f32[192,1536]{1,0:T(8,128)}, u32[]{:S(2)}) copy-start(f32[192,1536]{1,0:T(8,128)} %param.47) | copy-start | bytes 3538948
  2097.8 1138.0 %copy-start.7 = (f32[48,12288]{1,0:T(8,128)S(1)}, f32[48,12288]{1,0:T(8,128)}, u32[]{:S(2)}) copy-start(f32[48,12288]{1,0:T(8,128)} %param.43) | copy-start | bytes 7077892
  (70 other events, 601.9 us)
Sparse Core Ops, SparseCore 0:
  11.6 66.4 all-gather.13
  81.7 168.5 all-gather.7
  253.8 101.3 all-gather.9
  358.8 101.4 all-gather.11
  463.6 213.1 all-gather.15
  680.2 122.8 all-gather.17
  963.4 93.6 reduce-scatter.23
  1063.0 134.6 reduce-scatter.21
  1205.3 260.8 reduce-scatter.15
  1473.6 263.5 reduce-scatter.13
  1744.8 348.4 reduce-scatter.19
  2099.5 472.7 reduce-scatter.11
  2579.9 655.9 reduce-scatter.17
where the time goes:
time: 3330 us; the launch traced here: 3320 us
  waiting for transfers between devices  2710 us (81%)
  matrix products  318 us (10%)
  other arithmetic  114 us (3%)
  blocking collectives  109 us (3%)
  local copies, waits for them, and re-layouts  48.4 us (1%)
    reduce_scatter x1, waiting for transfers between devices, shards(): lax.psum_scatter(own_grads[4], ('dp', 'fsdp'), scatter_dimension=0, tiled...  657 us
    reduce_scatter x1, waiting for transfers between devices, shards(): lax.psum_scatter(own_grads[0], ('dp', 'fsdp'), scatter_dimension=0, tiled...  474 us
    reduce_scatter x1, waiting for transfers between devices, shards(): lax.psum_scatter(own_grads[5], ('dp', 'fsdp'), scatter_dimension=0, tiled...  352 us
    reduce_scatter x1, waiting for transfers between devices, shards(): lax.psum_scatter(own_grads[1], ('dp', 'fsdp'), scatter_dimension=0, tiled...  268 us
    reduce_scatter x1, waiting for transfers between devices, shards(): lax.psum_scatter(own_grads[2], ('dp', 'fsdp'), scatter_dimension=1, tiled...  266 us
    all_gather x1, waiting for transfers between devices, shards(): lax.all_gather(ff_in.astype(jnp.bfloat16), ('dp', 'fsdp'), axis=0, tiled=...  188 us
    all_gather x1, waiting for transfers between devices, shards(): lax.all_gather(mod_matrix.astype(jnp.bfloat16), ('dp', 'fsdp'), axis=0, t...  156 us
    all_gather x1, waiting for transfers between devices, shards(): lax.all_gather(ff_down.astype(jnp.bfloat16), ('dp', 'fsdp'), axis=0, tile...  99.4 us
  transfers between devices with their start and end apart: 13, of which 11 were waited for; matrix products, arithmetic and copies ran while one was open for 8% of the time, Pallas kernels for 0%

commit v1 on v0

v1 whole, which is shorter than its diff:
```python
import functools
import itertools

import jax
import jax.numpy as jnp
from jax import lax
from jax.experimental import pallas as pl
from jax.experimental.pallas import tpu as pltpu
from jax.sharding import Mesh, PartitionSpec as P

D = 1536
HEAD_DIM = 64
FF = 6144
STEP = 10


NORM_EPS = 1e-05
BETA_ONE = 0.9
BETA_TWO = 0.999
ADAM_EPS = 1e-06
DECAY = 0.01
RATE = 0.5
SCALE = 0.125

AXES = ("y", "c", "z", "x")
HALF = D // 2
PAIR = 2 * HEAD_DIM
BF16 = jnp.bfloat16
F32 = jnp.float32
ANY = pl.BlockSpec(memory_space=pl.ANY)
WHOLE = pl.BlockSpec(memory_space=pltpu.VMEM)
SCALARS = pl.BlockSpec(memory_space=pltpu.SMEM)


def norm_rows(matrix):
    centred = matrix - jnp.mean(matrix, axis=-1, keepdims=True)
    inverse = lax.rsqrt(jnp.mean(centred * centred, axis=-1, keepdims=True) + NORM_EPS)
    return (centred * inverse, inverse)


def norm_back(gradient, normed, inverse):
    return inverse * (
        gradient
        - jnp.mean(gradient, axis=-1, keepdims=True)
        - normed * jnp.mean(gradient * normed, axis=-1, keepdims=True)
    )


def dot(first, second):
    return jnp.dot(first, second, preferred_element_type=F32)


def dot_back(first, second):
    return lax.dot_general(first, second, (((1,), (1,)), ((), ())), preferred_element_type=F32)


def dot_rows(first, second):
    return lax.dot_general(first, second, (((0,), (0,)), ((), ())), preferred_element_type=F32)


def pick(array, index, axis):
    return lax.dynamic_index_in_dim(array, index, axis, keepdims=False)


def total(terms):
    return sum(term.astype(F32) for term in terms)


def only(block, head):
    lane = lax.broadcasted_iota(jnp.int32, block.shape, 1)
    mine = lane < HEAD_DIM if head == 0 else lane >= HEAD_DIM
    return jnp.where(mine, block, jnp.zeros_like(block))


def both_heads(first, second):
    lane = lax.broadcasted_iota(jnp.int32, first.shape, 1)
    return jnp.where(lane < HEAD_DIM, first, second)


def attend_kernel(valid_ref, query_ref, key_ref, value_ref, out_ref):
    valid = valid_ref[pl.program_id(0)]
    query, key, value = query_ref[...], key_ref[...], value_ref[...]
    mixed = []
    for head in range(2):
        scores = dot_back(only(query, head), key) * SCALE
        column = lax.broadcasted_iota(jnp.int32, scores.shape, 1)
        scores = jnp.where(column < valid, scores, -1e30)
        powers = jnp.exp(scores - jnp.max(scores, axis=-1, keepdims=True))
        chances = (powers / jnp.sum(powers, axis=-1, keepdims=True)).astype(BF16)
        mixed.append(dot(chances, value))
    out_ref[...] = both_heads(*mixed).astype(BF16)


def attend_back_kernel(
    valid_ref, query_ref, key_ref, value_ref, d_ref, d_query_ref, d_key_ref, d_value_ref
):
    valid = valid_ref[pl.program_id(0)]
    query, key, value, d_mix = query_ref[...], key_ref[...], value_ref[...], d_ref[...]
    parts = []
    for head in range(2):
        scores = dot_back(only(key, head), query) * SCALE
        row = lax.broadcasted_iota(jnp.int32, scores.shape, 0)
        scores = jnp.where(row < valid, scores, -1e30)
        powers = jnp.exp(scores - jnp.max(scores, axis=0, keepdims=True))
        chances = powers / jnp.sum(powers, axis=0, keepdims=True)
        d_chances = dot_back(only(value, head), d_mix)
        mean = jnp.sum(chances * d_chances, axis=0, keepdims=True)
        d_scores = (chances * (d_chances - mean)).astype(BF16)
        d_value = dot(chances.astype(BF16), d_mix)
        d_key = dot(d_scores, query) * SCALE
        d_query = dot_rows(d_scores, key) * SCALE
        parts.append((d_query, d_key, d_value))
    for out_ref, first, second in zip((d_query_ref, d_key_ref, d_value_ref), *parts):
        out_ref[...] = both_heads(first, second).astype(BF16)


def block_of(rows, row_shift, column_shift):
    return pl.BlockSpec((rows, PAIR), lambda b, j: (b + row_shift, j + column_shift))


def attend(valid, query, key, value):
    frames, words = query[1], key[1]
    pairs = HALF // PAIR
    return pl.pallas_call(
        attend_kernel,
        out_shape=jax.ShapeDtypeStruct((2 * frames, HALF), BF16),
        grid=(2, pairs),
        in_specs=[SCALARS] + [block_of(*part[1:]) for part in (query, key, value)],
        out_specs=block_of(frames, 0, 0),
        compiler_params=pltpu.CompilerParams(vmem_limit_bytes=32 * 2**20),
        cost_estimate=pl.CostEstimate(
            flops=32 * pairs * frames * words * PAIR,
            bytes_accessed=8 * (frames + words) * HALF,
            transcendentals=4 * pairs * frames * words,
        ),
    )(valid, query[0], key[0], value[0])


def attend_back(valid, query, key, value, d_mixture):
    frames, words = query[1], key[1]
    pairs = HALF // PAIR
    return pl.pallas_call(
        attend_back_kernel,
        out_shape=[
            jax.ShapeDtypeStruct((2 * rows, HALF), BF16) for rows in (frames, words, words)
        ],
        grid=(2, pairs),
        in_specs=[SCALARS]
        + [block_of(*part[1:]) for part in (query, key, value)]
        + [block_of(frames, 0, 0)],
        out_specs=[block_of(rows, 0, 0) for rows in (frames, words, words)],
        compiler_params=pltpu.CompilerParams(vmem_limit_bytes=48 * 2**20),
        cost_estimate=pl.CostEstimate(
            flops=80 * pairs * frames * words * PAIR,
            bytes_accessed=12 * (frames + words) * HALF,
            transcendentals=4 * pairs * frames * words,
        ),
    )(valid, query[0], key[0], value[0], d_mixture)


def copy_all(copies):
    for copy in copies:
        copy.start()
    for copy in copies:
        copy.wait()


def place_pieces(spot_ref, *refs, plan, sizes):
    ny, nb = sizes
    count = len(plan["offsets"]) * len(plan["parts"])
    pieces, outs, sem = refs[:count], refs[count:-1], refs[-1]
    y, x = spot_ref[0], spot_ref[3]
    copies = []
    for part, blocks in enumerate(plan["parts"]):
        for spot, (dy, dx) in enumerate(plan["offsets"]):
            from_y = lax.rem(y - dy + ny, ny)
            from_x = lax.rem(x - dx + nb, nb)
            piece = pieces[part * len(plan["offsets"]) + spot]
            for block, (out, lane, column, width) in enumerate(blocks):
                columns = pl.ds(column, width)
                if lane is None:
                    target = outs[out].at[from_y, :, from_x, :, columns]
                else:
                    target = outs[out].at[from_y, lane, :, from_x, :, columns]
                copies.append(
                    pltpu.make_async_copy(piece.at[:, block], target, sem.at[len(copies)])
                )
    copy_all(copies)


def place_ranks(spot_ref, lines_ref, in_ref, down_ref, sem, *, offsets, sizes, rows, depth):
    ny, na, nb = sizes
    y, c, x = spot_ref[0], spot_ref[1], spot_ref[3]
    copies = []
    for block, (dy, dc, dx) in enumerate(offsets):
        target = in_ref.at[
            lax.rem(y - dy + ny, ny), lax.rem(c + dc, 2), :, lax.rem(x - dx + nb, nb)
        ]
        source = lines_ref.at[:, pl.ds(block * rows, rows)]
        copies.append(pltpu.make_async_copy(source, target, sem.at[len(copies)]))
    source = lines_ref.at[:, pl.ds(len(offsets) * rows, depth)]
    copies.append(pltpu.make_async_copy(source, down_ref, sem.at[len(copies)]))
    copy_all(copies)


def place_columns(spot_ref, pieces_ref, out_ref, sem, *, offsets, sizes, width):
    ny, nb = sizes
    y, c, x = spot_ref[0], spot_ref[1], spot_ref[3]
    copies = []
    for k, (dy, dc, dx) in enumerate(offsets):
        rank = (lax.rem(y - dy + ny, ny) * 2 + lax.rem(c + dc, 2)) * nb + lax.rem(x - dx + nb, nb)
        for half in range(2):
            start = pl.multiple_of(half * FF + rank * width, 128)
            copies.append(
                pltpu.make_async_copy(
                    pieces_ref.at[k, :, pl.ds(half * width, width)],
                    out_ref.at[:, pl.ds(start, width)],
                    sem.at[len(copies)],
                )
            )
    copy_all(copies)


def place(kernel, spot, arrays, shapes, copies):
    size = sum(a.size * a.dtype.itemsize for a in arrays)
    return pl.pallas_call(
        kernel,
        out_shape=[jax.ShapeDtypeStruct(shape, BF16) for shape in shapes],
        in_specs=[SCALARS] + [ANY] * len(arrays),
        out_specs=[WHOLE] * len(shapes),
        scratch_shapes=[pltpu.SemaphoreType.DMA((copies,))],
        compiler_params=pltpu.CompilerParams(vmem_limit_bytes=40 * 2**20),
        cost_estimate=pl.CostEstimate(flops=0, bytes_accessed=2 * size, transcendentals=0),
    )(spot, *arrays)


def prepare_kernel(
    spot_ref, qkv_ref, square_ref, ctx_ref, in_ref, own_ref, other_ref, wide_ref, block_ref,
    *, offsets, sizes
):
    ny, nb = sizes
    y, c, x = spot_ref[0], spot_ref[1], spot_ref[3]
    part = D // (2 * ny)
    for out_ref, which in ((own_ref, c), (other_ref, 1 - c)):
        for k in range(5):
            for block in range(ny):
                start = block * 2 * part + which * part
                if k < 3:
                    values = qkv_ref[:, pl.ds(pl.multiple_of(k * D + start, part), part)]
                elif k == 3:
                    values = square_ref[1, :, pl.ds(pl.multiple_of(start, part), part)]
                else:
                    values = jnp.concatenate(
                        [
                            ctx_ref[:, pl.ds(pl.multiple_of(side * D + start, part), part)]
                            for side in range(2)
                        ]
                    )
                out_ref[k, :, block * part : (block + 1) * part] = values.astype(BF16)
    for k, matrix in enumerate((0, 2)):
        for side in range(2):
            values = square_ref[matrix, :, side * HALF : (side + 1) * HALF]
            wide_ref[2 * k + side] = values.astype(BF16)
    width = FF // len(offsets)
    for k, (dy, dc, dx) in enumerate(offsets):
        rank = (lax.rem(y + dy, ny) * 2 + lax.rem(c + dc, 2)) * nb + lax.rem(x + dx, nb)
        for side in range(2):
            start = pl.multiple_of(side * FF + rank * width, width)
            block_ref[k, :, side * width : (side + 1) * width] = in_ref[
                :, pl.ds(start, width)
            ].astype(BF16)


class Grid:
    def __init__(self, mesh):
        self.ny = mesh.shape["dp"] // 2
        self.nb = 2
        self.na = mesh.shape["fsdp"] // 2
        self.sizes = dict(y=self.ny, c=2, z=self.na, x=self.nb)
        self.count = self.ny * 2 * self.na * self.nb
        self.spots = list(itertools.product(*(range(self.sizes[axis]) for axis in AXES)))
        self.peers = list(itertools.product(range(self.ny), range(2), range(self.nb)))
        self.mesh = Mesh(mesh.devices.reshape(self.ny, 2, self.na, self.nb), AXES)

    def line(self, y, c, z, x):
        return ((y * 2 + c) * self.na + z) * self.nb + x

    def here(self):
        return {axis: lax.axis_index(axis) for axis in AXES}

    def move(self, array, **steps):
        steps = {axis: step % self.sizes[axis] for axis, step in steps.items()}
        steps = {axis: step for axis, step in steps.items() if step}
        if not steps:
            return array
        names = tuple(axis for axis in AXES if axis in steps)
        lengths = [self.sizes[axis] for axis in names]
        pairs = []
        for spot in itertools.product(*(range(n) for n in lengths)):
            source = target = 0
            for axis, at, n in zip(names, spot, lengths):
                source, target = source * n + at, target * n + (at + steps[axis]) % n
            pairs.append((source, target))
        return lax.ppermute(array, names, pairs)

    def rank(self, mine, offset):
        y, c, x = ((mine[axis] + step) % self.sizes[axis] for axis, step in zip("ycx", offset))
        return (y * 2 + c) * self.nb + x

    def swap(self, array):
        return self.move(array, c=1)

    def gather_small(self, array):
        shape = array.shape
        for axis in "xzcy":
            parts = [self.move(array, **{axis: k}) for k in range(self.sizes[axis])]
            array = jnp.concatenate([part.reshape((-1,) + shape) for part in parts])
        return array

    def scatter_small(self, array):
        sources = [array]
        for axis in "cyxz":
            where = 0
            arrays = []
            size = self.sizes[axis]
            sources = [s.reshape(self.small_shape(axis, s)) for s in sources]
            for k in range(1, size):
                part = total([s[:, k] for s in sources])
                arrays.append(self.move(part, **{axis: -k}))
            sources = [s[:, 0] for s in sources] + arrays
        return total(sources).reshape(array.shape[1:])

    def small_shape(self, axis, array):
        before = {"c": self.ny, "y": 1, "x": self.na, "z": 1}[axis]
        return (before, self.sizes[axis], -1, array.shape[-1])

    def sum_small(self, array):
        bit = 1
        while bit < self.count:
            array = array + lax.ppermute(array, AXES, [(d, d ^ bit) for d in range(self.count)])
            bit *= 2
        return array

    def spread(self, lines, turn):
        held = {(0, 0): lines}
        for axis in ("x", "y") if turn else ("y", "x"):
            for (y, x), piece in list(held.items()):
                for k in range(1, self.sizes[axis]):
                    step = dict(y=y, x=x)
                    step[axis] = k
                    held[(step["y"], step["x"])] = self.move(piece, **{axis: k})
        return held

    def gather_weights(self, parts, shapes, mine, spot):
        rows = parts[0][0][0].shape[0]
        mixed = jnp.stack([shard for part in parts for shard, *_ in part])
        lines = lax.all_gather(mixed, "z")
        start = 0
        held, plan = [], dict(parts=[])
        for turn, part in enumerate(parts):
            end = start + len(part)
            held.append(self.spread(lines[:, start:end], turn))
            start = end
            plan["parts"].append(
                [(out, lane, column, shard.shape[1]) for shard, out, lane, column in part]
            )
        plan["offsets"] = sorted(held[0])
        if rows % 16 == 0:
            arrays = [pieces[offset] for pieces in held for offset in plan["offsets"]]
            copies = len(plan["offsets"]) * sum(len(part) for part in parts)
            kernel = functools.partial(place_pieces, plan=plan, sizes=(self.ny, self.nb))
            return place(kernel, spot, arrays, shapes, copies)
        outs = [jnp.zeros(shape, BF16) for shape in shapes]
        for pieces, blocks in zip(held, plan["parts"]):
            for (dy, dx), piece in pieces.items():
                y = (mine["y"] - dy + self.ny) % self.ny
                x = (mine["x"] - dx + self.nb) % self.nb
                for block, (out, lane, column, width) in enumerate(blocks):
                    update = piece[:, block][None, :, None]
                    if lane is None:
                        at = (y, 0, x, 0, column)
                    else:
                        update = update[:, None]
                        at = (y, lane, 0, x, 0, column)
                    outs[out] = lax.dynamic_update_slice(outs[out], update, at)
        return outs

    def swap_ranks(self, blocks):
        shape = blocks.shape[1:]
        blocks = blocks.reshape((self.ny, 2, self.nb) + shape)
        for where, axis in ((1, "c"), (0, "y"), (2, "x")):
            parts = [
                self.move(lax.index_in_dim(blocks, k, where), **{axis: k})
                for k in range(self.sizes[axis])
            ]
            blocks = jnp.concatenate(parts, axis=where)
        return blocks.reshape((-1,) + shape)

    def gather_ranks(self, in_parts, down_part, mine, spot):
        peers, rows, width = in_parts.shape
        depth = down_part.shape[0]
        in_shape = (self.ny, 2, self.na, self.nb, rows, width)
        down_shape = (self.na, depth, D)
        if rows % 16 == 0 and width == D:
            mixed = jnp.concatenate([in_parts.reshape(-1, D), down_part])
            lines = lax.all_gather(mixed, "z")
            kernel = functools.partial(
                place_ranks,
                offsets=self.peers,
                sizes=(self.ny, self.na, self.nb),
                rows=rows,
                depth=depth,
            )
            rank_in, rank_down = place(kernel, spot, [lines], [in_shape, down_shape], peers + 1)
        else:
            rank_down = lax.all_gather(down_part, "z")
            lines = lax.all_gather(in_parts, "z")
            rank_in = jnp.zeros(in_shape, BF16)
            for k, (dy, dc, dx) in enumerate(self.peers):
                at = ((mine["y"] - dy) % self.ny, (mine["c"] + dc) % 2, 0, (mine["x"] - dx) % self.nb, 0, 0)
                rank_in = lax.dynamic_update_slice(rank_in, lines[:, k][None, None, :, None], at)
        return rank_in.reshape(-1, width), rank_down.reshape(-1, D)

    def join_columns(self, pieces, mine, spot):
        peers, rows, width = pieces.shape
        width = width // 2
        if rows % 16 == 0:
            kernel = functools.partial(
                place_columns, offsets=self.peers, sizes=(self.ny, self.nb), width=width
            )
            return place(kernel, spot, [pieces], [(rows, 2 * FF)], 2 * peers)[0]
        out = jnp.zeros((rows, 2, FF), BF16)
        for k, (dy, dc, dx) in enumerate(self.peers):
            y, x = (mine["y"] - dy) % self.ny, (mine["x"] - dx) % self.nb
            rank = (y * 2 + (mine["c"] + dc) % 2) * self.nb + x
            piece = pieces[k].reshape(rows, 2, width)
            out = lax.dynamic_update_slice(out, piece, (0, 0, rank * width))
        return out.reshape(rows, 2 * FF)

    def fold(self, array, turn, mine):
        names = "ycz"[: array.ndim - 3] if array.ndim == 6 else "yz"
        names = list(names + "x")
        sources = [array]
        for axis in "yx" if turn else "xy":
            where = names.index(axis)
            size = self.sizes[axis]
            arrived = []
            for k in range(1, size):
                away = total([pick(s, (mine[axis] + k) % size, where) for s in sources])
                arrived.append(self.move(away.astype(BF16), **{axis: k}))
            sources = [pick(s, mine[axis], where) for s in sources] + arrived
            names.remove(axis)
        out = total(sources).astype(BF16)
        return out if names[0] == "z" else jnp.swapaxes(out, 0, 1)

    def gather_rows(self, array):
        held = {}
        for y in range(self.ny):
            for x in range(self.nb):
                held[(y, 0, x)] = self.move(array, y=y, x=x)
                held[(y, 1, x)] = self.swap(held[(y, 0, x)])
        return held

    def scatter_rows(self, held):
        sources = []
        for (y, x), (own, other) in held.items():
            terms = [own, self.swap(other.astype(BF16))]
            if y or x:
                sources.append(self.move(total(terms).astype(BF16), y=-y, x=-x))
            else:
                sources += terms
        return total(sources)

    def to_rank(self, array, back=False):
        pairs = []
        for d in range(self.count):
            rank, z = divmod(d, self.na)
            y, c, x = self.peers[rank]
            pairs.append((d, self.line(y, c, z, x)))
        if back:
            pairs = [(b, a) for a, b in pairs]
        return lax.ppermute(array, AXES, pairs)


def lamb_terms(weight, first_moment, second_moment, gradient):
    first_new = BETA_ONE * first_moment + (1.0 - BETA_ONE) * gradient
    second_new = BETA_TWO * second_moment + (1.0 - BETA_TWO) * gradient * gradient
    direction = (
        first_new
        / (1.0 - BETA_ONE**STEP)
        / (jnp.sqrt(second_new / (1.0 - BETA_TWO**STEP)) + ADAM_EPS)
        + DECAY * weight
    )
    reduce_axes = (1, 2) if weight.ndim == 3 else None
    weight_part = jnp.sum(weight * weight, axis=reduce_axes).reshape(-1)
    update_part = jnp.sum(direction * direction, axis=reduce_axes).reshape(-1)
    return (direction, first_new, second_new, weight_part, update_part)


def shards(
    grid,
    latents,
    context,
    timestep,
    lengths,
    cotangent,
    mod_matrix,
    mod_first,
    mod_second,
    qkv_matrix,
    qkv_first,
    qkv_second,
    square_set,
    square_first,
    square_second,
    ctx_matrix,
    ctx_first,
    ctx_second,
    ff_in,
    in_first,
    in_second,
    ff_down,
    down_first,
    down_second,
    norm_gains,
    gains_first,
    gains_second,
):
    mine = grid.here()
    core = mine["c"]
    spot = jnp.stack([mine[axis] for axis in AXES]).astype(jnp.int32)
    device = grid.line(*(mine[axis] for axis in AXES))
    count, ranks = grid.count, len(grid.peers)
    rows = mod_matrix.shape[0]
    frames = latents.shape[1]
    words = context.shape[1]
    valid = lengths[0]
    keep_rows = (jnp.arange(frames) < valid).astype(F32)[:, None]

    lifted = jax.nn.silu(timestep[0].astype(F32)).astype(BF16)
    notes = jnp.concatenate([lifted, norm_gains.astype(BF16).reshape(-1)])
    notes = grid.gather_small(notes)
    origin = []
    for spot_of in grid.spots:
        source = [
            (mine[axis] - step) % grid.sizes[axis] for axis, step in zip(AXES, spot_of)
        ]
        origin.append(grid.line(*source))
    origin = jnp.stack(origin)
    sorter = (jnp.arange(count)[:, None] == origin[None, :]).astype(BF16)
    gain_rows = dot(sorter, notes[:, D:])
    gain_rows = gain_rows.reshape(count, 3, rows).transpose(1, 0, 2).reshape(3, D)
    lifted_own = lax.dynamic_slice(notes, (0, device * rows), (count, rows))
    shifts = grid.scatter_small(dot(lifted_own, mod_matrix.astype(BF16))).reshape(6, D)

    width = FF // ranks
    if rows % 16 == 0 and D // (2 * grid.ny) % 128 == 0:
        prepare = functools.partial(prepare_kernel, offsets=grid.peers, sizes=(grid.ny, grid.nb))
        five = (5, rows, HALF)
        five_own, five_other, wide_low, in_blocks = pl.pallas_call(
            prepare,
            out_shape=[
                jax.ShapeDtypeStruct(shape, BF16)
                for shape in (five, five, (4, rows, HALF), (ranks, rows, 2 * width))
            ],
            in_specs=[SCALARS] + [WHOLE] * 4,
            out_specs=[WHOLE] * 4,
            compiler_params=pltpu.CompilerParams(vmem_limit_bytes=40 * 2**20),
        )(spot, qkv_matrix, square_set, ctx_matrix, ff_in)
    else:
        five = [qkv_matrix[:, k * D : (k + 1) * D] for k in range(3)] + [
            square_set[1],
            jnp.concatenate([ctx_matrix[:, :D], ctx_matrix[:, D:]]),
        ]
        five = jnp.stack(five).astype(BF16).reshape(5, rows, grid.ny, 2, -1)
        five_own = pick(five, core, 3).reshape(5, rows, HALF)
        five_other = pick(five, 1 - core, 3).reshape(5, rows, HALF)
        wide_low = jnp.stack(
            [square_set[k, :, side * HALF : (side + 1) * HALF] for k in (0, 2) for side in range(2)]
        ).astype(BF16)
        in_halves = ff_in.reshape(rows, 2, FF)
        in_blocks = jnp.stack(
            [
                lax.dynamic_slice(in_halves, (0, 0, grid.rank(mine, offset) * width), (rows, 2, width))
                for offset in grid.peers
            ]
        ).astype(BF16).reshape(ranks, rows, 2 * width)
    five_other = grid.swap(five_other)
    five_low = jnp.where(core == 0, five_own, five_other)
    five_high = jnp.where(core == 0, five_other, five_own)
    tall = (grid.ny, 2, grid.na, grid.nb, rows)
    wide = (grid.ny, grid.na, grid.nb, rows, D)
    both = lambda k, out, at: [(five_low[k], out, 0, at), (five_high[k], out, 1, at)]
    sides = lambda k, out: [
        (wide_low[2 * k], out, None, 0),
        (wide_low[2 * k + 1], out, None, HALF),
    ]
    first = both(0, 0, 0) + both(1, 0, HALF) + both(2, 0, 2 * HALF)
    (matrix_qkv,) = grid.gather_weights(
        [first[:3], first[3:]], [tall + (3 * HALF,)], mine, spot
    )
    matrix_qkv = matrix_qkv.reshape(D, 3 * HALF)
    second = [sides(0, 0) + both(3, 1, 0), both(4, 2, 0) + sides(1, 3)]
    matrix_out, matrix_query, matrix_ctx, matrix_cross = grid.gather_weights(
        second, [wide, tall + (HALF,), tall + (HALF,), wide], mine, spot
    )
    matrix_out, matrix_cross = matrix_out.reshape(HALF, D), matrix_cross.reshape(HALF, D)
    matrix_query, matrix_ctx = matrix_query.reshape(D, HALF), matrix_ctx.reshape(D, HALF)

    in_parts = grid.swap_ranks(in_blocks)
    down_part = grid.to_rank(ff_down.astype(BF16))
    rank_in, rank_down = grid.gather_ranks(in_parts, down_part, mine, spot)

    pair_lengths = jnp.concatenate([lengths, grid.swap(lengths)])
    all_words = jnp.full((2,), words, jnp.int32)
    text = jnp.concatenate([context[0], grid.swap(context[0])])
    stream = latents[0].astype(F32)
    normed_one, inverse_one = norm_rows(stream)
    entry_attn = (normed_one * gain_rows[0] * (1.0 + shifts[1]) + shifts[0]).astype(BF16)
    d_result = cotangent[0].astype(F32) * keep_rows
    d_branch_ffn = (d_result * shifts[5]).astype(BF16)

    pair = lambda array: jnp.concatenate([array, grid.swap(array)])
    unpair = lambda sums: sums[:frames] + grid.swap(sums[frames:].astype(BF16)).astype(F32)
    columns = HALF // PAIR
    entry_pair = pair(entry_attn)
    qkv = dot(entry_pair, matrix_qkv).astype(BF16)
    self_parts = tuple((qkv, frames, 0, k * columns) for k in range(3))
    mixture_attn = attend(pair_lengths, *self_parts)
    branch_attn = unpair(dot(mixture_attn, matrix_out))
    after_attn = stream + shifts[2] * branch_attn
    normed_two, inverse_two = norm_rows(after_attn)
    entry_cross = pair((normed_two * gain_rows[1]).astype(BF16))
    query_cross = dot(entry_cross, matrix_query).astype(BF16)
    blank = jnp.zeros((2 * words, count, rows // 2), BF16)
    text_cut = text.reshape(2 * words, count, rows // 2)
    text_key = jnp.concatenate([text_cut, blank], axis=-1).reshape(2 * words, -1)
    text_value = jnp.concatenate([blank, text_cut], axis=-1).reshape(2 * words, -1)
    text_both = jnp.concatenate([text_key, text_value])
    kv_cross = dot(text_both, matrix_ctx).astype(BF16)
    cross_parts = ((query_cross, frames, 0, 0), (kv_cross, words, 0, 0), (kv_cross, words, 2, 0))
    mixture_cross = attend(all_words, *cross_parts)
    branch_cross = unpair(dot(mixture_cross, matrix_cross))
    after_cross = after_attn + branch_cross
    normed_three, inverse_three = norm_rows(after_cross)
    entry_ffn = (normed_three * gain_rows[2] * (1.0 + shifts[4]) + shifts[3]).astype(BF16)

    d_branch_held = grid.gather_rows(d_branch_ffn)
    entry_held = grid.gather_rows(entry_ffn)
    branch_held, d_entry_held = {}, {}
    entry_parts, d_branch_parts, hidden_parts, d_gate_up_parts = [], [], [], []
    for y in range(grid.ny):
        for x in range(grid.nb):
            entry_part = jnp.concatenate([entry_held[(y, c, x)] for c in range(2)])
            d_branch_part = jnp.concatenate([d_branch_held[(y, c, x)] for c in range(2)])
            gate_up = dot(entry_part, rank_in)
            gate_part, up_part = gate_up[:, :width], gate_up[:, width:]
            logistic = jax.nn.sigmoid(gate_part)
            hidden = (gate_part * logistic * up_part).astype(BF16)
            d_hidden = dot_back(d_branch_part, rank_down)
            d_gate_up = jnp.concatenate(
                [
                    d_hidden * up_part * logistic * (1.0 + gate_part * (1.0 - logistic)),
                    d_hidden * gate_part * logistic,
                ],
                axis=1,
            ).astype(BF16)
            d_entry_part = dot_back(d_gate_up, rank_in)
            branch_part = dot(hidden, rank_down)
            branch_held[(y, x)] = (branch_part[:frames], branch_part[frames:])
            d_entry_held[(y, x)] = (d_entry_part[:frames], d_entry_part[frames:])
            entry_parts.append(entry_part)
            d_branch_parts.append(d_branch_part)
            hidden_parts.append(hidden)
            d_gate_up_parts.append(d_gate_up)
    d_entry_ffn = grid.scatter_rows(d_entry_held)
    branch_ffn = grid.scatter_rows(branch_held)
    grad_down = dot_rows(jnp.concatenate(hidden_parts), jnp.concatenate(d_branch_parts))
    grad_down = lax.psum_scatter(grad_down.astype(BF16), "z", tiled=True)
    grad_down = grid.to_rank(grad_down, back=True).astype(F32)
    grad_in = dot_rows(jnp.concatenate(entry_parts), jnp.concatenate(d_gate_up_parts)).astype(BF16)
    grad_in = grad_in.reshape(grid.ny, 2, grid.na, grid.nb, rows, 2 * width)
    grad_in = grad_in.transpose(2, 0, 1, 3, 4, 5).reshape(-1, 2 * width)
    grad_in = lax.psum_scatter(grad_in, "z", tiled=True)
    grad_in = grad_in.reshape(ranks, rows, 2 * width)
    by_offset = jnp.stack(
        [
            pick(grad_in, grid.rank(mine, offset), 0)
            for offset in grid.peers
        ]
    )
    grad_in = grid.join_columns(grid.swap_ranks(by_offset), mine, spot).astype(F32)

    result = after_cross + shifts[5] * branch_ffn
    branches = (result, shifts[2] * branch_attn, branch_cross, shifts[5] * branch_ffn)
    stream_terms = jnp.stack([jnp.sum(keep_rows * branch * branch) for branch in branches])

    d_gate_ffn = jnp.sum(d_result * branch_ffn, axis=0)
    d_gain_ffn = jnp.sum(d_entry_ffn * normed_three * (1.0 + shifts[4]), axis=0)
    d_scale_ffn = jnp.sum(d_entry_ffn * normed_three * gain_rows[2], axis=0)
    d_shift_ffn = jnp.sum(d_entry_ffn, axis=0)
    d_after_cross = d_result + norm_back(
        d_entry_ffn * gain_rows[2] * (1.0 + shifts[4]), normed_three, inverse_three
    )

    def join(own, other):
        lead = own.shape[:-1]
        shape = lead + (grid.ny, 1, D // (2 * grid.ny))
        own, other = own.reshape(shape), other.reshape(shape)
        low = jnp.where(core == 0, own, other)
        high = jnp.where(core == 0, other, own)
        return jnp.concatenate([low, high], axis=-2).reshape(lead + (D,))

    d_branch_cross = pair(d_after_cross.astype(BF16))
    d_mixture_cross = dot_back(d_branch_cross, matrix_cross).astype(BF16)
    grad_cross = grid.fold(
        dot_rows(mixture_cross, d_branch_cross).astype(BF16).reshape(wide), 0, mine
    )
    d_query_cross, d_key_cross, d_value_cross = attend_back(
        all_words, *cross_parts, d_mixture_cross
    )
    d_entry_cross = unpair(dot_back(d_query_cross, matrix_query))
    d_kv_cross = jnp.concatenate([d_key_cross, d_value_cross])
    grad_ctx = dot_rows(text_both, d_kv_cross).astype(BF16)
    grad_ctx = grid.fold(grad_ctx.reshape(tall + (HALF,)), 0, mine)
    grad_query = dot_rows(entry_cross, d_query_cross).astype(BF16)
    grad_query = grid.fold(grad_query.reshape(tall + (HALF,)), 1, mine)
    d_gain_cross = jnp.sum(d_entry_cross * normed_two, axis=0)
    d_after_attn = d_after_cross + norm_back(d_entry_cross * gain_rows[1], normed_two, inverse_two)
    d_branch_attn = pair((d_after_attn * shifts[2]).astype(BF16))
    d_gate_attn = jnp.sum(d_after_attn * branch_attn, axis=0)
    d_mixture_attn = dot_back(d_branch_attn, matrix_out).astype(BF16)
    grad_out = grid.fold(
        dot_rows(mixture_attn, d_branch_attn).astype(BF16).reshape(wide), 1, mine
    )
    sums = jnp.concatenate(
        [
            grad_query.reshape(grid.na, 2 * rows, HALF),
            grad_ctx.reshape(grid.na, 2 * rows, HALF),
            grad_out[..., :HALF],
            grad_out[..., HALF:],
            grad_cross[..., :HALF],
            grad_cross[..., HALF:],
        ],
        axis=1,
    )
    sums = lax.psum_scatter(sums, "z").reshape(4, 2, rows, HALF)
    narrow = sums[:2]
    narrow_own = pick(narrow, core, 1)
    narrow_other = grid.swap(pick(narrow, 1 - core, 1))
    grad_query, grad_ctx = (join(narrow_own[k], narrow_other[k]).astype(F32) for k in range(2))
    grad_ctx = jnp.concatenate([grad_ctx[: rows // 2], grad_ctx[rows // 2 :]], axis=1)
    grad_out = jnp.concatenate([sums[2, 0], sums[2, 1]], axis=1).astype(F32)
    grad_cross = jnp.concatenate([sums[3, 0], sums[3, 1]], axis=1).astype(F32)

    d_qkv = jnp.concatenate(
        attend_back(pair_lengths, *self_parts, d_mixture_attn), axis=1
    )
    cut = 3 * HALF // 2
    folded = [
        grid.fold(
            dot_rows(entry_pair, part).astype(BF16).reshape(tall + (cut,)), turn, mine
        )
        for turn, part in enumerate((d_qkv[:, :cut], d_qkv[:, cut:]))
    ]
    folded = jnp.concatenate(folded, axis=-1).reshape(grid.na, 2 * rows, 3 * HALF)
    folded = lax.psum_scatter(folded, "z").reshape(2, rows, 3 * HALF)
    qkv_own = pick(folded, core, 0)
    qkv_other = grid.swap(pick(folded, 1 - core, 0))
    grad_qkv = jnp.concatenate(
        [
            join(qkv_own[:, k * HALF : (k + 1) * HALF], qkv_other[:, k * HALF : (k + 1) * HALF])
            for k in range(3)
        ],
        axis=1,
    ).astype(F32)
    d_entry_attn = unpair(dot_back(d_qkv, matrix_qkv))
    d_gain_attn = jnp.sum(d_entry_attn * normed_one * (1.0 + shifts[1]), axis=0)
    d_scale_attn = jnp.sum(d_entry_attn * normed_one * gain_rows[0], axis=0)
    d_shift_attn = jnp.sum(d_entry_attn, axis=0)
    d_latents = d_after_attn + norm_back(
        d_entry_attn * gain_rows[0] * (1.0 + shifts[1]), normed_one, inverse_one
    )
    small = jnp.concatenate(
        [
            d_shift_attn,
            d_scale_attn,
            d_gate_attn,
            d_shift_ffn,
            d_scale_ffn,
            d_gate_ffn,
            d_gain_attn,
            d_gain_cross,
            d_gain_ffn,
        ]
    ).astype(BF16)
    small = grid.gather_small(small)
    grad_mod = dot_rows(lifted_own, small[:, : 6 * D])
    gain_sums = jnp.sum(small[:, 6 * D :].astype(F32), axis=0).reshape(3, D)
    grad_gains = lax.dynamic_slice(gain_sums, (0, device * rows), (3, rows))

    summed = (
        grad_mod,
        grad_qkv,
        jnp.stack([grad_out, grad_query, grad_cross]),
        grad_ctx,
        grad_in,
        grad_down,
        grad_gains,
    )
    masters = (mod_matrix, qkv_matrix, square_set, ctx_matrix, ff_in, ff_down, norm_gains)
    firsts = (mod_first, qkv_first, square_first, ctx_first, in_first, down_first, gains_first)
    seconds = (
        mod_second,
        qkv_second,
        square_second,
        ctx_second,
        in_second,
        down_second,
        gains_second,
    )
    pending = []
    weight_parts = []
    update_parts = []
    for weight, first_moment, second_moment, gradient in zip(masters, firsts, seconds, summed):
        direction, first_new, second_new, weight_part, update_part = lamb_terms(
            weight, first_moment, second_moment, gradient
        )
        weight_parts.append(weight_part)
        update_parts.append(update_part)
        pending.append((weight, direction, first_new, second_new))
    totals = jnp.concatenate(
        weight_parts + update_parts + [stream_terms, jnp.sum(lengths).astype(F32).reshape(1)]
    )
    totals = grid.sum_small(totals)
    weight_norms = jnp.sqrt(totals[:9])
    update_norms = jnp.sqrt(totals[9:18])
    stream_rms = jnp.sqrt(totals[18:22] / (totals[22] * D))
    ratios = weight_norms / update_norms
    outputs = [result.astype(BF16)[None], d_latents.astype(BF16)[None]]
    cursor = 0
    for weight, direction, first_new, second_new in pending:
        if weight.ndim == 3:
            factor = ratios[cursor : cursor + weight.shape[0]].reshape(-1, 1, 1)
            cursor = cursor + weight.shape[0]
        else:
            factor = ratios[cursor]
            cursor = cursor + 1
        outputs.append(weight - RATE * factor * direction)
        outputs.append(first_new)
        outputs.append(second_new)
    outputs.append(weight_norms)
    outputs.append(update_norms)
    outputs.append(stream_rms)
    return tuple(outputs)


def solution(mesh):
    grid = Grid(mesh)
    clip = P(AXES, None, None)
    row = P(AXES, None)
    square = P(None, AXES, None)
    gains = P(None, AXES)
    weights = (row,) * 6 + (square,) * 3 + (row,) * 9 + (gains,) * 3
    in_specs = (clip, clip, row, P(AXES), clip) + weights
    out_specs = (clip, clip) + weights + (P(), P(), P())
    return jax.shard_map(
        functools.partial(shards, grid),
        mesh=grid.mesh,
        in_specs=in_specs,
        out_specs=out_specs,
        check_vma=False,
    )
```

time: 3330 us -> 1050 us (0.32)
  waiting for transfers between devices: 2710 us -> 431 us
  matrix products: 318 us -> 149 us
  blocking collectives: 109 us -> 0 us
  starting transfers between devices: 0.92 us -> 96.7 us
  local copies, waits for them, and re-layouts: 48.4 us -> 144 us
  Pallas kernels: 0 us -> 67.1 us
    reduce_scatter x6 -> x4, waiting for transfers between devices: 2120 us -> 0.06 us  [the longest x1 0.02 us: shards(): folded = lax.psum_scatter(folded, 'z').reshape(2, rows, 3 * HALF)]
    all_gather x6 -> x3, waiting for transfers between devices: 597 us -> 57.6 us  [the longest x2 57.6 us: gather_weights(): lines = lax.all_gather(mixed, 'z')]
    ppermute x0 -> x96, waiting for transfers between devices: none -> 373 us  [the longest x89 368 us: move(): return lax.ppermute(array, names, pairs)]
    dot_general x33 -> x36, matrix products: 318 us -> 149 us  [the longest x9 57.9 us: dot_rows(): lax.dot_general(first, second, (((0,), (0,)), ((), ())), preferred_elemen...]
    ppermute x0 -> x96, starting transfers between devices: none -> 96.2 us  [the longest x89 78 us: move(): return lax.ppermute(array, names, pairs)]
    all_gather x1 -> x0, blocking collectives: 69.8 us -> none  [shards(): lax.all_gather(norm_gains.astype(jnp.bfloat16), ('dp', 'fsdp'), axis=1, t...]
    pallas_call x0 -> x9, Pallas kernels: none -> 67.1 us  [the longest x2 31.4 us: attend_back(): pl.pallas_call(attend_back_kernel, out_shape=[jax.ShapeDtypeStruct((2 * r...]
    unnamed x186 -> x389, local copies, waits for them, and re-layouts: 25.6 us -> 66.4 us
  transfers between devices with their start and end apart: 13 -> 103, of which waited for: 11 -> 43; matrix products, arithmetic and copies ran while one was open for 8% -> 32% of each run, Pallas kernels for 0% -> 6%
where the time goes in v1:
time: 1050 us
  waiting for transfers between devices  431 us (41%)
  matrix products  149 us (14%)
  local copies, waits for them, and re-layouts  144 us (14%)
  other arithmetic  136 us (13%)
  starting transfers between devices  96.7 us (9%)
  Pallas kernels  67.1 us (6%)
  between operations  22.4 us (2%)
    ppermute x89, waiting for transfers between devices, move(): return lax.ppermute(array, names, pairs)  368 us
    ppermute x89, starting transfers between devices, move(): return lax.ppermute(array, names, pairs)  78 us
    unnamed x389, local copies, waits for them, and re-layouts  66.4 us
    dot_general x9, matrix products, dot_rows(): lax.dot_general(first, second, (((0,), (0,)), ((), ())), preferred_elemen...  57.9 us
    all_gather x2, waiting for transfers between devices, gather_weights(): lines = lax.all_gather(mixed, 'z')  57.6 us
    dot_general x12, matrix products, dot_back(): lax.dot_general(first, second, (((1,), (1,)), ((), ())), preferred_elemen...  50.7 us
    dot_general x15, matrix products, dot(): return jnp.dot(first, second, preferred_element_type=F32)  40.5 us
    pallas_call x2, Pallas kernels, attend_back(): pl.pallas_call(attend_back_kernel, out_shape=[jax.ShapeDtypeStruct((2 * r...  31.4 us
  transfers between devices with their start and end apart: 103, of which 43 were waited for; matrix products, arithmetic and copies ran while one was open for 32% of the time, Pallas kernels for 6%

profile of v1, /device:TPU:0, one launch (start us, length us, event | category | flops | bytes accessed | tf_op | source)
XLA Modules:
  0.0 1046.2 jit_solution(7566736064671107230)
XLA Ops:
  40.1 7.1 collective-permute-done.7
  63.8 15.5 %all-gather.7.cloned.1.call-done = bf16[24,48,768]{2,1,0:T(8,128)(2,1)} async-done(((bf16[6,48,768]{2,1,0:T(8,128)(2,1)}), bf16[24,48,768]{2,1,0:T(8,128)(2,1)}) %all-gather.7.cloned.1.call-update) | async-done | bytes 1769488 | tf_op jit(solution)/shard_map/all_gather | solution.py:357
  88.6 42.1 %all-gather.9.cloned.1.call-done = bf16[32,48,768]{2,1,0:T(8,128)(2,1)} async-done(((bf16[8,48,768]{2,1,0:T(8,128)(2,1)}), bf16[32,48,768]{2,1,0:T(8,128)(2,1)}) %all-gather.9.cloned.1.call-update) | async-done | bytes 2359312 | tf_op jit(solution)/shard_map/all_gather | solution.py:357
  139.4 41.9 %collective-permute-done.17.refs_3_ = bf16[4,3,48,768]{3,2,1,0:T(8,128)(2,1)S(1)} collective-permute-done((bf16[4,3,48,768]{3,2,1,0:T(8,128)(2,1)S(1)}, bf16[4,3,48,768]{3,2,1,0:T(8,128)(2,1)S(1)}, u32[]{:S(2)}, u32[]{:S(2)}) %collective-permute-start.17) | collective-permute-done | bytes 884768 | tf_op jit(solution)/shard_map/ppermute | solution.py:304
  188.3 6.6 convolution_convert_fusion.2.query_ref.key_ref.value_ref
  195.0 14.4 %shard_map.451 = bf16[768,768]{1,0:T(8,128)(2,1)S(1)} custom-call(s32[2]{0:T(128)S(1)} %pad_add_fusion.valid_ref, bf16[768,2304]{1,0:T(8,128)(2,1)S(1)} %convolution_convert_fusion.2.query_ref.key_ref.value_ref, bf16[768,2304]{1,0:T(8,128)(2,1)S(1)} %convolution_convert_fusion.2.query_ref.key_ref.value_ref, ...), custom_call_target="tpu_custom_call" | custom-call | flops 3623878656 | bytes 4718592 | tf_op jit(solution)/shard_map/pallas_call | solution.py:124
  210.8 12.1 %collective-permute-done.25.refs_6_ = bf16[4,4,48,768]{3,2,1,0:T(8,128)(2,1)S(1)} collective-permute-done((bf16[4,4,48,768]{3,2,1,0:T(8,128)(2,1)S(1)}, bf16[4,4,48,768]{3,2,1,0:T(8,128)(2,1)S(1)}, u32[]{:S(2)}, u32[]{:S(2)}) %collective-permute-start.25) | collective-permute-done | bytes 1179680 | tf_op jit(solution)/shard_map/ppermute | solution.py:304
  222.8 11.2 %collective-permute-done.23.refs_3_ = bf16[4,4,48,768]{3,2,1,0:T(8,128)(2,1)S(1)} collective-permute-done((bf16[4,4,48,768]{3,2,1,0:T(8,128)(2,1)S(1)}, bf16[4,4,48,768]{3,2,1,0:T(8,128)(2,1)S(1)}, u32[]{:S(2)}, u32[]{:S(2)}) %collective-permute-start.23) | collective-permute-done | bytes 1179680 | tf_op jit(solution)/shard_map/ppermute | solution.py:304
  234.1 12.4 %collective-permute-done.26.refs_7_ = bf16[4,4,48,768]{3,2,1,0:T(8,128)(2,1)S(1)} collective-permute-done((bf16[4,4,48,768]{3,2,1,0:T(8,128)(2,1)S(1)}, bf16[4,4,48,768]{3,2,1,0:T(8,128)(2,1)S(1)}, u32[]{:S(2)}, u32[]{:S(2)}) %collective-permute-start.26) | collective-permute-done | bytes 1179680 | tf_op jit(solution)/shard_map/ppermute | solution.py:304
  262.5 20.6 %collective-permute-done.34 = bf16[2,2,1,48,1536]{4,3,2,1,0:T(8,128)(2,1)} collective-permute-done((bf16[2,2,1,48,1536]{4,3,2,1,0:T(8,128)(2,1)}, bf16[2,2,1,48,1536]{4,3,2,1,0:T(8,128)(2,1)}, u32[]{:S(2)}, u32[]{:S(2)}) %collective-permute-start.34) | collective-permute-done | bytes 589856 | tf_op jit(solution)/shard_map/ppermute | solution.py:304
  302.0 11.7 %shard_map.453 = bf16[768,768]{1,0:T(8,128)(2,1)S(1)} custom-call(s32[2]{0:T(128)S(1)} %broadcast_13_valid_ref.2.valid_ref, bf16[768,768]{1,0:T(8,128)(2,1)S(1)} %convolution_convert_fusion.9.query_ref, bf16[512,768]{1,0:T(8,128)(2,1)S(1)} %convolution_convert_fusion.10.key_ref.value_ref, bf16[512,768]{1,0:T(8,128)(2,1)S(1)} %convolution_convert_fusion.10.key_ref.value_ref), custom_call_target="tpu_custom_call" | custom-call | flops 1207959552 | bytes 3145728 | tf_op jit(solution)/shard_map/pallas_call | solution.py:124
  325.0 26.2 %collective-permute-done.55 = bf16[384,1536]{1,0:T(8,128)(2,1)} collective-permute-done((bf16[384,1536]{1,0:T(8,128)(2,1)}, bf16[384,1536]{1,0:T(8,128)(2,1)}, u32[]{:S(2)}, u32[]{:S(2)}) %collective-permute-start.55) | collective-permute-done | bytes 1179680 | tf_op jit(solution)/shard_map/ppermute | solution.py:304
  370.0 15.7 %collective-permute-done.37 = bf16[384,1536]{1,0:T(8,128)(2,1)S(1)} collective-permute-done((bf16[384,1536]{1,0:T(8,128)(2,1)}, bf16[384,1536]{1,0:T(8,128)(2,1)S(1)}, u32[]{:S(2)}, u32[]{:S(2)}) %collective-permute-start.37) | collective-permute-done | bytes 1179680 | tf_op jit(solution)/shard_map/ppermute | solution.py:304
  390.4 22.8 %collective-permute-done.41 = bf16[384,1536]{1,0:T(8,128)(2,1)S(1)} collective-permute-done((bf16[384,1536]{1,0:T(8,128)(2,1)}, bf16[384,1536]{1,0:T(8,128)(2,1)S(1)}, u32[]{:S(2)}, u32[]{:S(2)}) %collective-permute-start.41) | collective-permute-done | bytes 1179680 | tf_op jit(solution)/shard_map/ppermute | solution.py:304
  460.6 6.3 multiply_convert_fusion.4
  525.6 18.8 %collective-permute-done.40 = bf16[384,1536]{1,0:T(8,128)(2,1)S(1)} collective-permute-done((bf16[384,1536]{1,0:T(8,128)(2,1)S(1)}, bf16[384,1536]{1,0:T(8,128)(2,1)S(1)}, u32[]{:S(2)}, u32[]{:S(2)}) %collective-permute-start.40) | collective-permute-done | bytes 1179680 | tf_op jit(solution)/shard_map/ppermute | solution.py:304
  547.2 11.5 %fusion.33 = bf16[768,1536]{1,0:T(8,128)(2,1)} fusion(bf16[3072,1536]{1,0:T(8,128)(2,1)} %constant_dynamic-update-slice_fusion.31, bf16[768,768]{1,0:T(8,128)(2,1)S(1)} %copy-done.155, bf16[768,768]{1,0:T(8,128)(2,1)S(1)} %copy-done.153, bf16[768,768]{1,0:T(8,128)(2,1)S(1)} %copy-done.151, bf16[768,768]{1,0:T(8,128)(2,1)S(1)} %copy-done.149), kind=kOutput, calls=%fused_computation.43 | convolution fusion | flops 7267811328 | bytes 16515072 | tf_op jit(solution)/shard_map/dot_general | solution.py:58
  558.8 14.4 %collective-permute-done.44 = bf16[384,1536]{1,0:T(8,128)(2,1)} collective-permute-done((bf16[384,1536]{1,0:T(8,128)(2,1)}, bf16[384,1536]{1,0:T(8,128)(2,1)}, u32[]{:S(2)}, u32[]{:S(2)}) %collective-permute-start.44) | collective-permute-done | bytes 1179680 | tf_op jit(solution)/shard_map/ppermute | solution.py:304
  573.2 21.9 %collective-permute-done.54 = bf16[384,1536]{1,0:T(8,128)(2,1)} collective-permute-done((bf16[384,1536]{1,0:T(8,128)(2,1)}, bf16[384,1536]{1,0:T(8,128)(2,1)}, u32[]{:S(2)}, u32[]{:S(2)}) %collective-permute-start.54) | collective-permute-done | bytes 1179680 | tf_op jit(solution)/shard_map/ppermute | solution.py:304
  595.2 27.6 %collective-permute-done.58 = bf16[384,1536]{1,0:T(8,128)(2,1)} collective-permute-done((bf16[384,1536]{1,0:T(8,128)(2,1)}, bf16[384,1536]{1,0:T(8,128)(2,1)}, u32[]{:S(2)}, u32[]{:S(2)}) %collective-permute-start.58) | collective-permute-done | bytes 1179680 | tf_op jit(solution)/shard_map/ppermute | solution.py:304
  622.8 9.3 fusion.58
  635.3 24.3 %fusion.16 = bf16[1536,1536]{1,0:T(8,128)(2,1)} fusion(bf16[3072,1536]{1,0:T(8,128)(2,1)} %constant_dynamic-update-slice_fusion.23, bf16[768,768]{1,0:T(8,128)(2,1)} %get-tuple-element.142, bf16[768,768]{1,0:T(8,128)(2,1)} %get-tuple-element.141, bf16[768,768]{1,0:T(8,128)(2,1)} %get-tuple-element.140, bf16[768,768]{1,0:T(8,128)(2,1)} %get-tuple-element.139, ...), kind=kOutput, calls=%fused_computation.16 | convolution fusion | flops 14573371392 | bytes 23592960 | tf_op jit(solution)/shard_map/dot_general | solution.py:58
  675.4 11.8 %shard_map.455 = (bf16[768,768]{1,0:T(8,128)(2,1)S(1)}, bf16[256,768]{1,0:T(8,128)(2,1)S(1)}, bf16[256,768]{1,0:T(8,128)(2,1)S(1)}) custom-call(s32[2]{0:T(128)S(1)} %copy-done.18, bf16[768,768]{1,0:T(8,128)(2,1)S(1)} %copy-done.20, bf16[512,768]{1,0:T(8,128)(2,1)S(1)} %copy-done.24, bf16[512,768]{1,0:T(8,128)(2,1)S(1)} %copy-done.24, ...), custom_call_target="tpu_custom_call" | custom-call | flops 3019898880 | bytes 4718592 | tf_op jit(solution)/shard_map/pallas_call | solution.py:142
  711.2 21.0 %collective-permute-done.80 = bf16[2,2,4,48,768]{4,3,1,2,0:T(8,128)(2,1)} collective-permute-done((bf16[2,2,4,48,768]{4,3,1,2,0:T(8,128)(2,1)}, bf16[2,2,4,48,768]{4,3,1,2,0:T(8,128)(2,1)}, u32[]{:S(2)}, u32[]{:S(2)}) %collective-permute-start.80) | collective-permute-done | bytes 1179680 | tf_op jit(solution)/shard_map/ppermute | solution.py:304
  746.0 7.2 collective-permute-done.81
  765.0 19.6 %shard_map.456 = (bf16[768,768]{1,0:T(8,128)(2,1)S(1)}, bf16[768,768]{1,0:T(8,128)(2,1)S(1)}, bf16[768,768]{1,0:T(8,128)(2,1)S(1)}) custom-call(s32[2]{0:T(128)S(1)} %copy-done.16, bf16[768,2304]{1,0:T(8,128)(2,1)} %copy-done.25, bf16[768,2304]{1,0:T(8,128)(2,1)} %copy-done.25, bf16[768,2304]{1,0:T(8,128)(2,1)} %copy-done.25, ...), custom_call_target="tpu_custom_call" | custom-call | flops 9059696640 | bytes 7077888 | tf_op jit(solution)/shard_map/pallas_call | solution.py:142
  807.4 23.9 %collective-permute-done.73 = bf16[2,2,4,48,1152]{4,3,1,2,0:T(8,128)(2,1)} collective-permute-done((bf16[2,2,4,48,1152]{4,3,1,2,0:T(8,128)(2,1)}, bf16[2,2,4,48,1152]{4,3,1,2,0:T(8,128)(2,1)}, u32[]{:S(2)}, u32[]{:S(2)}) %collective-permute-start.73) | collective-permute-done | bytes 1769504 | tf_op jit(solution)/shard_map/ppermute | solution.py:304
  846.6 7.8 collective-permute-done.74
  915.9 6.2 collective-permute-done.88
  930.3 7.6 collective-permute-done.89
  940.4 7.2 multiply_reduce_fusion
  985.1 11.3 %concatenate.315 = f32[23]{0:T(128)} concatenate(f32[1]{0:T(128)} %bitcast.76, f32[1]{0:T(128)} %bitcast.77, f32[3]{0:T(128)} %get-tuple-element.87, f32[1]{0:T(128)} %bitcast.78, f32[1]{0:T(128)} %bitcast.79, f32[1]{0:T(128)} %bitcast.80, f32[1]{0:T(128)} %bitcast.81, f32[1]{0:T(128)} %bitcast.82, f32[1]{0:T(128)} %bitcast.101, f32[3]{0:T(128)} %get-tuple-element.86, ...), dimensions={0} | concatenate | bytes 184 | tf_op jit(solution)/shard_map/concatenate | solution.py:832
  (813 shorter events, 505.6 us)
Async XLA Ops:
  7.2 72.1 %all-gather.7.cloned.1.call-start = ((), (), s32[]{:S(2)}) async-start(), calls=%async_computation.8 | async-start | bytes 2211840 | tf_op jit(solution)/shard_map/all_gather | solution.py:357
  17.7 67.5 %collective-permute-start.12 = (s32[1]{0:T(128)}, s32[1]{0:T(128)}, u32[]{:S(2)}, u32[]{:S(2)}) collective-permute-start(s32[1]{0:T(128)} %param.29), channel_id=1, source_target_pairs={{0,8},{8,0},{1,9},{9,1},{2,10},{10,2},{3,11},{11,3},{4,12},{12,4},... | collective-permute-start | bytes 20 | tf_op jit(solution)/shard_map/ppermute | solution.py:304
  25.2 107.5 %collective-permute-start.32 = (bf16[2,1,2,48,1536]{4,3,2,1,0:T(8,128)(2,1)}, bf16[2,1,2,48,1536]{4,3,2,1,0:T(8,128)(2,1)}, u32[]{:S(2)}, u32[]{:S(2)}) collective-permute-start(bf16[2,1,2,48,1536]{4,3,2,1,0:T(8,128)(2,1)} %get-tuple-element.171), channel_id=1, source_target_pairs={{0,8},{8,0},{1,9},{9,1},{2,10},{10,2},{3,11},{11,3},{4,12},{12,4},... | collective-permute-start | bytes 1769480 | tf_op jit(solution)/shard_map/ppermute | solution.py:304
  35.8 94.9 %all-gather.9.cloned.1.call-start = ((), (), s32[]{:S(2)}) async-start(), calls=%async_computation.9 | async-start | bytes 2949120 | tf_op jit(solution)/shard_map/all_gather | solution.py:357
  37.6 386.3 %all-gather.11.cloned.1.call-start = ((), (), s32[]{:S(2)}) async-start(), calls=%async_computation.10 | async-start | bytes 8847360 | tf_op jit(solution)/shard_map/all_gather | solution.py:406
  80.9 51.9 %collective-permute-start.16 = (bf16[4,3,48,768]{3,2,1,0:T(8,128)(2,1)S(1)}, bf16[4,3,48,768]{3,2,1,0:T(8,128)(2,1)S(1)}, u32[]{:S(2)}, u32[]{:S(2)}) collective-permute-start(bf16[4,3,48,768]{3,2,1,0:T(8,128)(2,1)S(1)} %get-tuple-element.159.refs_0_), channel_id=1, source_target_pairs={{0,16},{16,0},{1,17},{17,1},{2,18},{18,2},{3,19},{19,3},{4,20},{20... | collective-permute-start | bytes 2654216 | tf_op jit(solution)/shard_map/ppermute | solution.py:304
  82.4 51.9 %collective-permute-start.18 = (bf16[4,3,48,768]{3,2,1,0:T(8,128)(2,1)S(1)}, bf16[4,3,48,768]{3,2,1,0:T(8,128)(2,1)S(1)}, u32[]{:S(2)}, u32[]{:S(2)}) collective-permute-start(bf16[4,3,48,768]{3,2,1,0:T(8,128)(2,1)S(1)} %get-tuple-element.158.refs_4_), channel_id=1, source_target_pairs={{0,1},{1,0},{2,3},{3,2},{4,5},{5,4},{6,7},{7,6},{8,9},{9,8},{10,11... | collective-permute-start | bytes 2654216 | tf_op jit(solution)/shard_map/ppermute | solution.py:304
  84.6 51.2 %collective-permute-start.15 = (bf16[4,3,48,768]{3,2,1,0:T(8,128)(2,1)S(1)}, bf16[4,3,48,768]{3,2,1,0:T(8,128)(2,1)}, u32[]{:S(2)}, u32[]{:S(2)}) collective-permute-start(bf16[4,3,48,768]{3,2,1,0:T(8,128)(2,1)S(1)} %get-tuple-element.159.refs_0_), channel_id=1, source_target_pairs={{0,1},{1,0},{2,3},{3,2},{4,5},{5,4},{6,7},{7,6},{8,9},{9,8},{10,11... | collective-permute-start | bytes 2654216 | tf_op jit(solution)/shard_map/ppermute | solution.py:304
  85.1 51.2 %collective-permute-start.19 = (bf16[4,3,48,768]{3,2,1,0:T(8,128)(2,1)S(1)}, bf16[4,3,48,768]{3,2,1,0:T(8,128)(2,1)}, u32[]{:S(2)}, u32[]{:S(2)}) collective-permute-start(bf16[4,3,48,768]{3,2,1,0:T(8,128)(2,1)S(1)} %get-tuple-element.158.refs_4_), channel_id=1, source_target_pairs={{0,16},{16,0},{1,17},{17,1},{2,18},{18,2},{3,19},{19,3},{4,20},{20... | collective-permute-start | bytes 2654216 | tf_op jit(solution)/shard_map/ppermute | solution.py:304
  132.7 52.9 %collective-permute-start.13 = (bf16[384,1536]{1,0:T(8,128)(2,1)S(1)}, bf16[384,1536]{1,0:T(8,128)(2,1)S(1)}, u32[]{:S(2)}, u32[]{:S(2)}) collective-permute-start(bf16[384,1536]{1,0:T(8,128)(2,1)S(1)} %copy-done.72), channel_id=1, source_target_pairs={{0,8},{8,0},{1,9},{9,1},{2,10},{10,2},{3,11},{11,3},{4,12},{12,4},... | collective-permute-start | bytes 3538952 | tf_op jit(solution)/shard_map/ppermute | solution.py:304
  132.8 54.5 %collective-permute-start.22 = (bf16[4,4,48,768]{3,2,1,0:T(8,128)(2,1)S(1)}, bf16[4,4,48,768]{3,2,1,0:T(8,128)(2,1)S(1)}, u32[]{:S(2)}, u32[]{:S(2)}) collective-permute-start(bf16[4,4,48,768]{3,2,1,0:T(8,128)(2,1)S(1)} %get-tuple-element.157.refs_0_), channel_id=1, source_target_pairs={{0,16},{16,0},{1,17},{17,1},{2,18},{18,2},{3,19},{19,3},{4,20},{20... | collective-permute-start | bytes 3538952 | tf_op jit(solution)/shard_map/ppermute | solution.py:304
  134.3 53.5 %collective-permute-start.24 = (bf16[4,4,48,768]{3,2,1,0:T(8,128)(2,1)S(1)}, bf16[4,4,48,768]{3,2,1,0:T(8,128)(2,1)S(1)}, u32[]{:S(2)}, u32[]{:S(2)}) collective-permute-start(bf16[4,4,48,768]{3,2,1,0:T(8,128)(2,1)S(1)} %get-tuple-element.156.refs_4_), channel_id=1, source_target_pairs={{0,1},{1,0},{2,3},{3,2},{4,5},{5,4},{6,7},{7,6},{8,9},{9,8},{10,11... | collective-permute-start | bytes 3538952 | tf_op jit(solution)/shard_map/ppermute | solution.py:304
  181.3 72.2 %collective-permute-start.33 = (bf16[1,2,2,48,1536]{4,3,2,1,0:T(8,128)(2,1)S(1)}, bf16[1,2,2,48,1536]{4,3,2,1,0:T(8,128)(2,1)}, u32[]{:S(2)}, u32[]{:S(2)}) collective-permute-start(bf16[1,2,2,48,1536]{4,3,2,1,0:T(8,128)(2,1)S(1)} %get-tuple-element.169), channel_id=1, source_target_pairs={{0,16},{16,0},{1,17},{17,1},{2,18},{18,2},{3,19},{19,3},{4,20},{20... | collective-permute-start | bytes 1769480 | tf_op jit(solution)/shard_map/ppermute | solution.py:304
  187.8 58.6 %collective-permute-start.26 = (bf16[4,4,48,768]{3,2,1,0:T(8,128)(2,1)S(1)}, bf16[4,4,48,768]{3,2,1,0:T(8,128)(2,1)S(1)}, u32[]{:S(2)}, u32[]{:S(2)}) collective-permute-start(bf16[4,4,48,768]{3,2,1,0:T(8,128)(2,1)S(1)} %collective-permute-done.24.refs_5_), channel_id=1, source_target_pairs={{0,16},{16,0},{1,17},{17,1},{2,18},{18,2},{3,19},{19,3},{4,20},{20... | collective-permute-start | bytes 3538952 | tf_op jit(solution)/shard_map/ppermute | solution.py:304
  287.7 414.3 %reduce-scatter.11.cloned.1.call-start = ((), (), s32[]{:S(2)}) async-start(), calls=%async_computation.7 | async-start | bytes 2949120 | tf_op jit(solution)/shard_map/reduce_scatter | solution.py:679
  297.9 53.3 %collective-permute-start.55 = (bf16[384,1536]{1,0:T(8,128)(2,1)}, bf16[384,1536]{1,0:T(8,128)(2,1)}, u32[]{:S(2)}, u32[]{:S(2)}) collective-permute-start(bf16[384,1536]{1,0:T(8,128)(2,1)} %get-tuple-element.112), channel_id=1, source_target_pairs={{0,16},{16,0},{1,17},{17,1},{2,18},{18,2},{3,19},{19,3},{4,20},{20... | collective-permute-start | bytes 3538952 | tf_op jit(solution)/shard_map/ppermute | solution.py:304
  356.9 56.3 %collective-permute-start.60 = (bf16[384,1536]{1,0:T(8,128)(2,1)}, bf16[384,1536]{1,0:T(8,128)(2,1)S(1)}, u32[]{:S(2)}, u32[]{:S(2)}) collective-permute-start(bf16[384,1536]{1,0:T(8,128)(2,1)} %collective-permute-done.59), channel_id=1, source_target_pairs={{0,8},{8,0},{1,9},{9,1},{2,10},{10,2},{3,11},{11,3},{4,12},{12,4},... | collective-permute-start | bytes 3538952 | tf_op jit(solution)/shard_map/ppermute | solution.py:304
  359.9 53.4 %collective-permute-start.41 = (bf16[384,1536]{1,0:T(8,128)(2,1)}, bf16[384,1536]{1,0:T(8,128)(2,1)S(1)}, u32[]{:S(2)}, u32[]{:S(2)}) collective-permute-start(bf16[384,1536]{1,0:T(8,128)(2,1)} %get-tuple-element.116), channel_id=1, source_target_pairs={{0,16},{16,0},{1,17},{17,1},{2,18},{18,2},{3,19},{19,3},{4,20},{20... | collective-permute-start | bytes 3538952 | tf_op jit(solution)/shard_map/ppermute | solution.py:304
  362.7 52.1 %collective-permute-start.31 = (bf16[384,1536]{1,0:T(8,128)(2,1)}, bf16[384,1536]{1,0:T(8,128)(2,1)S(1)}, u32[]{:S(2)}, u32[]{:S(2)}) collective-permute-start(bf16[384,1536]{1,0:T(8,128)(2,1)} %get-tuple-element.116), channel_id=1, source_target_pairs={{0,8},{8,0},{1,9},{9,1},{2,10},{10,2},{3,11},{11,3},{4,12},{12,4},... | collective-permute-start | bytes 3538952 | tf_op jit(solution)/shard_map/ppermute | solution.py:304
  362.7 51.8 %collective-permute-start.45 = (bf16[384,1536]{1,0:T(8,128)(2,1)}, bf16[384,1536]{1,0:T(8,128)(2,1)S(1)}, u32[]{:S(2)}, u32[]{:S(2)}) collective-permute-start(bf16[384,1536]{1,0:T(8,128)(2,1)} %get-tuple-element.116), channel_id=1, source_target_pairs={{0,17},{1,16},{16,1},{17,0},{2,19},{3,18},{18,3},{19,2},{4,21},{5,... | collective-permute-start | bytes 3538952 | tf_op jit(solution)/shard_map/ppermute | solution.py:304
  443.2 80.2 %collective-permute-start.36 = (bf16[384,1536]{1,0:T(8,128)(2,1)S(1)}, bf16[384,1536]{1,0:T(8,128)(2,1)}, u32[]{:S(2)}, u32[]{:S(2)}) collective-permute-start(bf16[384,1536]{1,0:T(8,128)(2,1)S(1)} %slice.948), channel_id=1, source_target_pairs={{0,8},{8,0},{1,9},{9,1},{2,10},{10,2},{3,11},{11,3},{4,12},{12,4},... | collective-permute-start | bytes 3538952 | tf_op jit(solution)/shard_map/ppermute | solution.py:304
  456.5 50.1 %collective-permute-start.39 = (bf16[384,1536]{1,0:T(8,128)(2,1)}, bf16[384,1536]{1,0:T(8,128)(2,1)}, u32[]{:S(2)}, u32[]{:S(2)}) collective-permute-start(bf16[384,1536]{1,0:T(8,128)(2,1)} %slice.947), channel_id=1, source_target_pairs={{0,8},{8,0},{1,9},{9,1},{2,10},{10,2},{3,11},{11,3},{4,12},{12,4},... | collective-permute-start | bytes 3538952 | tf_op jit(solution)/shard_map/ppermute | solution.py:304
  518.8 54.4 %collective-permute-start.44 = (bf16[384,1536]{1,0:T(8,128)(2,1)}, bf16[384,1536]{1,0:T(8,128)(2,1)}, u32[]{:S(2)}, u32[]{:S(2)}) collective-permute-start(bf16[384,1536]{1,0:T(8,128)(2,1)} %fusion.66), channel_id=1, source_target_pairs={{0,16},{16,0},{1,17},{17,1},{2,18},{18,2},{3,19},{19,3},{4,20},{20... | collective-permute-start | bytes 3538952 | tf_op jit(solution)/shard_map/ppermute | solution.py:304
  520.7 52.5 %collective-permute-start.48 = (bf16[384,1536]{1,0:T(8,128)(2,1)}, bf16[384,1536]{1,0:T(8,128)(2,1)}, u32[]{:S(2)}, u32[]{:S(2)}) collective-permute-start(bf16[384,1536]{1,0:T(8,128)(2,1)} %fusion.65), channel_id=1, source_target_pairs={{0,17},{1,16},{16,1},{17,0},{2,19},{3,18},{18,3},{19,2},{4,21},{5,... | collective-permute-start | bytes 3538952 | tf_op jit(solution)/shard_map/ppermute | solution.py:304
  523.4 71.8 %collective-permute-start.54 = (bf16[384,1536]{1,0:T(8,128)(2,1)}, bf16[384,1536]{1,0:T(8,128)(2,1)}, u32[]{:S(2)}, u32[]{:S(2)}) collective-permute-start(bf16[384,1536]{1,0:T(8,128)(2,1)} %fusion.61), channel_id=1, source_target_pairs={{0,1},{1,0},{2,3},{3,2},{4,5},{5,4},{6,7},{7,6},{8,9},{9,8},{10,11... | collective-permute-start | bytes 3538952 | tf_op jit(solution)/shard_map/ppermute | solution.py:304
  525.2 97.6 %collective-permute-start.58 = (bf16[384,1536]{1,0:T(8,128)(2,1)}, bf16[384,1536]{1,0:T(8,128)(2,1)}, u32[]{:S(2)}, u32[]{:S(2)}) collective-permute-start(bf16[384,1536]{1,0:T(8,128)(2,1)} %fusion.60), channel_id=1, source_target_pairs={{0,16},{16,0},{1,17},{17,1},{2,18},{18,2},{3,19},{19,3},{4,20},{20... | collective-permute-start | bytes 3538952 | tf_op jit(solution)/shard_map/ppermute | solution.py:304
  545.5 77.3 %collective-permute-start.62 = (bf16[384,1536]{1,0:T(8,128)(2,1)}, bf16[384,1536]{1,0:T(8,128)(2,1)}, u32[]{:S(2)}, u32[]{:S(2)}) collective-permute-start(bf16[384,1536]{1,0:T(8,128)(2,1)} %fusion.59), channel_id=1, source_target_pairs={{0,17},{1,16},{16,1},{17,0},{2,19},{3,18},{18,3},{19,2},{4,21},{5,... | collective-permute-start | bytes 3538952 | tf_op jit(solution)/shard_map/ppermute | solution.py:304
  558.7 313.3 %reduce-scatter.9.cloned.1.call-start = ((), (), s32[]{:S(2)}) async-start(), calls=%async_computation.6 | async-start | bytes 5898240 | tf_op jit(solution)/shard_map/reduce_scatter | solution.py:684
  664.5 274.7 %reduce-scatter.5.cloned.1.call-start = ((), (), s32[]{:S(2)}) async-start(), calls=%async_computation.4 | async-start | bytes 2211840 | tf_op jit(solution)/shard_map/reduce_scatter | solution.py:767
  702.0 197.9 %collective-permute-start.90 = (bf16[192,1536]{1,0:T(8,128)(2,1)}, bf16[192,1536]{1,0:T(8,128)(2,1)}, u32[]{:S(2)}, u32[]{:S(2)}) collective-permute-start(bf16[192,1536]{1,0:T(8,128)(2,1)} %reduce-scatter.11.cloned.1.call-done), channel_id=1, source_target_pairs={{0,0},{2,1},{4,2},{6,3},{1,4},{3,5},{5,6},{7,7},{8,8},{10,9},{12,1... | collective-permute-start | bytes 1769480 | tf_op jit(solution)/shard_map/ppermute | solution.py:482
  807.4 61.4 %collective-permute-start.83 = (bf16[4,48,1536]{2,1,0:T(8,128)(2,1)}, bf16[4,48,1536]{2,1,0:T(8,128)(2,1)}, u32[]{:S(2)}, u32[]{:S(2)}) collective-permute-start(bf16[4,48,1536]{2,1,0:T(8,128)(2,1)} %fusion.142), channel_id=1, source_target_pairs={{0,1},{1,0},{2,3},{3,2},{4,5},{5,4},{6,7},{7,6},{8,9},{9,8},{10,11... | collective-permute-start | bytes 1769480 | tf_op jit(solution)/shard_map/ppermute | solution.py:304
  864.8 94.1 %reduce-scatter.7.cloned.1.call-start = ((), (), s32[]{:S(2)}) async-start(), calls=%async_computation.5 | async-start | bytes 2949120 | tf_op jit(solution)/shard_map/reduce_scatter | solution.py:747
  (241 other events, 3436.8 us)
Sparse Core Ops, SparseCore 0:
  35.9 43.3 all-gather.6
  81.4 49.2 all-gather.8
  287.8 127.1 all-gather.10
  558.9 45.9 reduce-scatter.10
  664.6 95.4 reduce-scatter.8
  864.9 43.1 reduce-scatter.4
  910.5 47.3 reduce-scatter.6

commit v2 on v1

--- a/solution.py
+++ b/solution.py
@@ -30,6 +30,7 @@
 ANY = pl.BlockSpec(memory_space=pl.ANY)
 WHOLE = pl.BlockSpec(memory_space=pltpu.VMEM)
 SCALARS = pl.BlockSpec(memory_space=pltpu.SMEM)
+LIGHT = pl.CostEstimate(flops=2**20, bytes_accessed=2**20, transcendentals=0)
 
 
 def norm_rows(matrix):
@@ -60,6 +61,21 @@
 
 def pick(array, index, axis):
     return lax.dynamic_index_in_dim(array, index, axis, keepdims=False)
+
+
+def no_work(*refs):
+    pass
+
+
+def after(values, others):
+    values = list(values)
+    return pl.pallas_call(
+        no_work,
+        out_shape=[jax.ShapeDtypeStruct(value.shape, value.dtype) for value in values],
+        in_specs=[ANY] * (len(values) + len(others)),
+        out_specs=[ANY] * len(values),
+        input_output_aliases={k: k for k in range(len(values))},
+    )(*values, *others)
 
 
 def total(terms):
@@ -128,11 +144,7 @@
         in_specs=[SCALARS] + [block_of(*part[1:]) for part in (query, key, value)],
         out_specs=block_of(frames, 0, 0),
         compiler_params=pltpu.CompilerParams(vmem_limit_bytes=32 * 2**20),
-        cost_estimate=pl.CostEstimate(
-            flops=32 * pairs * frames * words * PAIR,
-            bytes_accessed=8 * (frames + words) * HALF,
-            transcendentals=4 * pairs * frames * words,
-        ),
+        cost_estimate=LIGHT,
     )(valid, query[0], key[0], value[0])
 
 
@@ -150,11 +162,7 @@
         + [block_of(frames, 0, 0)],
         out_specs=[block_of(rows, 0, 0) for rows in (frames, words, words)],
         compiler_params=pltpu.CompilerParams(vmem_limit_bytes=48 * 2**20),
-        cost_estimate=pl.CostEstimate(
-            flops=80 * pairs * frames * words * PAIR,
-            bytes_accessed=12 * (frames + words) * HALF,
-            transcendentals=4 * pairs * frames * words,
-        ),
+        cost_estimate=LIGHT,
     )(valid, query[0], key[0], value[0], d_mixture)
 
 
@@ -271,6 +279,1260 @@
             ].astype(BF16)
 
 
+def ffn_kernel(
+    entry_a, entry_b, d_a, d_b, in_hbm, down_hbm,
+    hidden_ref, d_gate_up_ref, d_branch_ref, own_ref, other_ref,
+    entry_ref, d_ref, in_ref, down_ref, sem,
+):
+    step = pl.program_id(0)
+    sources = (entry_a, in_hbm, d_a, down_hbm, entry_b, d_b)
+    targets = (entry_ref.at[0], in_ref, d_ref.at[0], down_ref, entry_ref.at[1], d_ref.at[1])
+    copies = [
+        pltpu.make_async_copy(source, target, sem.at[k])
+        for k, (source, target) in enumerate(zip(sources, targets))
+    ]
+
+    @pl.when(step == 0)
+    def _():
+        for copy in copies:
+            copy.start()
+        for copy in copies[:4]:
+            copy.wait()
+
+    @pl.when(step == 1)
+    def _():
+        for copy in copies[4:]:
+            copy.wait()
+
+    width = down_ref.shape[0]
+    frames = d_ref.shape[1]
+    notes = entry_ref[step, frames:, :].astype(F32)
+    gate_row = notes[0:1] + notes[1:2] + notes[2:3]
+    d_branch = (d_ref[step].astype(F32) * gate_row).astype(BF16)
+    d_branch_ref[...] = d_branch
+    gate_up = dot(entry_ref[step, :frames, :], in_ref[...])
+    gate, up = gate_up[:, :width], gate_up[:, width:]
+    logistic = jax.nn.sigmoid(gate)
+    hidden = (gate * logistic * up).astype(BF16)
+    hidden_ref[...] = hidden
+    d_hidden = dot_back(d_branch, down_ref[...])
+    d_gate = d_hidden * up * logistic * (1.0 + gate * (1.0 - logistic))
+    d_gate_up_ref[:, :width] = d_gate.astype(BF16)
+    d_gate_up_ref[:, width:] = (d_hidden * gate * logistic).astype(BF16)
+    d_entry = dot_back(d_gate_up_ref[...], in_ref[...]).astype(BF16)
+    branch = dot(hidden, down_ref[...]).astype(BF16)
+
+    @pl.when(step == 0)
+    def _():
+        own_ref[0] = d_entry
+        own_ref[1] = branch
+
+    @pl.when(step == 1)
+    def _():
+        other_ref[0] = d_entry
+        other_ref[1] = branch
+
+
+NOTE_ROWS = 16
+
+
+def gate_notes(gate):
+    high = gate.astype(BF16)
+    rest = gate - high.astype(F32)
+    middle = rest.astype(BF16)
+    low = (rest - middle.astype(F32)).astype(BF16)
+    blank = jnp.zeros((NOTE_ROWS - 3, gate.shape[0]), BF16)
+    return jnp.concatenate([jnp.stack([high, middle, low]), blank])
+
+
+def ffn_both_ways(entries, cotangents, rank_in, rank_down):
+    frames = cotangents[0].shape[0]
+    width = rank_down.shape[0]
+    rows_of = lambda cols: pl.BlockSpec((frames, cols), lambda i: (i, 0))
+    whole = pl.BlockSpec((2, frames, D), lambda i: (0, 0, 0))
+    shape = lambda *sizes: jax.ShapeDtypeStruct(sizes, BF16)
+    return pl.pallas_call(
+        ffn_kernel,
+        out_shape=[shape(2 * frames, cols) for cols in (width, 2 * width, D)]
+        + [shape(2, frames, D)] * 2,
+        grid=(2,),
+        in_specs=[ANY] * 6,
+        out_specs=[rows_of(cols) for cols in (width, 2 * width, D)] + [whole] * 2,
+        scratch_shapes=[
+            pltpu.VMEM((2, frames + NOTE_ROWS, D), BF16),
+            pltpu.VMEM((2, frames, D), BF16),
+            pltpu.VMEM((D, 2 * width), BF16),
+            pltpu.VMEM((width, D), BF16),
+            pltpu.SemaphoreType.DMA((6,)),
+        ],
+        compiler_params=pltpu.CompilerParams(vmem_limit_bytes=56 * 2**20),
+        cost_estimate=LIGHT,
+    )(*entries, *cotangents, rank_in, rank_down)
+
+
+def outer_kernel(*refs, lefts, groups, rows, lanes):
+    left_refs, right_refs, out_ref = refs[:lefts], refs[lefts:-1], refs[-1]
+
+    def pieces(group):
+        return [ref[k : k + rows, :] for ref in group for k in range(0, ref.shape[0], rows)]
+
+    left_pieces = pieces(left_refs)
+    start = column = 0
+    for size in groups:
+        group = right_refs[start : start + size]
+        start += size
+        sums = None
+        for left, right in zip(left_pieces, pieces(group)):
+            term = dot_rows(left, right)
+            sums = term if sums is None else sums + term
+        sums = sums.astype(BF16)
+        end = column + sums.shape[1]
+        if lanes is None:
+            out_ref[0, :, column:end] = sums
+        else:
+            for k in range(out_ref.shape[0]):
+                out_ref[k, 0, :, column:end] = sums[k * lanes : (k + 1) * lanes]
+        column = end
+
+
+def outer_sum(lefts, groups, rows, block, lanes=None, halves=1):
+    depth = lefts[0].shape[1]
+    cols = sum(group[0][1] for group in groups) // halves
+    blocks = depth // block * halves
+    if block % 128:
+        left = jnp.concatenate([a[: a.shape[0] // rows * rows] for a in lefts])
+        right = jnp.concatenate(
+            [
+                jnp.concatenate([a[:, at * width : (at + 1) * width] for a, width, at in group])
+                for group in groups
+            ],
+            axis=1,
+        )
+        out = dot_rows(left, right).astype(BF16).reshape(depth // block, block, halves, cols)
+        return jnp.swapaxes(out, 1, 2).reshape(blocks, block, cols)
+    if lanes is None:
+        out_shape = (blocks, block, cols)
+        out_spec = pl.BlockSpec((1, block, cols), lambda i: (i, 0, 0))
+    else:
+        out_shape = (block // lanes, blocks, lanes, cols)
+        out_spec = pl.BlockSpec((block // lanes, 1, lanes, cols), lambda i: (0, i, 0, 0))
+    used = lambda array: array.shape[0] // rows * rows
+
+    def right_spec(right):
+        array, width, at = right
+        if halves > 1:
+            return pl.BlockSpec((array.shape[0], width // halves), lambda i: (0, i % halves))
+        return pl.BlockSpec(
+            (array.shape[0], width), lambda i: (0, at), pipeline_mode=pl.Buffered(1)
+        )
+
+    rights = [right for group in groups for right in group]
+    return pl.pallas_call(
+        functools.partial(
+            outer_kernel,
+            lefts=len(lefts),
+            groups=[len(group) for group in groups],
+            rows=rows,
+            lanes=lanes,
+        ),
+        out_shape=jax.ShapeDtypeStruct(out_shape, BF16),
+        grid=(blocks,),
+        in_specs=[pl.BlockSpec((used(a), block), lambda i: (0, i // halves)) for a in lefts]
+        + [right_spec(right) for right in rights],
+        out_specs=out_spec,
+        compiler_params=pltpu.CompilerParams(vmem_limit_bytes=56 * 2**20),
+        cost_estimate=LIGHT,
+    )(*lefts, *[right[0] for right in rights])
+
+
+def reduce_kernel(*refs, plan, inputs):
+    arrays, (small_hbm, in_hbm, down_hbm) = refs[:inputs], refs[inputs : inputs + 3]
+    out_ref, small_ref, in_ref, down_ref, down_in = refs[inputs + 3 : inputs + 8]
+    (
+        blocks, first_x, first_y, second, second_in, kept, lines_in, mine, other_in, left_ref, right_ref, notes,
+        load_sem, first_send, first_recv, second_send, second_recv, line_send, line_recv,
+        core_send, core_recv, note_send, note_recv,
+        in_own, in_core, in_y, in_x, in_send, in_recv, down_send, down_recv, down_sem,
+    ) = refs[inputs + 8 :]
+    y, c, z, x = (lax.axis_index(axis) for axis in AXES)
+    na, rows = kept.shape[1], kept.shape[3]
+    far_y, far_c, far_x = 1 - y, 1 - c, 1 - x
+    count = len(plan)
+    names = [("y", far_y), ("c", far_c), ("x", far_x)]
+    names += [("z", lax.rem(z + k, na)) for k in range(1, na)]
+    slots = {}
+    for m, (_, _, _, turn) in enumerate(plan):
+        slots[m] = sum(1 for other in plan[:m] if other[3] == turn)
+
+    def remote(source, target, send, recv, axis, at):
+        return pltpu.make_async_remote_copy(
+            src_ref=source,
+            dst_ref=target,
+            send_sem=send,
+            recv_sem=recv,
+            device_id={axis: at},
+            device_id_type=pl.DeviceIdType.MESH,
+        )
+
+    barrier = pltpu.get_barrier_semaphore()
+    for axis, at in names:
+        pl.semaphore_signal(
+            barrier, inc=1, device_id={axis: at}, device_id_type=pl.DeviceIdType.MESH
+        )
+    pl.semaphore_wait(barrier, len(names))
+
+    def first_copy(m):
+        if plan[m][3]:
+            source, target, axis, at = blocks.at[m, far_y], first_y.at[slots[m]], "y", far_y
+        else:
+            source, target, axis, at = blocks.at[m, :, :, :, far_x], first_x.at[slots[m]], "x", far_x
+        return remote(source, target, first_send.at[m], first_recv.at[m], axis, at)
+
+    def second_copy(m):
+        axis, at = ("x", far_x) if plan[m][3] else ("y", far_y)
+        return remote(
+            second.at[m], second_in.at[m], second_send.at[m], second_recv.at[m], axis, at
+        )
+
+    def line_copies(m):
+        return [
+            remote(
+                kept.at[m, lax.rem(z + k, na)],
+                lines_in.at[m, k - 1],
+                line_send.at[m * (na - 1) + k - 1],
+                line_recv.at[m * (na - 1) + k - 1],
+                "z",
+                lax.rem(z + k, na),
+            )
+            for k in range(1, na)
+        ]
+
+    def core_copy(m):
+        return remote(
+            mine.at[m, far_c], other_in.at[m], core_send.at[m], core_recv.at[m], "c", far_c
+        )
+
+    def note_copies(hop):
+        if hop == 0:
+            hops = [(notes.at[0, 0, 0, 0], notes.at[0, 0, 0, 1], "x", far_x)]
+        elif hop == 1:
+            hops = [
+                (notes.at[0, 0, 0], notes.at[0, 0, k], "z", lax.rem(z + k, na))
+                for k in range(1, na)
+            ]
+        elif hop == 2:
+            hops = [(notes.at[0, 0], notes.at[0, 1], "c", far_c)]
+        else:
+            hops = [(notes.at[0], notes.at[1], "y", far_y)]
+        at = 0 if hop == 0 else hop + (na - 2 if hop > 1 else 0)
+        return [
+            remote(source, target, note_send.at[at + k], note_recv.at[at + k], axis, to)
+            for k, (source, target, axis, to) in enumerate(hops)
+        ]
+
+    def loads(m):
+        copies = []
+        for group, buffer in ((plan[m][1], left_ref), (plan[m][2], right_ref)):
+            start = 0
+            for place_of in group:
+                height, width = arrays[place_of].shape
+                copies.append(
+                    pltpu.make_async_copy(
+                        arrays[place_of],
+                        buffer.at[m % 2, pl.ds(start, height), pl.ds(0, width)],
+                        load_sem.at[m % 2, len(copies)],
+                    )
+                )
+                start += height
+        return copies
+
+    def compute(m):
+        kind, lefts, rights, _ = plan[m]
+        height = sum(arrays[place_of].shape[0] for place_of in lefts)
+        depth = na * 2 * rows
+
+        @pl.loop(0, 4)
+        def _(step):
+            at_y, at_c = step // 2, step % 2
+            at, columns = (step, 0) if kind == "tall" else (at_y, at_c)
+            left = left_ref[m % 2, :height, pl.ds(pl.multiple_of(at * depth, 128), depth)]
+            right = right_ref[m % 2, :height, pl.ds(pl.multiple_of(columns * HALF, 128), HALF)]
+            sums = dot_rows(left, right).astype(BF16)
+            for k in range(2 * na):
+                blocks[m, at_y, at_c, k // 2, k % 2] = sums[k * rows : (k + 1) * rows]
+
+    def arrived(m, at_c, at_z, at_y, at_x):
+        if plan[m][3]:
+            came = first_y[slots[m], at_c, at_z, at_x]
+        else:
+            came = first_x[slots[m], at_y, at_c, at_z]
+        return blocks[m, at_y, at_c, at_z, at_x].astype(F32) + came.astype(F32)
+
+    load = pltpu.make_async_copy(small_hbm, notes.at[0, 0, 0, 0], load_sem.at[0, 0])
+    load.start()
+    load.wait()
+    hops = [note_copies(hop) for hop in range(4)]
+    for copy in hops[0]:
+        copy.start()
+
+    load = pltpu.make_async_copy(in_hbm, in_own, load_sem.at[0, 0])
+    load.start()
+    load.wait()
+
+    def in_copies(first, pairs, axis, at):
+        return [
+            remote(source, target, in_send.at[first + k], in_recv.at[first + k], axis, at)
+            for k, (source, target) in enumerate(pairs)
+        ]
+
+    in_hops = [
+        in_copies(0, [(in_own.at[:, far_c], in_core)], "c", far_c),
+        in_copies(
+            1, [(in_own.at[far_y, c], in_y.at[0]), (in_core.at[far_y], in_y.at[1])], "y", far_y
+        ),
+        in_copies(
+            3,
+            [
+                (in_own.at[y, c, far_x], in_x.at[0]),
+                (in_core.at[y, far_x], in_x.at[1]),
+                (in_y.at[0, far_x], in_x.at[2]),
+                (in_y.at[1, far_x], in_x.at[3]),
+            ],
+            "x",
+            far_x,
+        ),
+    ]
+    for copy in in_hops[0]:
+        copy.start()
+    down_copies = [
+        remote(
+            down_hbm.at[lax.rem(z + k, na)], down_in.at[k - 1],
+            down_send.at[k - 1], down_recv.at[k - 1], "z", lax.rem(z + k, na),
+        )
+        for k in range(1, na)
+    ]
+    for copy in down_copies:
+        copy.start()
+    for copy in loads(0):
+        copy.start()
+    def second_step(m):
+        first_copy(m).wait_recv()
+
+        @pl.loop(0, 2 * na)
+        def _(step):
+            at_c, at_z = step // na, step % na
+            at_y, at_x = (y, far_x) if plan[m][3] else (far_y, x)
+            second[m, at_c, at_z] = arrived(m, at_c, at_z, at_y, at_x).astype(BF16)
+
+        second_copy(m).start()
+
+    def line_step(m):
+        second_copy(m).wait_recv()
+
+        @pl.loop(0, 2 * na)
+        def _(step):
+            at_c, at_z = step // na, step % na
+            sums = arrived(m, at_c, at_z, y, x) + second_in[m, at_c, at_z].astype(F32)
+            kept[m, at_z, at_c] = sums.astype(BF16)
+
+        for copy in line_copies(m):
+            copy.start()
+
+    def last_step(m):
+        sums = kept[m, z].astype(F32)
+        for k, copy in enumerate(line_copies(m)):
+            copy.wait_recv()
+            sums += lines_in[m, k].astype(F32)
+        mine[m] = sums.astype(BF16)
+        if plan[m][0] == "tall":
+            core_copy(m).start()
+
+    for m in range(count + 6):
+        if m < count:
+            for copy in loads(m):
+                copy.wait()
+            if m + 1 < count:
+                for copy in loads(m + 1):
+                    copy.start()
+            compute(m)
+            first_copy(m).start()
+        if m in (1, 3):
+            for copy in in_hops[m // 2]:
+                copy.wait_recv()
+            for copy in in_hops[m // 2 + 1]:
+                copy.start()
+        if m in (0, 2, 4):
+            hop = m // 2
+            for copy in hops[hop]:
+                copy.wait_recv()
+            for copy in hops[hop + 1]:
+                copy.start()
+        for behind, step in ((2, second_step), (4, line_step), (6, last_step)):
+            if 0 <= m - behind < count:
+                step(m - behind)
+    order = range(count)
+    for m in order:
+        if plan[m][0] == "tall":
+            core_copy(m).wait_recv()
+            out_ref[m, 0] = mine[m, c]
+            out_ref[m, 1] = other_in[m]
+        else:
+            out_ref[m] = mine[m]
+    for copy in hops[3]:
+        copy.wait_recv()
+    small_ref[...] = notes[...]
+
+    for copy in in_hops[2]:
+        copy.wait_recv()
+    width = in_own.shape[-1] // 2
+    for at_y in range(2):
+        for at_c in range(2):
+            if at_y:
+                near = in_y[at_c, x]
+            else:
+                near = in_core[y, x] if at_c else in_own[y, c, x]
+            for at_x, piece in ((0, near), (1, in_x[at_y * 2 + at_c])):
+                rank = (
+                    lax.rem(y + at_y, 2) * 2 + lax.rem(c + at_c, 2)
+                ) * 2 + lax.rem(x + at_x, 2)
+                for half in range(2):
+                    start = pl.multiple_of(half * FF + rank * width, 128)
+                    in_ref[:, pl.ds(start, width)] = piece[:, half * width : (half + 1) * width]
+    depth = down_ref.shape[0]
+    sums = None
+    for k in range(na):
+        if k:
+            down_copies[k - 1].wait_recv()
+        source = down_in.at[k - 1] if k else down_hbm.at[z]
+        copy = pltpu.make_async_copy(source, left_ref.at[0, pl.ds(0, depth)], down_sem.at[0])
+        copy.start()
+        copy.wait()
+        term = left_ref[0, :depth, :].astype(F32)
+        sums = term if sums is None else sums + term
+    down_ref[...] = sums.astype(BF16)
+
+    for hop in hops + in_hops + [down_copies]:
+        for copy in hop:
+            copy.wait_send()
+    for m in range(count):
+        first_copy(m).wait_send()
+        second_copy(m).wait_send()
+        for copy in line_copies(m):
+            copy.wait_send()
+        if plan[m][0] == "tall":
+            core_copy(m).wait_send()
+
+
+def reduce_group(matrices, small, grad_in, grad_down, na, rows):
+    arrays, plan = [], []
+    for kind, lefts, rights, turn in matrices:
+        places = []
+        for group in (lefts, rights):
+            places.append([])
+            for array in group:
+                found = [k for k, known in enumerate(arrays) if known is array]
+                if not found:
+                    arrays.append(array)
+                    found = [len(arrays) - 1]
+                places[-1].append(found[0])
+        plan.append((kind, *places, turn))
+    count = len(plan)
+    tall = max(sum(a.shape[0] for a in lefts) for _, lefts, _, _ in matrices)
+    turns = [turn for *_, turn in plan]
+    low = lambda *shape: pltpu.VMEM(shape, BF16)
+    sem = lambda *shape: pltpu.SemaphoreType.DMA(shape)
+    all_small = (2, 2, na, 2) + small.shape
+    return pl.pallas_call(
+        functools.partial(reduce_kernel, plan=plan, inputs=len(arrays)),
+        out_shape=[
+            jax.ShapeDtypeStruct((count, 2, rows, HALF), BF16),
+            jax.ShapeDtypeStruct(all_small, BF16),
+            jax.ShapeDtypeStruct((rows, 2 * FF), BF16),
+            jax.ShapeDtypeStruct(grad_down.shape[1:], BF16),
+            jax.ShapeDtypeStruct((na - 1,) + grad_down.shape[1:], BF16),
+        ],
+        in_specs=[ANY] * (len(arrays) + 3),
+        out_specs=[WHOLE] * 4 + [ANY],
+        scratch_shapes=[
+            low(count, 2, 2, na, 2, rows, HALF),
+            low(turns.count(0), 2, 2, na, rows, HALF),
+            low(turns.count(1), 2, na, 2, rows, HALF),
+            low(count, 2, na, rows, HALF),
+            low(count, 2, na, rows, HALF),
+            low(count, na, 2, rows, HALF),
+            low(count, na - 1, 2, rows, HALF),
+            low(count, 2, rows, HALF),
+            low(count, rows, HALF),
+            low(2, tall, D),
+            low(2, tall, D),
+            low(*all_small),
+            sem(2, 4),
+            sem(count),
+            sem(count),
+            sem(count),
+            sem(count),
+            sem(count * (na - 1)),
+            sem(count * (na - 1)),
+            sem(count),
+            sem(count),
+            sem(na + 2),
+            sem(na + 2),
+            low(*grad_in.shape),
+            low(2, 2, *grad_in.shape[-2:]),
+            low(2, 2, *grad_in.shape[-2:]),
+            low(4, *grad_in.shape[-2:]),
+            sem(7),
+            sem(7),
+            sem(na - 1),
+            sem(na - 1),
+            sem(1),
+        ],
+        compiler_params=pltpu.CompilerParams(
+            vmem_limit_bytes=60 * 2**20, collective_id=1, has_side_effects=True
+        ),
+        cost_estimate=LIGHT,
+    )(*arrays, small, grad_in, grad_down)
+
+
+def pair_in_kernel(own_ref, other_ref, weight_ref, out_ref, *, product):
+    for step, ref in enumerate((own_ref, other_ref)):
+
+        @pl.when(pl.program_id(0) == step)
+        def _():
+            out_ref[...] = product(ref[...], weight_ref[...]).astype(BF16)
+
+
+def pair_in(own, other, weight, product):
+    frames = own.shape[0]
+    cols = weight.shape[1] if product is dot else weight.shape[0]
+    whole = lambda array: pl.BlockSpec(
+        array.shape, lambda i: (0, 0), pipeline_mode=pl.Buffered(1)
+    )
+    return pl.pallas_call(
+        functools.partial(pair_in_kernel, product=product),
+        out_shape=jax.ShapeDtypeStruct((2 * frames, cols), BF16),
+        grid=(2,),
+        in_specs=[whole(own), whole(other), whole(weight)],
+        out_specs=pl.BlockSpec((frames, cols), lambda i: (i, 0)),
+        compiler_params=pltpu.CompilerParams(vmem_limit_bytes=48 * 2**20),
+        cost_estimate=LIGHT,
+    )(own, other, weight)
+
+
+def pair_out_kernel(*refs, product):
+    part_refs, weight_ref, own_ref, other_ref = refs[:-3], refs[-3], refs[-2], refs[-1]
+    sums = None
+    column = 0
+    for ref in part_refs:
+        weight = weight_ref[...]
+        if len(part_refs) > 1:
+            weight = weight_ref[:, column : column + ref.shape[1]]
+            column += ref.shape[1]
+        term = product(ref[...], weight)
+        sums = term if sums is None else sums + term
+
+    @pl.when(pl.program_id(0) == 0)
+    def _():
+        own_ref[...] = sums
+
+    @pl.when(pl.program_id(0) == 1)
+    def _():
+        other_ref[...] = sums.astype(BF16)
+
+
+def pair_out(parts, weight, product):
+    frames = parts[0].shape[0] // 2
+    cols = weight.shape[1] if product is dot else weight.shape[0]
+    whole = pl.BlockSpec((frames, cols), lambda i: (0, 0))
+    return pl.pallas_call(
+        functools.partial(pair_out_kernel, product=product),
+        out_shape=[
+            jax.ShapeDtypeStruct((frames, cols), F32),
+            jax.ShapeDtypeStruct((frames, cols), BF16),
+        ],
+        grid=(2,),
+        in_specs=[pl.BlockSpec((frames, part.shape[1]), lambda i: (i, 0)) for part in parts]
+        + [pl.BlockSpec(weight.shape, lambda i: (0, 0), pipeline_mode=pl.Buffered(1))],
+        out_specs=[whole, whole],
+        compiler_params=pltpu.CompilerParams(vmem_limit_bytes=48 * 2**20),
+        cost_estimate=LIGHT,
+    )(*parts, weight)
+
+
+def shift_kernel(
+    terms_ref, cot_hbm, in_ref, shifts_ref, cots_hbm, parts_ref,
+    from_core, line_out, line_in, y_out, y_in, x_out, x_in,
+    in_core, in_y, in_x,
+    core_sem, line_send, line_recv, step_sem, cot_send, cot_recv, relay_send, relay_recv,
+    in_send, in_recv,
+):
+    y, c, z, x = (lax.axis_index(axis) for axis in AXES)
+    na = terms_ref.shape[2]
+    far_y, far_c, far_x = 1 - y, 1 - c, 1 - x
+
+    def remote(source, target, send, recv, device):
+        return pltpu.make_async_remote_copy(
+            src_ref=source,
+            dst_ref=target,
+            send_sem=send,
+            recv_sem=recv,
+            device_id=device,
+            device_id_type=pl.DeviceIdType.MESH,
+        )
+
+    devices = [{"y": far_y}, {"c": far_c}, {"x": far_x}]
+    devices += [{"z": lax.rem(z + k, na)} for k in range(1, na)]
+    barrier = pltpu.get_barrier_semaphore()
+    for device in devices:
+        pl.semaphore_signal(
+            barrier, inc=1, device_id=device, device_id_type=pl.DeviceIdType.MESH
+        )
+    pl.semaphore_wait(barrier, len(devices))
+
+    to_core = remote(terms_ref.at[:, 1], from_core, core_sem.at[0], core_sem.at[1], {"c": far_c})
+    to_core.start()
+
+    def block_copies(first, pairs, device):
+        return [
+            remote(source, target, in_send.at[first + k], in_recv.at[first + k], device)
+            for k, (source, target) in enumerate(pairs)
+        ]
+
+    in_hops = [
+        block_copies(0, [(in_ref.at[:, 1], in_core)], {"c": far_c}),
+        block_copies(1, [(in_ref.at[1, 0], in_y.at[0]), (in_core.at[1], in_y.at[1])], {"y": far_y}),
+        block_copies(
+            3,
+            [
+                (in_ref.at[0, 0, 1], in_x.at[0]),
+                (in_core.at[0, 1], in_x.at[1]),
+                (in_y.at[0, 1], in_x.at[2]),
+                (in_y.at[1, 1], in_x.at[3]),
+            ],
+            {"x": far_x},
+        ),
+    ]
+    for copy in in_hops[0]:
+        copy.start()
+    chips = {1: {"x": far_x}, 2: {"y": far_y}}
+    cots = {
+        2 * k: remote(cot_hbm, cots_hbm.at[2 * k], cot_send.at[2 * k], cot_recv.at[2 * k], chips[k])
+        for k in chips
+    }
+    cots[1] = remote(cot_hbm, cots_hbm.at[1], cot_send.at[1], cot_recv.at[1], {"c": far_c})
+    for k in (1, 2, 3):
+        cots[2 * k + 1] = remote(
+            cots_hbm.at[2 * k], cots_hbm.at[2 * k + 1],
+            cot_send.at[2 * k + 1], cot_recv.at[2 * k + 1], {"c": far_c},
+        )
+    relays = []
+    for k, (part, size) in enumerate(halves_of(cot_hbm.shape[0])):
+        near, next_to = (1, 2) if k == 0 else (2, 1)
+        here = pl.ds(part, size)
+        relays.append(
+            remote(
+                cots_hbm.at[2 * near, here], cots_hbm.at[6, here],
+                relay_send.at[k], relay_recv.at[k], chips[next_to],
+            )
+        )
+    cots[2].start()
+    cots[4].start()
+    cots[1].start()
+
+    to_core.wait_recv()
+    for copy in in_hops[0]:
+        copy.wait_recv()
+    for copy in in_hops[1]:
+        copy.start()
+    lines = []
+    for k in range(1, na):
+        line_out[k - 1] = terms_ref[:, 0, k] + from_core[:, k]
+        lines.append(
+            remote(
+                line_out.at[k - 1], line_in.at[k - 1], line_send.at[k - 1], line_recv.at[k - 1],
+                {"z": lax.rem(z - k + na, na)},
+            )
+        )
+        lines[-1].start()
+    here = terms_ref[:, 0, 0] + from_core[:, 0]
+    for k, copy in enumerate(lines):
+        copy.wait_recv()
+        here = here + line_in[k]
+    y_out[...] = here[1]
+    to_y = remote(y_out, y_in, step_sem.at[0], step_sem.at[1], {"y": far_y})
+    to_y.start()
+    for k in (1, 2):
+        cots[2 * k].wait_recv()
+    for copy in relays:
+        copy.start()
+    for k in (1, 2):
+        cots[2 * k + 1].start()
+    to_y.wait_recv()
+    here = here[0] + y_in[...]
+    x_out[...] = here[1]
+    to_x = remote(x_out, x_in, step_sem.at[2], step_sem.at[3], {"x": far_x})
+    to_x.start()
+    for copy in in_hops[1]:
+        copy.wait_recv()
+    for copy in in_hops[2]:
+        copy.start()
+    to_x.wait_recv()
+    shifts_ref[...] = here[0] + x_in[...]
+
+    for copy in relays:
+        copy.wait_recv()
+    cots[7].start()
+    for copy in in_hops[2]:
+        copy.wait_recv()
+    for at_y in range(2):
+        for at_c in range(2):
+            near = in_ref[0, 0, 0] if not at_y and not at_c else None
+            if near is None:
+                near = in_y[at_c, 0] if at_y else in_core[0, 0]
+            parts_ref[at_y, at_c, 0] = near
+            parts_ref[at_y, at_c, 1] = in_x[at_y * 2 + at_c]
+    for k in (1, 3, 5, 7):
+        cots[k].wait_recv()
+        cots[k].wait_send()
+    for copy in [to_core, to_y, to_x, cots[2], cots[4]] + lines + relays + sum(in_hops, []):
+        copy.wait_send()
+
+
+def sum_shifts(terms, cotangent, blocks, na):
+    rows = terms.shape[-2]
+    full = lambda *shape: pltpu.VMEM(shape + (rows, 128), F32)
+    sem = lambda size: pltpu.SemaphoreType.DMA((size,))
+    block = blocks.shape[-2:]
+    low = lambda *shape: pltpu.VMEM(shape + block, BF16)
+    return pl.pallas_call(
+        shift_kernel,
+        out_shape=[
+            jax.ShapeDtypeStruct((rows, 128), F32),
+            jax.ShapeDtypeStruct((8,) + cotangent.shape, BF16),
+            jax.ShapeDtypeStruct(blocks.shape, BF16),
+        ],
+        in_specs=[WHOLE, ANY, WHOLE],
+        out_specs=[WHOLE, ANY, WHOLE],
+        scratch_shapes=[
+            full(2, na, 2),
+            full(na - 1, 2, 2),
+            full(na - 1, 2, 2),
+            full(2),
+            full(2),
+            full(),
+            full(),
+            low(2, 2),
+            low(2, 2),
+            low(4),
+            sem(2),
+            sem(na - 1),
+            sem(na - 1),
+            sem(4),
+            sem(8),
+            sem(8),
+            sem(2),
+            sem(2),
+            sem(7),
+            sem(7),
+        ],
+        compiler_params=pltpu.CompilerParams(
+            vmem_limit_bytes=32 * 2**20, collective_id=2, has_side_effects=True
+        ),
+        cost_estimate=LIGHT,
+    )(terms, cotangent, blocks)
+
+
+def halves_of(height):
+    cut = height // 32 * 16
+    return (0, cut), (cut, height - cut)
+
+
+def ffn_group_kernel(
+    entry_hbm, notes_hbm, cot_hbm, cots_hbm, in_hbm, down_hbm,
+    d_entry_hbm, grad_down_hbm, grad_in_hbm, branch_hbm, own_hbm, other_hbm, pair_hbm, back_hbm,
+    sum_hbm, branch_back_hbm,
+    entry, d_branch, hidden, d_gate_up, in_ref, down_ref, partial, away, branch, loaded, sums,
+    local_sem, entry_send, entry_recv, cot_sem,
+    pair_send, pair_recv, back_send, back_recv, branch_sem, out_sem,
+    relay_send, relay_recv, branch_pair_send, branch_pair_recv, branch_send, branch_recv,
+    *, chips, sizes,
+):
+    ny, nb = sizes
+    y, c, x = lax.axis_index("y"), lax.axis_index("c"), lax.axis_index("x")
+    frames = cot_hbm.shape[0]
+    rows = frames // 2
+    width = down_ref.shape[0]
+    count = len(chips)
+    sibling = {"c": 1 - c}
+    ahead = [{"y": lax.rem(y + dy, ny), "x": lax.rem(x + dx, nb)} for dy, dx in chips]
+    behind = [
+        {"y": lax.rem(y - dy + ny, ny), "x": lax.rem(x - dx + nb, nb)} for dy, dx in chips
+    ]
+
+    def remote(source, target, send, recv, device):
+        return pltpu.make_async_remote_copy(
+            src_ref=source,
+            dst_ref=target,
+            send_sem=send,
+            recv_sem=recv,
+            device_id=device,
+            device_id_type=pl.DeviceIdType.MESH,
+        )
+
+    barrier = pltpu.get_barrier_semaphore()
+    for device in [sibling] + behind[1:]:
+        pl.semaphore_signal(
+            barrier, inc=1, device_id=device, device_id_type=pl.DeviceIdType.MESH
+        )
+    pl.semaphore_wait(barrier, count)
+
+    loads = [
+        pltpu.make_async_copy(source, target, local_sem.at[k])
+        for k, (source, target) in enumerate(
+            [
+                (entry_hbm, entry.at[0, pl.ds(0, frames)]),
+                (notes_hbm, entry.at[0, pl.ds(frames, NOTE_ROWS)]),
+                (in_hbm, in_ref),
+                (down_hbm, down_ref),
+            ]
+        )
+    ]
+    for load in loads:
+        load.start()
+    cot_loads = [
+        pltpu.make_async_copy(
+            cots_hbm.at[k] if k else cot_hbm, d_branch.at[k], cot_sem.at[k]
+        )
+        for k in range(2 * count)
+    ]
+    for load in cot_loads:
+        load.start()
+    entry_copies = {
+        1: remote(entry.at[0], entry.at[1], entry_send.at[1], entry_recv.at[1], sibling)
+    }
+    for k in range(1, count):
+        entry_copies[2 * k] = remote(
+            entry.at[0], entry.at[2 * k], entry_send.at[2 * k], entry_recv.at[2 * k], ahead[k]
+        )
+        entry_copies[2 * k + 1] = remote(
+            entry.at[2 * k], entry.at[2 * k + 1],
+            entry_send.at[2 * k + 1], entry_recv.at[2 * k + 1], sibling,
+        )
+    for load in loads[:2]:
+        load.wait()
+    for k in (2, 4, 1):
+        entry_copies[k].start()
+
+    relays = []
+    height = entry.shape[1]
+    for k, (part, size) in enumerate(halves_of(height)):
+        near, next_to = (1, 2) if k == 0 else (2, 1)
+        here = pl.ds(part, size)
+        relays.append(
+            remote(
+                entry.at[2 * near, here], entry.at[2 * 3, here],
+                relay_send.at[k], relay_recv.at[k], ahead[next_to],
+            )
+        )
+
+    def branch_copies(k):
+        copies = []
+        if k == 0:
+            copies.append(pltpu.make_async_copy(branch.at[0], own_hbm, branch_sem.at[0]))
+        copies.append(
+            remote(
+                branch.at[1], other_hbm.at[k], branch_pair_send.at[k], branch_pair_recv.at[k], sibling
+            )
+        )
+        return copies
+
+    def branch_wait(k):
+        for copy in branch_copies(k)[:-1]:
+            copy.wait()
+        branch_copies(k)[-1].wait_send()
+
+    def branch_copy(k):
+        return remote(
+            sum_hbm.at[k - 1], branch_back_hbm.at[k - 1], branch_send.at[k], branch_recv.at[k],
+            behind[k],
+        )
+
+    def pair_copy(k):
+        return remote(
+            away.at[k % 2], pair_hbm.at[k], pair_send.at[k], pair_recv.at[k], sibling
+        )
+
+    def back_copy(k):
+        return remote(
+            partial.at[k], back_hbm.at[k - 1], back_send.at[k], back_recv.at[k], behind[k]
+        )
+
+    def compute(k, i):
+        @pl.loop(0, 2)
+        def _(part):
+            slot = 2 * k + i
+            here = pl.ds(pl.multiple_of(part * rows, rows), rows)
+            notes = entry[slot, frames:, :].astype(F32)
+            gate_row = notes[0:1] + notes[1:2] + notes[2:3]
+            d_here = (d_branch[slot, here, :].astype(F32) * gate_row).astype(BF16)
+            d_branch[slot, here, :] = d_here
+            gate_up = dot(entry[slot, here, :], in_ref[...])
+            gate, up = gate_up[:, :width], gate_up[:, width:]
+            logistic = jax.nn.sigmoid(gate)
+            hidden_here = (gate * logistic * up).astype(BF16)
+            hidden[slot, here, :] = hidden_here
+            d_hidden = dot_back(d_here, down_ref[...])
+            d_gate = d_hidden * up * logistic * (1.0 + gate * (1.0 - logistic))
+            d_gate_up[slot, here, :width] = d_gate.astype(BF16)
+            d_gate_up[slot, here, width:] = (d_hidden * gate * logistic).astype(BF16)
+            d_entry = dot_back(d_gate_up[slot, here, :], in_ref[...]).astype(BF16)
+            branch[i, here, :] = dot(hidden_here, down_ref[...]).astype(BF16)
+
+            if i == 0:
+                partial[k, here, :] = d_entry
+            else:
+                away[k % 2, here, :] = d_entry
+
+    def move(source, target):
+        copy = pltpu.make_async_copy(source, target, out_sem.at[0])
+        copy.start()
+        copy.wait()
+
+    def fetch(source):
+        move(source, loaded)
+        return loaded[...].astype(F32)
+
+    def branch_terms(k):
+        branch_copies(k)[-1].wait_recv()
+        own = branch[0].astype(F32) if k else fetch(own_hbm)
+        return own + fetch(other_hbm.at[k])
+
+    def finish(k):
+        pair_copy(k).wait_recv()
+        partial[k] = (partial[k].astype(F32) + fetch(pair_hbm.at[k])).astype(BF16)
+        if k:
+            back_copy(k).start()
+            pair_copy(k).wait_send()
+            away[k % 2] = branch_terms(k).astype(BF16)
+            move(away.at[k % 2], sum_hbm.at[k - 1])
+            branch_copy(k).start()
+        else:
+            pair_copy(k).wait_send()
+
+    for k in range(count):
+        if k == 0:
+            for load in loads[2:]:
+                load.wait()
+        elif k < 3:
+            if k == 1:
+                entry_copies[2].wait_recv()
+                entry_copies[4].wait_recv()
+                for copy in relays:
+                    copy.start()
+            entry_copies[2 * k + 1].start()
+        else:
+            for copy in relays:
+                copy.wait_recv()
+            entry_copies[2 * k + 1].start()
+        entry_copies[2 * k + 1].wait_recv()
+        cot_loads[2 * k].wait()
+        cot_loads[2 * k + 1].wait()
+        if k:
+            branch_wait(k - 1)
+        compute(k, 0)
+        if k == 1:
+            finish(0)
+        compute(k, 1)
+        pair_copy(k).start()
+        for copy in branch_copies(k):
+            copy.start()
+        if k:
+            finish(k)
+    branch_wait(count - 1)
+
+    down_rows = 256 if width % 256 == 0 else 128
+
+    @pl.loop(0, width // down_rows)
+    def _(block):
+        columns = pl.ds(pl.multiple_of(block * down_rows, down_rows), down_rows)
+        term = dot_rows(hidden[0, :, columns], d_branch[0])
+        for slot in range(1, 2 * count):
+            term += dot_rows(hidden[slot, :, columns], d_branch[slot])
+        branch[0, :down_rows, :] = term.astype(BF16)
+        copy = pltpu.make_async_copy(
+            branch.at[0, pl.ds(0, down_rows)], grad_down_hbm.at[columns], out_sem.at[1]
+        )
+        copy.start()
+        copy.wait()
+
+    na, _, lanes, _ = grad_in_hbm.shape
+    in_rows = na * lanes
+
+    @pl.loop(0, D // in_rows)
+    def _(block):
+        columns = pl.ds(pl.multiple_of(block * in_rows, 128), in_rows)
+        term = dot_rows(entry[0, :frames, columns], d_gate_up[0])
+        for slot in range(1, 2 * count):
+            term += dot_rows(entry[slot, :frames, columns], d_gate_up[slot])
+        branch[1, :in_rows, :] = term.astype(BF16)
+        copies = [
+            pltpu.make_async_copy(
+                branch.at[1, pl.ds(z * lanes, lanes)], grad_in_hbm.at[z, block], out_sem.at[2 + z]
+            )
+            for z in range(na)
+        ]
+        copy_all(copies)
+
+    total_here = partial[0].astype(F32)
+    for k in range(1, count):
+        back_copy(k).wait_recv()
+        total_here += fetch(back_hbm.at[k - 1])
+    sums[...] = total_here
+    move(sums, d_entry_hbm)
+    total_here = branch_terms(0)
+    for k in range(1, count):
+        branch_copy(k).wait_recv()
+        total_here += fetch(branch_back_hbm.at[k - 1])
+    sums[...] = total_here
+    move(sums, branch_hbm)
+
+    entry_copies[1].wait_send()
+    for k in range(1, count):
+        if k < 3:
+            entry_copies[2 * k].wait_send()
+            relays[k - 1].wait_send()
+        entry_copies[2 * k + 1].wait_send()
+        back_copy(k).wait_send()
+        branch_copy(k).wait_send()
+
+
+def ffn_group(entry, notes, cotangent, cotangents, rank_in, rank_down, chips, sizes, na, lanes):
+    frames = cotangent.shape[0]
+    width = rank_down.shape[0]
+    count = len(chips)
+    low = lambda *shape: jax.ShapeDtypeStruct(shape, BF16)
+    sem = lambda size: pltpu.SemaphoreType.DMA((size,))
+    clip = (frames, D)
+    return pl.pallas_call(
+        functools.partial(ffn_group_kernel, chips=chips, sizes=sizes),
+        out_shape=[
+            jax.ShapeDtypeStruct(clip, F32),
+            low(width, D),
+            low(na, D // (na * lanes), lanes, 2 * width),
+            jax.ShapeDtypeStruct(clip, F32),
+            low(*clip),
+            low(count, *clip),
+            low(count, *clip),
+            low(count - 1, *clip),
+            low(count - 1, *clip),
+            low(count - 1, *clip),
+        ],
+        in_specs=[ANY] * 6,
+        out_specs=[ANY] * 10,
+        scratch_shapes=[
+            pltpu.VMEM((2 * count, frames + NOTE_ROWS, D), BF16),
+            pltpu.VMEM((2 * count, frames, D), BF16),
+            pltpu.VMEM((2 * count, frames, width), BF16),
+            pltpu.VMEM((2 * count, frames, 2 * width), BF16),
+            pltpu.VMEM((D, 2 * width), BF16),
+            pltpu.VMEM((width, D), BF16),
+            pltpu.VMEM((count, frames, D), BF16),
+            pltpu.VMEM((2, frames, D), BF16),
+            pltpu.VMEM((2, frames, D), BF16),
+            pltpu.VMEM(clip, BF16),
+            pltpu.VMEM(clip, F32),
+            sem(4),
+            sem(2 * count),
+            sem(2 * count),
+            sem(2 * count),
+            sem(count),
+            sem(count),
+            sem(count),
+            sem(count),
+            sem(2),
+            sem(2 + na),
+            sem(2),
+            sem(2),
+            sem(count),
+            sem(count),
+            sem(count),
+            sem(count),
+        ],
+        compiler_params=pltpu.CompilerParams(
+            vmem_limit_bytes=60 * 2**20, collective_id=0, has_side_effects=True
+        ),
+        cost_estimate=LIGHT,
+    )(entry, notes, cotangent, cotangents, rank_in, rank_down)
+
+
+def stack_kernel(*refs):
+    out_ref = refs[-1]
+    out_ref[...] = jnp.zeros_like(out_ref)
+    rows = refs[0].shape[0]
+    for k, ref in enumerate(refs[:-1]):
+        out_ref[k * rows : (k + 1) * rows, :] = ref[...].astype(BF16)
+
+
+def stack_vectors(vectors):
+    parts = [vector.reshape(-1, 128) for vector in vectors]
+    rows = sum(part.shape[0] for part in parts)
+    return pl.pallas_call(
+        stack_kernel,
+        out_shape=jax.ShapeDtypeStruct((rows + -rows % 16, 128), BF16),
+        in_specs=[WHOLE] * len(parts),
+        out_specs=WHOLE,
+        cost_estimate=LIGHT,
+    )(*parts)
+
+
+def total_kernel(sums_ref, out_ref, steps, lines, step_send, step_recv, line_send, line_recv):
+    y, c, z, x = (lax.axis_index(axis) for axis in AXES)
+    na = lines.shape[0]
+
+    def remote(source, target, send, recv, device):
+        return pltpu.make_async_remote_copy(
+            src_ref=source,
+            dst_ref=target,
+            send_sem=send,
+            recv_sem=recv,
+            device_id=device,
+            device_id_type=pl.DeviceIdType.MESH,
+        )
+
+    near = [{"c": 1 - c}, {"x": 1 - x}, {"y": 1 - y}]
+    far = [{"z": lax.rem(z + k, na)} for k in range(1, na)]
+    barrier = pltpu.get_barrier_semaphore()
+    for device in near + far:
+        pl.semaphore_signal(
+            barrier, inc=1, device_id=device, device_id_type=pl.DeviceIdType.MESH
+        )
+    pl.semaphore_wait(barrier, len(near) + len(far))
+    steps[0, 0] = sums_ref[...]
+    for k, device in enumerate(near):
+        copy = remote(steps.at[k, 0], steps.at[k, 1], step_send.at[k], step_recv.at[k], device)
+        copy.start()
+        copy.wait()
+        both = steps[k, 0] + steps[k, 1]
+        if k < 2:
+            steps[k + 1, 0] = both
+    lines[z] = both
+    copies = [
+        remote(lines.at[z], lines.at[z], line_send.at[k], line_recv.at[k], device)
+        for k, device in enumerate(far)
+    ]
+    for copy in copies:
+        copy.start()
+    for copy in copies:
+        copy.wait()
+    whole = lines[0]
+    for k in range(1, na):
+        whole = whole + lines[k]
+    out_ref[...] = whole
+
+
+def total_over_devices(sums, na):
+    sem = lambda size: pltpu.SemaphoreType.DMA((size,))
+    return pl.pallas_call(
+        total_kernel,
+        out_shape=jax.ShapeDtypeStruct(sums.shape, F32),
+        in_specs=[WHOLE],
+        out_specs=WHOLE,
+        scratch_shapes=[
+            pltpu.VMEM((3, 2) + sums.shape, F32),
+            pltpu.VMEM((na,) + sums.shape, F32),
+            sem(3),
+            sem(3),
+            sem(na - 1),
+            sem(na - 1),
+        ],
+        compiler_params=pltpu.CompilerParams(collective_id=3, has_side_effects=True),
+        cost_estimate=LIGHT,
+    )(sums)
+
+
+def step_kernel(factor_ref, *refs):
+    count = len(refs) // 3
+    at = 0
+    for weight_ref, direction_ref, out_ref in zip(refs[:count], refs[count : 2 * count], refs[2 * count :]):
+        if len(weight_ref.shape) == 3:
+            for k in range(weight_ref.shape[0]):
+                out_ref[k] = weight_ref[k] - factor_ref[at] * direction_ref[k]
+                at += 1
+        else:
+            out_ref[...] = weight_ref[...] - factor_ref[at] * direction_ref[...]
+            at += 1
+
+
+def step_weights(factors, weights, directions):
+    return pl.pallas_call(
+        step_kernel,
+        out_shape=[jax.ShapeDtypeStruct(weight.shape, F32) for weight in weights],
+        in_specs=[SCALARS] + [WHOLE] * (2 * len(weights)),
+        out_specs=[WHOLE] * len(weights),
+        compiler_params=pltpu.CompilerParams(vmem_limit_bytes=56 * 2**20),
+        cost_estimate=LIGHT,
+    )(factors, *weights, *directions)
+
+
+def lamb_kernel(spot_ref, weight_ref, first_ref, second_ref, *refs):
+    gradient_refs = refs[:-4]
+    first_out, second_out, direction_out, sums_ref = refs[-4:]
+    gradient = gradient_refs[0][...].astype(F32)
+    if len(gradient_refs) == 2:
+        ours = pl.program_id(1) % 2 == spot_ref[1]
+        gradient = jnp.where(ours, gradient, gradient_refs[1][...].astype(F32))
+    weight = weight_ref[...]
+    first_new = BETA_ONE * first_ref[...] + (1.0 - BETA_ONE) * gradient
+    second_new = BETA_TWO * second_ref[...] + (1.0 - BETA_TWO) * gradient * gradient
+    direction = (
+        first_new
+        / (1.0 - BETA_ONE**STEP)
+        / (jnp.sqrt(second_new / (1.0 - BETA_TWO**STEP)) + ADAM_EPS)
+        + DECAY * weight
+    )
+    first_out[...] = first_new
+    second_out[...] = second_new
+    direction_out[...] = direction
+
+    @pl.when(pl.program_id(1) == 0)
+    def _():
+        sums_ref[...] = jnp.zeros_like(sums_ref)
+
+    for row, values in enumerate((weight, direction)):
+        squares = jnp.sum(values * values, axis=1)
+        for start in range(0, squares.shape[1], 128):
+            sums_ref[:, row, :] += squares[:, start : start + 128]
+
+
+def lamb_terms(spot, weight, first_moment, second_moment, gradients, block):
+    shape = weight.shape
+    arrays = [
+        array.reshape((-1,) + array.shape[-2:])
+        for array in (weight, first_moment, second_moment, *gradients)
+    ]
+    groups, rows, cols = arrays[0].shape
+    in_blocks = len(gradients) == 1 and arrays[3].shape != arrays[0].shape
+    spec = pl.BlockSpec((1, rows, block), lambda i, j: (i, 0, j))
+    turns = 2 * HALF // block
+    halves = pl.BlockSpec((1, rows, block), lambda i, j: (j // turns, 0, j % turns // 2))
+    by_block = pl.BlockSpec((1, rows, block), lambda i, j: (j, 0, 0))
+    full = jax.ShapeDtypeStruct((groups, rows, cols), F32)
+    out = pl.pallas_call(
+        lamb_kernel,
+        out_shape=[full, full, full, jax.ShapeDtypeStruct((groups, 8, 128), F32)],
+        grid=(groups, cols // block),
+        in_specs=[SCALARS]
+        + [spec] * 3
+        + [by_block if in_blocks else spec if len(gradients) == 1 else halves] * len(gradients),
+        out_specs=[spec] * 3 + [pl.BlockSpec((1, 8, 128), lambda i, j: (i, 0, 0))],
+        compiler_params=pltpu.CompilerParams(vmem_limit_bytes=40 * 2**20),
+        cost_estimate=pl.CostEstimate(
+            flops=20 * weight.size, bytes_accessed=28 * weight.size, transcendentals=weight.size
+        ),
+    )(spot, *arrays)
+    return [array.reshape(shape) for array in out[:3]] + [jnp.sum(out[3][:, :2], axis=-1)]
+
+
 class Grid:
     def __init__(self, mesh):
         self.ny = mesh.shape["dp"] // 2
@@ -280,6 +1542,13 @@
         self.count = self.ny * 2 * self.na * self.nb
         self.spots = list(itertools.product(*(range(self.sizes[axis]) for axis in AXES)))
         self.peers = list(itertools.product(range(self.ny), range(2), range(self.nb)))
+        self.chips = list(itertools.product(range(self.ny), range(self.nb)))
+        self.back = [
+            (dy, dc, dx)
+            for dx in range(self.nb)
+            for dy in range(self.ny)
+            for dc in range(2)
+        ]
         self.mesh = Mesh(mesh.devices.reshape(self.ny, 2, self.na, self.nb), AXES)
 
     def line(self, y, c, z, x):
@@ -342,24 +1611,29 @@
         return array
 
     def spread(self, lines, turn):
-        held = {(0, 0): lines}
+        held, marks = {(0, 0): lines}, []
         for axis in ("x", "y") if turn else ("y", "x"):
             for (y, x), piece in list(held.items()):
                 for k in range(1, self.sizes[axis]):
                     step = dict(y=y, x=x)
                     step[axis] = k
                     held[(step["y"], step["x"])] = self.move(piece, **{axis: k})
-        return held
-
-    def gather_weights(self, parts, shapes, mine, spot):
+            marks = marks or list(held.values())[1:]
+        return held, marks
+
+    def gather_weights(self, parts, shapes, mine, spot, first):
         rows = parts[0][0][0].shape[0]
         mixed = jnp.stack([shard for part in parts for shard, *_ in part])
         lines = lax.all_gather(mixed, "z")
+        if first:
+            (lines,) = after([lines], first)
         start = 0
-        held, plan = [], dict(parts=[])
+        held, marks, plan = [], [], dict(parts=[])
         for turn, part in enumerate(parts):
             end = start + len(part)
-            held.append(self.spread(lines[:, start:end], turn))
+            pieces, arrived = self.spread(lines[:, start:end], turn)
+            held.append(pieces)
+            marks += arrived
             start = end
             plan["parts"].append(
                 [(out, lane, column, shard.shape[1]) for shard, out, lane, column in part]
@@ -369,7 +1643,7 @@
             arrays = [pieces[offset] for pieces in held for offset in plan["offsets"]]
             copies = len(plan["offsets"]) * sum(len(part) for part in parts)
             kernel = functools.partial(place_pieces, plan=plan, sizes=(self.ny, self.nb))
-            return place(kernel, spot, arrays, shapes, copies)
+            return place(kernel, spot, arrays, shapes, copies), marks
         outs = [jnp.zeros(shape, BF16) for shape in shapes]
         for pieces, blocks in zip(held, plan["parts"]):
             for (dy, dx), piece in pieces.items():
@@ -383,7 +1657,7 @@
                         update = update[:, None]
                         at = (y, lane, 0, x, 0, column)
                     outs[out] = lax.dynamic_update_slice(outs[out], update, at)
-        return outs
+        return outs, marks
 
     def swap_ranks(self, blocks):
         shape = blocks.shape[1:]
@@ -395,6 +1669,15 @@
             ]
             blocks = jnp.concatenate(parts, axis=where)
         return blocks.reshape((-1,) + shape)
+
+    def swap_back(self, blocks, mine):
+        for where, axis in ((1, "c"), (1, "y"), (2, "x")):
+            parts = [
+                self.move(pick(blocks, (mine[axis] + k) % self.sizes[axis], where), **{axis: k})
+                for k in range(self.sizes[axis])
+            ]
+            blocks = jnp.stack(parts)
+        return blocks.reshape((-1,) + blocks.shape[-2:])
 
     def gather_ranks(self, in_parts, down_part, mine, spot):
         peers, rows, width = in_parts.shape
@@ -426,50 +1709,34 @@
         width = width // 2
         if rows % 16 == 0:
             kernel = functools.partial(
-                place_columns, offsets=self.peers, sizes=(self.ny, self.nb), width=width
+                place_columns, offsets=self.back, sizes=(self.ny, self.nb), width=width
             )
             return place(kernel, spot, [pieces], [(rows, 2 * FF)], 2 * peers)[0]
         out = jnp.zeros((rows, 2, FF), BF16)
-        for k, (dy, dc, dx) in enumerate(self.peers):
+        for k, (dy, dc, dx) in enumerate(self.back):
             y, x = (mine["y"] - dy) % self.ny, (mine["x"] - dx) % self.nb
             rank = (y * 2 + (mine["c"] + dc) % 2) * self.nb + x
             piece = pieces[k].reshape(rows, 2, width)
             out = lax.dynamic_update_slice(out, piece, (0, 0, rank * width))
         return out.reshape(rows, 2 * FF)
 
-    def fold(self, array, turn, mine):
-        names = "ycz"[: array.ndim - 3] if array.ndim == 6 else "yz"
-        names = list(names + "x")
+    def fold(self, array, names, turn, mine, between=(), behind=(), marks=None):
+        names = list(names)
         sources = [array]
-        for axis in "yx" if turn else "xy":
+        for axis, waits in zip("yx" if turn else "xy", (between, behind)):
             where = names.index(axis)
             size = self.sizes[axis]
             arrived = []
             for k in range(1, size):
                 away = total([pick(s, (mine[axis] + k) % size, where) for s in sources])
                 arrived.append(self.move(away.astype(BF16), **{axis: k}))
-            sources = [pick(s, mine[axis], where) for s in sources] + arrived
+            if waits:
+                arrived = after(arrived, waits)
+            if marks is not None and len(names) > len(array.shape) - 3:
+                marks += arrived
+            sources = [pick(s, mine[axis], where) for s in sources] + list(arrived)
             names.remove(axis)
-        out = total(sources).astype(BF16)
-        return out if names[0] == "z" else jnp.swapaxes(out, 0, 1)
-
-    def gather_rows(self, array):
-        held = {}
-        for y in range(self.ny):
-            for x in range(self.nb):
-                held[(y, 0, x)] = self.move(array, y=y, x=x)
-                held[(y, 1, x)] = self.swap(held[(y, 0, x)])
-        return held
-
-    def scatter_rows(self, held):
-        sources = []
-        for (y, x), (own, other) in held.items():
-            terms = [own, self.swap(other.astype(BF16))]
-            if y or x:
-                sources.append(self.move(total(terms).astype(BF16), y=-y, x=-x))
-            else:
-                sources += terms
-        return total(sources)
+        return total(sources).astype(BF16)
 
     def to_rank(self, array, back=False):
         pairs = []
@@ -482,7 +1749,7 @@
         return lax.ppermute(array, AXES, pairs)
 
 
-def lamb_terms(weight, first_moment, second_moment, gradient):
+def lamb_small(weight, first_moment, second_moment, gradient):
     first_new = BETA_ONE * first_moment + (1.0 - BETA_ONE) * gradient
     second_new = BETA_TWO * second_moment + (1.0 - BETA_TWO) * gradient * gradient
     direction = (
@@ -491,10 +1758,8 @@
         / (jnp.sqrt(second_new / (1.0 - BETA_TWO**STEP)) + ADAM_EPS)
         + DECAY * weight
     )
-    reduce_axes = (1, 2) if weight.ndim == 3 else None
-    weight_part = jnp.sum(weight * weight, axis=reduce_axes).reshape(-1)
-    update_part = jnp.sum(direction * direction, axis=reduce_axes).reshape(-1)
-    return (direction, first_new, second_new, weight_part, update_part)
+    sums = jnp.stack([jnp.sum(weight * weight), jnp.sum(direction * direction)])
+    return [first_new, second_new, direction, sums[None]]
 
 
 def shards(
@@ -537,22 +1802,6 @@
     valid = lengths[0]
     keep_rows = (jnp.arange(frames) < valid).astype(F32)[:, None]
 
-    lifted = jax.nn.silu(timestep[0].astype(F32)).astype(BF16)
-    notes = jnp.concatenate([lifted, norm_gains.astype(BF16).reshape(-1)])
-    notes = grid.gather_small(notes)
-    origin = []
-    for spot_of in grid.spots:
-        source = [
-            (mine[axis] - step) % grid.sizes[axis] for axis, step in zip(AXES, spot_of)
-        ]
-        origin.append(grid.line(*source))
-    origin = jnp.stack(origin)
-    sorter = (jnp.arange(count)[:, None] == origin[None, :]).astype(BF16)
-    gain_rows = dot(sorter, notes[:, D:])
-    gain_rows = gain_rows.reshape(count, 3, rows).transpose(1, 0, 2).reshape(3, D)
-    lifted_own = lax.dynamic_slice(notes, (0, device * rows), (count, rows))
-    shifts = grid.scatter_small(dot(lifted_own, mod_matrix.astype(BF16))).reshape(6, D)
-
     width = FF // ranks
     if rows % 16 == 0 and D // (2 * grid.ny) % 128 == 0:
         prepare = functools.partial(prepare_kernel, offsets=grid.peers, sizes=(grid.ny, grid.nb))
@@ -588,6 +1837,34 @@
     five_other = grid.swap(five_other)
     five_low = jnp.where(core == 0, five_own, five_other)
     five_high = jnp.where(core == 0, five_other, five_own)
+    lifted = jax.nn.silu(timestep[0].astype(F32)).astype(BF16)
+    notes = jnp.concatenate([lifted, norm_gains.astype(BF16).reshape(-1)])
+    (notes,) = after([notes], (five_other,))
+    notes = grid.gather_small(notes)
+    origin = []
+    for spot_of in grid.spots:
+        source = [
+            (mine[axis] - step) % grid.sizes[axis] for axis, step in zip(AXES, spot_of)
+        ]
+        origin.append(grid.line(*source))
+    origin = jnp.stack(origin)
+    sorter = (jnp.arange(count)[:, None] == origin[None, :]).astype(BF16)
+    gain_rows = dot(sorter, notes[:, D:])
+    gain_rows = gain_rows.reshape(count, 3, rows).transpose(1, 0, 2).reshape(3, D)
+    lifted_own = lax.dynamic_slice(notes, (0, device * rows), (count, rows))
+    shift_terms = dot(lifted_own, mod_matrix.astype(BF16))
+    grouped = rows % 16 == 0 and grid.ny == 2 and grid.nb == 2
+    cotangent_own = (cotangent[0].astype(F32) * keep_rows).astype(BF16)
+    if grouped:
+        shift_terms = shift_terms.reshape(grid.ny, 2, grid.na, grid.nb, 6 * D // 128, 128)
+        blocks = in_blocks.reshape(grid.ny, 2, grid.nb, rows, 2 * width)
+        shifts, cotangents, in_parts = sum_shifts(shift_terms, cotangent_own, blocks, grid.na)
+        in_parts = in_parts.reshape(ranks, rows, 2 * width)
+        shifts = shifts.reshape(6, D)
+    else:
+        shifts = grid.scatter_small(shift_terms).reshape(6, D)
+        in_parts = grid.swap_ranks(in_blocks)
+
     tall = (grid.ny, 2, grid.na, grid.nb, rows)
     wide = (grid.ny, grid.na, grid.nb, rows, D)
     both = lambda k, out, at: [(five_low[k], out, 0, at), (five_high[k], out, 1, at)]
@@ -596,19 +1873,22 @@
         (wide_low[2 * k + 1], out, None, HALF),
     ]
     first = both(0, 0, 0) + both(1, 0, HALF) + both(2, 0, 2 * HALF)
-    (matrix_qkv,) = grid.gather_weights(
-        [first[:3], first[3:]], [tall + (3 * HALF,)], mine, spot
+    (down_low,) = after([ff_down.astype(BF16)], (shifts,))
+    down_part = grid.to_rank(down_low)
+    (matrix_qkv,), marks = grid.gather_weights(
+        [first[:3], first[3:]], [tall + (3 * HALF,)], mine, spot, (shifts,)
     )
+    (down_part,) = after([down_part], (*marks, matrix_qkv))
     matrix_qkv = matrix_qkv.reshape(D, 3 * HALF)
-    second = [sides(0, 0) + both(3, 1, 0), both(4, 2, 0) + sides(1, 3)]
-    matrix_out, matrix_query, matrix_ctx, matrix_cross = grid.gather_weights(
-        second, [wide, tall + (HALF,), tall + (HALF,), wide], mine, spot
+    (matrix_out, matrix_query), marks = grid.gather_weights(
+        [sides(0, 0), both(3, 1, 0)], [wide, tall + (HALF,)], mine, spot, marks
+    )
+    (matrix_ctx, matrix_cross), marks = grid.gather_weights(
+        [both(4, 0, 0), sides(1, 1)], [tall + (HALF,), wide], mine, spot, marks
     )
     matrix_out, matrix_cross = matrix_out.reshape(HALF, D), matrix_cross.reshape(HALF, D)
     matrix_query, matrix_ctx = matrix_query.reshape(D, HALF), matrix_ctx.reshape(D, HALF)
 
-    in_parts = grid.swap_ranks(in_blocks)
-    down_part = grid.to_rank(ff_down.astype(BF16))
     rank_in, rank_down = grid.gather_ranks(in_parts, down_part, mine, spot)
 
     pair_lengths = jnp.concatenate([lengths, grid.swap(lengths)])
@@ -618,20 +1898,19 @@
     normed_one, inverse_one = norm_rows(stream)
     entry_attn = (normed_one * gain_rows[0] * (1.0 + shifts[1]) + shifts[0]).astype(BF16)
     d_result = cotangent[0].astype(F32) * keep_rows
-    d_branch_ffn = (d_result * shifts[5]).astype(BF16)
-
-    pair = lambda array: jnp.concatenate([array, grid.swap(array)])
-    unpair = lambda sums: sums[:frames] + grid.swap(sums[frames:].astype(BF16)).astype(F32)
+
     columns = HALF // PAIR
-    entry_pair = pair(entry_attn)
-    qkv = dot(entry_pair, matrix_qkv).astype(BF16)
+    entry_pair = [entry_attn, grid.swap(entry_attn)]
+    qkv = pair_in(*entry_pair, matrix_qkv, dot)
     self_parts = tuple((qkv, frames, 0, k * columns) for k in range(3))
     mixture_attn = attend(pair_lengths, *self_parts)
-    branch_attn = unpair(dot(mixture_attn, matrix_out))
+    own, away = pair_out([mixture_attn], matrix_out, dot)
+    branch_attn = own + grid.swap(away).astype(F32)
     after_attn = stream + shifts[2] * branch_attn
     normed_two, inverse_two = norm_rows(after_attn)
-    entry_cross = pair((normed_two * gain_rows[1]).astype(BF16))
-    query_cross = dot(entry_cross, matrix_query).astype(BF16)
+    entry_cross = (normed_two * gain_rows[1]).astype(BF16)
+    cross_pair = [entry_cross, grid.swap(entry_cross)]
+    query_cross = pair_in(*cross_pair, matrix_query, dot)
     blank = jnp.zeros((2 * words, count, rows // 2), BF16)
     text_cut = text.reshape(2 * words, count, rows // 2)
     text_key = jnp.concatenate([text_cut, blank], axis=-1).reshape(2 * words, -1)
@@ -640,62 +1919,72 @@
     kv_cross = dot(text_both, matrix_ctx).astype(BF16)
     cross_parts = ((query_cross, frames, 0, 0), (kv_cross, words, 0, 0), (kv_cross, words, 2, 0))
     mixture_cross = attend(all_words, *cross_parts)
-    branch_cross = unpair(dot(mixture_cross, matrix_cross))
+    own, away = pair_out([mixture_cross], matrix_cross, dot)
+    branch_cross = own + grid.swap(away).astype(F32)
     after_cross = after_attn + branch_cross
     normed_three, inverse_three = norm_rows(after_cross)
     entry_ffn = (normed_three * gain_rows[2] * (1.0 + shifts[4]) + shifts[3]).astype(BF16)
 
-    d_branch_held = grid.gather_rows(d_branch_ffn)
-    entry_held = grid.gather_rows(entry_ffn)
-    branch_held, d_entry_held = {}, {}
-    entry_parts, d_branch_parts, hidden_parts, d_gate_up_parts = [], [], [], []
-    for y in range(grid.ny):
-        for x in range(grid.nb):
-            entry_part = jnp.concatenate([entry_held[(y, c, x)] for c in range(2)])
-            d_branch_part = jnp.concatenate([d_branch_held[(y, c, x)] for c in range(2)])
-            gate_up = dot(entry_part, rank_in)
-            gate_part, up_part = gate_up[:, :width], gate_up[:, width:]
-            logistic = jax.nn.sigmoid(gate_part)
-            hidden = (gate_part * logistic * up_part).astype(BF16)
-            d_hidden = dot_back(d_branch_part, rank_down)
-            d_gate_up = jnp.concatenate(
-                [
-                    d_hidden * up_part * logistic * (1.0 + gate_part * (1.0 - logistic)),
-                    d_hidden * gate_part * logistic,
-                ],
-                axis=1,
-            ).astype(BF16)
-            d_entry_part = dot_back(d_gate_up, rank_in)
-            branch_part = dot(hidden, rank_down)
-            branch_held[(y, x)] = (branch_part[:frames], branch_part[frames:])
-            d_entry_held[(y, x)] = (d_entry_part[:frames], d_entry_part[frames:])
-            entry_parts.append(entry_part)
-            d_branch_parts.append(d_branch_part)
+    notes = gate_notes(shifts[5])
+    whole = lambda array: (array, array.shape[1], 0)
+    chips = grid.chips
+    if grouped:
+        d_entry_ffn, grad_down, grad_in, branch_ffn, *_ = ffn_group(
+            entry_ffn, notes, cotangent_own, cotangents, rank_in, rank_down,
+            chips, (grid.ny, grid.nb), grid.na, grid.nb * rows,
+        )
+        grad_in = grad_in.reshape(-1, 2 * width)
+    else:
+        entry_ext = jnp.concatenate([entry_ffn, notes])
+        cot_arrived = [grid.move(cotangent_own, y=y, x=x) for y, x in grid.chips]
+        (entry_ext,) = after([entry_ext], cot_arrived[1:])
+        arrived = [grid.move(entry_ext, y=y, x=x) for y, x in grid.chips]
+        entry_parts, hidden_parts, d_gate_up_parts, d_branch_parts = [], [], [], []
+        d_entry_sources, folded_rows, branch_own, branch_away = [], [], [], []
+        for k, (y, x) in enumerate(grid.chips):
+            own_entry, own_cot = arrived[k], cot_arrived[k]
+            if k in (1, 2):
+                own_entry, own_cot = after([own_entry, own_cot], hidden_parts[:1])
+            elif k > 2:
+                own_entry, own_cot = after([own_entry, own_cot], folded_rows[k - 2 : k - 1])
+            entries = [own_entry, grid.swap(own_entry)]
+            hidden, d_gate_up, d_branch, own, other = ffn_both_ways(
+                entries, [own_cot, grid.swap(own_cot)], rank_in, rank_down
+            )
+            other = grid.swap(other)
+            folded_rows.append(total([own[0], other[0]]).astype(BF16))
+            if k:
+                d_entry_sources.append(grid.move(folded_rows[k], y=-y, x=-x))
+                branch_away.append(total([own[1], other[1]]).astype(BF16))
+            else:
+                d_entry_sources += [own[0], other[0]]
+                branch_own += [own[1], other[1]]
+            entry_parts += entries
             hidden_parts.append(hidden)
             d_gate_up_parts.append(d_gate_up)
-    d_entry_ffn = grid.scatter_rows(d_entry_held)
-    branch_ffn = grid.scatter_rows(branch_held)
-    grad_down = dot_rows(jnp.concatenate(hidden_parts), jnp.concatenate(d_branch_parts))
-    grad_down = lax.psum_scatter(grad_down.astype(BF16), "z", tiled=True)
-    grad_down = grid.to_rank(grad_down, back=True).astype(F32)
-    grad_in = dot_rows(jnp.concatenate(entry_parts), jnp.concatenate(d_gate_up_parts)).astype(BF16)
-    grad_in = grad_in.reshape(grid.ny, 2, grid.na, grid.nb, rows, 2 * width)
-    grad_in = grad_in.transpose(2, 0, 1, 3, 4, 5).reshape(-1, 2 * width)
+            d_branch_parts.append(d_branch)
+        hidden_parts[:1] = after(hidden_parts[:1], folded_rows[-2:-1])
+        grad_down = outer_sum(
+            hidden_parts, [[whole(a) for a in d_branch_parts]], frames, 256 if width % 256 == 0 else 128
+        ).reshape(width, D)
+        d_gate_up_parts[:1] = after(d_gate_up_parts[:1], folded_rows[-1:])
+        in_group = [[whole(a) for a in d_gate_up_parts]]
+        if rows % 16 == 0:
+            grad_in = outer_sum(
+                entry_parts, in_group, frames, D // (2 * grid.ny), grid.nb * rows
+            )
+        else:
+            grad_in = outer_sum(entry_parts, in_group, frames, D // 4)
+            grad_in = grad_in.reshape(2 * grid.ny, grid.na, grid.nb * rows, 2 * width)
+            grad_in = jnp.swapaxes(grad_in, 0, 1)
+        grad_in = grad_in.reshape(-1, 2 * width)
+        d_entry_ffn = total(after(d_entry_sources, (grad_down, grad_in)))
+        branch_arrived = [
+            grid.move(away, y=-y, x=-x) for away, (y, x) in zip(branch_away, chips[1:])
+        ]
+        branch_ffn = total(branch_own + branch_arrived)
     grad_in = lax.psum_scatter(grad_in, "z", tiled=True)
-    grad_in = grad_in.reshape(ranks, rows, 2 * width)
-    by_offset = jnp.stack(
-        [
-            pick(grad_in, grid.rank(mine, offset), 0)
-            for offset in grid.peers
-        ]
-    )
-    grad_in = grid.join_columns(grid.swap_ranks(by_offset), mine, spot).astype(F32)
-
-    result = after_cross + shifts[5] * branch_ffn
-    branches = (result, shifts[2] * branch_attn, branch_cross, shifts[5] * branch_ffn)
-    stream_terms = jnp.stack([jnp.sum(keep_rows * branch * branch) for branch in branches])
-
-    d_gate_ffn = jnp.sum(d_result * branch_ffn, axis=0)
+
     d_gain_ffn = jnp.sum(d_entry_ffn * normed_three * (1.0 + shifts[4]), axis=0)
     d_scale_ffn = jnp.sum(d_entry_ffn * normed_three * gain_rows[2], axis=0)
     d_shift_ffn = jnp.sum(d_entry_ffn, axis=0)
@@ -711,144 +2000,131 @@
         high = jnp.where(core == 0, other, own)
         return jnp.concatenate([low, high], axis=-2).reshape(lead + (D,))
 
-    d_branch_cross = pair(d_after_cross.astype(BF16))
-    d_mixture_cross = dot_back(d_branch_cross, matrix_cross).astype(BF16)
-    grad_cross = grid.fold(
-        dot_rows(mixture_cross, d_branch_cross).astype(BF16).reshape(wide), 0, mine
-    )
+    d_branch_cross = d_after_cross.astype(BF16)
+    d_cross_pair = [d_branch_cross, grid.swap(d_branch_cross)]
+    d_mixture_cross = pair_in(*d_cross_pair, matrix_cross, dot_back)
     d_query_cross, d_key_cross, d_value_cross = attend_back(
         all_words, *cross_parts, d_mixture_cross
     )
-    d_entry_cross = unpair(dot_back(d_query_cross, matrix_query))
-    d_kv_cross = jnp.concatenate([d_key_cross, d_value_cross])
-    grad_ctx = dot_rows(text_both, d_kv_cross).astype(BF16)
-    grad_ctx = grid.fold(grad_ctx.reshape(tall + (HALF,)), 0, mine)
-    grad_query = dot_rows(entry_cross, d_query_cross).astype(BF16)
-    grad_query = grid.fold(grad_query.reshape(tall + (HALF,)), 1, mine)
+    own, away = pair_out([d_query_cross], matrix_query, dot_back)
+    d_entry_cross = own + grid.swap(away).astype(F32)
     d_gain_cross = jnp.sum(d_entry_cross * normed_two, axis=0)
     d_after_attn = d_after_cross + norm_back(d_entry_cross * gain_rows[1], normed_two, inverse_two)
-    d_branch_attn = pair((d_after_attn * shifts[2]).astype(BF16))
+    d_branch_attn = (d_after_attn * shifts[2]).astype(BF16)
+    d_attn_pair = [d_branch_attn, grid.swap(d_branch_attn)]
     d_gate_attn = jnp.sum(d_after_attn * branch_attn, axis=0)
-    d_mixture_attn = dot_back(d_branch_attn, matrix_out).astype(BF16)
-    grad_out = grid.fold(
-        dot_rows(mixture_attn, d_branch_attn).astype(BF16).reshape(wide), 1, mine
-    )
-    sums = jnp.concatenate(
-        [
-            grad_query.reshape(grid.na, 2 * rows, HALF),
-            grad_ctx.reshape(grid.na, 2 * rows, HALF),
-            grad_out[..., :HALF],
-            grad_out[..., HALF:],
-            grad_cross[..., :HALF],
-            grad_cross[..., HALF:],
-        ],
-        axis=1,
-    )
-    sums = lax.psum_scatter(sums, "z").reshape(4, 2, rows, HALF)
-    narrow = sums[:2]
-    narrow_own = pick(narrow, core, 1)
-    narrow_other = grid.swap(pick(narrow, 1 - core, 1))
-    grad_query, grad_ctx = (join(narrow_own[k], narrow_other[k]).astype(F32) for k in range(2))
-    grad_ctx = jnp.concatenate([grad_ctx[: rows // 2], grad_ctx[rows // 2 :]], axis=1)
-    grad_out = jnp.concatenate([sums[2, 0], sums[2, 1]], axis=1).astype(F32)
-    grad_cross = jnp.concatenate([sums[3, 0], sums[3, 1]], axis=1).astype(F32)
-
-    d_qkv = jnp.concatenate(
-        attend_back(pair_lengths, *self_parts, d_mixture_attn), axis=1
-    )
-    cut = 3 * HALF // 2
-    folded = [
-        grid.fold(
-            dot_rows(entry_pair, part).astype(BF16).reshape(tall + (cut,)), turn, mine
-        )
-        for turn, part in enumerate((d_qkv[:, :cut], d_qkv[:, cut:]))
-    ]
-    folded = jnp.concatenate(folded, axis=-1).reshape(grid.na, 2 * rows, 3 * HALF)
-    folded = lax.psum_scatter(folded, "z").reshape(2, rows, 3 * HALF)
-    qkv_own = pick(folded, core, 0)
-    qkv_other = grid.swap(pick(folded, 1 - core, 0))
-    grad_qkv = jnp.concatenate(
-        [
-            join(qkv_own[:, k * HALF : (k + 1) * HALF], qkv_other[:, k * HALF : (k + 1) * HALF])
-            for k in range(3)
-        ],
-        axis=1,
-    ).astype(F32)
-    d_entry_attn = unpair(dot_back(d_qkv, matrix_qkv))
+    d_mixture_attn = pair_in(*d_attn_pair, matrix_out, dot_back)
+    d_queries, d_keys, d_values = attend_back(pair_lengths, *self_parts, d_mixture_attn)
+    own, away = pair_out([d_queries, d_keys, d_values], matrix_qkv, dot_back)
+    d_entry_attn = own + grid.swap(away).astype(F32)
     d_gain_attn = jnp.sum(d_entry_attn * normed_one * (1.0 + shifts[1]), axis=0)
     d_scale_attn = jnp.sum(d_entry_attn * normed_one * gain_rows[0], axis=0)
     d_shift_attn = jnp.sum(d_entry_attn, axis=0)
     d_latents = d_after_attn + norm_back(
         d_entry_attn * gain_rows[0] * (1.0 + shifts[1]), normed_one, inverse_one
     )
-    small = jnp.concatenate(
-        [
-            d_shift_attn,
-            d_scale_attn,
-            d_gate_attn,
-            d_shift_ffn,
-            d_scale_ffn,
-            d_gate_ffn,
-            d_gain_attn,
-            d_gain_cross,
-            d_gain_ffn,
+
+
+    d_gate_ffn = jnp.sum(d_result * branch_ffn, axis=0)
+    result = after_cross + shifts[5] * branch_ffn
+    branches = (result, shifts[2] * branch_attn, branch_cross, shifts[5] * branch_ffn)
+    stream_terms = jnp.stack([jnp.sum(keep_rows * branch * branch) for branch in branches])
+    vectors = [
+        d_shift_attn,
+        d_scale_attn,
+        d_gate_attn,
+        d_shift_ffn,
+        d_scale_ffn,
+        d_gate_ffn,
+        d_gain_attn,
+        d_gain_cross,
+        d_gain_ffn,
+    ]
+    small = stack_vectors(vectors)
+
+    beside = lambda halves: jnp.concatenate([halves[0], halves[1]], axis=1)
+    if grouped:
+        reduced, small, grad_in, grad_down, _ = reduce_group(
+            [
+                ("wide", [mixture_cross], d_cross_pair, 0),
+                ("tall", cross_pair, [d_query_cross], 1),
+                ("tall", [text_both], [d_key_cross, d_value_cross], 0),
+                ("wide", [mixture_attn], d_attn_pair, 1),
+                ("tall", entry_pair, [d_queries], 0),
+                ("tall", entry_pair, [d_keys], 1),
+                ("tall", entry_pair, [d_values], 0),
+            ],
+            small, grad_in.reshape(grid.ny, 2, grid.nb, rows, 2 * width),
+            grad_down.reshape(grid.na, -1, D), grid.na, rows,
+        )
+        small = small.reshape(count, -1, 128)[:, : 9 * D // 128].reshape(count, 9, D)
+        grad_cross, grad_out = beside(reduced[0]), beside(reduced[3])
+        grad_query, grad_ctx = (join(reduced[k, 0], reduced[k, 1]) for k in (1, 2))
+        qkv_parts = [reduced[4:, 0], reduced[4:, 1]]
+        turn_width = D // (2 * grid.ny)
+    else:
+        grad_down = lax.psum_scatter(grad_down, "z", tiled=True)
+        grad_in = grid.swap_back(grad_in.reshape(grid.ny, 2, grid.nb, rows, 2 * width), mine)
+        grad_in = grid.join_columns(grad_in, mine, spot)
+        small = grid.gather_small(small[: 9 * D // 128].reshape(9, D))
+        block = D // (2 * grid.ny)
+
+        def reduce(lefts, right, piece, halves=1):
+            groups = [[whole(array) for array in right]]
+            gradient = outer_sum(lefts, groups, piece, block, None, halves)
+            gradient = grid.fold(gradient.reshape(tall + (-1,)), "yczx", 0, mine)
+            return lax.psum_scatter(jnp.swapaxes(gradient, 0, 1), "z")
+
+        def reduce_tall(lefts, right, piece):
+            sums = reduce(lefts, right, piece)
+            return join(pick(sums, core, 0), grid.swap(pick(sums, 1 - core, 0)))
+
+        grad_cross = beside(reduce([mixture_cross], d_cross_pair, frames, 2))
+        grad_out = beside(reduce([mixture_attn], d_attn_pair, frames, 2))
+        grad_query = reduce_tall(cross_pair, [d_query_cross], frames)
+        grad_ctx = reduce_tall([text_both], [d_key_cross, d_value_cross], 2 * words)
+        qkv_parts = [
+            jnp.concatenate(
+                [reduce_tall(entry_pair, [d], frames) for d in (d_queries, d_keys, d_values)],
+                axis=1,
+            )
         ]
-    ).astype(BF16)
-    small = grid.gather_small(small)
-    grad_mod = dot_rows(lifted_own, small[:, : 6 * D])
-    gain_sums = jnp.sum(small[:, 6 * D :].astype(F32), axis=0).reshape(3, D)
+        turn_width = D
+    grad_ctx = jnp.concatenate([grad_ctx[: rows // 2], grad_ctx[rows // 2 :]], axis=1)
+    grad_square = jnp.stack([grad_out, grad_query, grad_cross])
+    grad_mod = jnp.einsum("nd,nkm->kdm", lifted_own, small[:, :6], preferred_element_type=F32)
+    gain_sums = jnp.sum(small[:, 6:].astype(F32), axis=0)
     grad_gains = lax.dynamic_slice(gain_sums, (0, device * rows), (3, rows))
-
-    summed = (
-        grad_mod,
-        grad_qkv,
-        jnp.stack([grad_out, grad_query, grad_cross]),
-        grad_ctx,
-        grad_in,
-        grad_down,
-        grad_gains,
-    )
-    masters = (mod_matrix, qkv_matrix, square_set, ctx_matrix, ff_in, ff_down, norm_gains)
-    firsts = (mod_first, qkv_first, square_first, ctx_first, in_first, down_first, gains_first)
-    seconds = (
-        mod_second,
-        qkv_second,
-        square_second,
-        ctx_second,
-        in_second,
-        down_second,
-        gains_second,
-    )
-    pending = []
-    weight_parts = []
-    update_parts = []
-    for weight, first_moment, second_moment, gradient in zip(masters, firsts, seconds, summed):
-        direction, first_new, second_new, weight_part, update_part = lamb_terms(
-            weight, first_moment, second_moment, gradient
-        )
-        weight_parts.append(weight_part)
-        update_parts.append(update_part)
-        pending.append((weight, direction, first_new, second_new))
-    totals = jnp.concatenate(
-        weight_parts + update_parts + [stream_terms, jnp.sum(lengths).astype(F32).reshape(1)]
-    )
-    totals = grid.sum_small(totals)
-    weight_norms = jnp.sqrt(totals[:9])
-    update_norms = jnp.sqrt(totals[9:18])
-    stream_rms = jnp.sqrt(totals[18:22] / (totals[22] * D))
-    ratios = weight_norms / update_norms
+    grad_down = grid.to_rank(grad_down, back=True)
+
+    lamb = functools.partial(lamb_terms, spot)
+    done = {}
+    done["qkv"] = lamb(qkv_matrix, qkv_first, qkv_second, qkv_parts, turn_width)
+    done["mod"] = lamb(mod_matrix, mod_first, mod_second, [grad_mod], D)
+    done["square"] = lamb(square_set, square_first, square_second, [grad_square], HALF)
+    done["ctx"] = lamb(ctx_matrix, ctx_first, ctx_second, [grad_ctx], D)
+    done["down"] = lamb(ff_down, down_first, down_second, [grad_down], 256)
+    done["in"] = lamb(ff_in, in_first, in_second, [grad_in], 1024)
+    done["gains"] = lamb_small(norm_gains, gains_first, gains_second, grad_gains)
+    names = ("mod", "qkv", "square", "ctx", "in", "down", "gains")
+    sums = [done[name][3] for name in names]
+    sums.append(jnp.stack([stream_terms, jnp.sum(lengths) * jnp.ones(4)]).T)
+    sums = jnp.concatenate(sums)
+    if grouped:
+        wanted = sums.shape
+        sums = jnp.pad(sums, ((0, -wanted[0] % 8), (0, 128 - wanted[1])))
+        sums = total_over_devices(sums, grid.na)[: wanted[0], : wanted[1]]
+    else:
+        sums = grid.sum_small(sums)
+    norms = jnp.sqrt(sums[:9])
+    weight_norms, update_norms = norms[:, 0], norms[:, 1]
+    stream_rms = jnp.sqrt(sums[9:, 0] / (sums[9:, 1] * D))
+    factors = RATE * (weight_norms / update_norms)
+    masters = [mod_matrix, qkv_matrix, square_set, ctx_matrix, ff_in, ff_down, norm_gains]
+    weights_new = step_weights(factors, masters, [done[name][2] for name in names])
     outputs = [result.astype(BF16)[None], d_latents.astype(BF16)[None]]
-    cursor = 0
-    for weight, direction, first_new, second_new in pending:
-        if weight.ndim == 3:
-            factor = ratios[cursor : cursor + weight.shape[0]].reshape(-1, 1, 1)
-            cursor = cursor + weight.shape[0]
-        else:
-            factor = ratios[cursor]
-            cursor = cursor + 1
-        outputs.append(weight - RATE * factor * direction)
-        outputs.append(first_new)
-        outputs.append(second_new)
+    for name, weight_new in zip(names, weights_new):
+        outputs += [weight_new, done[name][0], done[name][1]]
     outputs.append(weight_norms)
     outputs.append(update_norms)
     outputs.append(stream_rms)

time: 1050 us -> 916 us (0.87)
  Pallas kernels: 67.1 us -> 615 us
  waiting for transfers between devices: 431 us -> 115 us
  matrix products: 149 us -> 3.84 us
  local copies, waits for them, and re-layouts: 144 us -> 63.4 us
  other arithmetic: 136 us -> 56 us
  starting transfers between devices: 96.7 us -> 38.4 us
    pallas_call x0 -> x26, Pallas kernels: none -> 548 us  [the longest x1 204 us: reduce_group(): pl.pallas_call(functools.partial(reduce_kernel, plan=plan, inputs=len(arr...]
    ppermute x89 -> x35, waiting for transfers between devices: 368 us -> 115 us  [move(): return lax.ppermute(array, names, pairs)]
    dot_general x21 -> x1, matrix products: 109 us -> 1.23 us  [shards(): jnp.einsum('nd,nkm->kdm', lifted_own, small[:, :6], preferred_element_typ...]
    all_gather x2 -> x3, waiting for transfers between devices: 57.6 us -> 0.02 us  [gather_weights(): lines = lax.all_gather(mixed, 'z')]
    ppermute x89 -> x35, starting transfers between devices: 78 us -> 30.4 us  [move(): return lax.ppermute(array, names, pairs)]
    dot_general x15 -> x3, matrix products: 40.5 us -> 2.61 us  [dot(): return jnp.dot(first, second, preferred_element_type=F32)]
    convert_element_type x22 -> x7, other arithmetic: 35 us -> 5.79 us  [the longest x1 1.59 us: shards(): (normed_three * gain_rows[2] * (1.0 + shifts[4]) + shifts[3]).astype(BF16)]
    unnamed x389 -> x243, local copies, waits for them, and re-layouts: 66.4 us -> 41.9 us
  transfers between devices with their start and end apart: 103 -> 42, of which waited for: 43 -> 23; matrix products, arithmetic and copies ran while one was open for 32% -> 8% of each run, Pallas kernels for 6% -> 21%
where the time goes in v2:
time: 916 us; the launch traced here: 908 us
  Pallas kernels  615 us (67%)
  waiting for transfers between devices  115 us (13%)
  local copies, waits for them, and re-layouts  63.4 us (7%)
  other arithmetic  56 us (6%)
  starting transfers between devices  38.4 us (4%)
  between operations  16.7 us (2%)
    pallas_call x1, Pallas kernels, reduce_group(): pl.pallas_call(functools.partial(reduce_kernel, plan=plan, inputs=len(arr...  204 us
    pallas_call x1, Pallas kernels, ffn_group(): pl.pallas_call(functools.partial(ffn_group_kernel, chips=chips, sizes=siz...  189 us
    ppermute x35, waiting for transfers between devices, move(): return lax.ppermute(array, names, pairs)  115 us
    pallas_call x1, Pallas kernels, sum_shifts(): pl.pallas_call(shift_kernel, out_shape=[jax.ShapeDtypeStruct((rows, 128),...  59.8 us
    unnamed x243, local copies, waits for them, and re-layouts  41.9 us
    pallas_call x2, Pallas kernels, attend_back(): pl.pallas_call(attend_back_kernel, out_shape=[jax.ShapeDtypeStruct((2 * r...  30.8 us
    ppermute x35, starting transfers between devices, move(): return lax.ppermute(array, names, pairs)  30.4 us
    pallas_call x2, Pallas kernels, attend(): pl.pallas_call(attend_kernel, out_shape=jax.ShapeDtypeStruct((2 * frames,...  26.3 us
  transfers between devices with their start and end apart: 42, of which 23 were waited for; matrix products, arithmetic and copies ran while one was open for 8% of the time, Pallas kernels for 21%

profile of v2, /device:TPU:0, one launch (start us, length us, event | category | flops | bytes accessed | tf_op | source)
XLA Modules:
  0.0 908.0 jit_solution(2985552272981188314)
XLA Ops:
  23.8 4.2 collective-permute-start.4
  41.5 59.8 %shard_map.451 = (f32[72,128]{1,0:T(8,128)S(1)}, bf16[8,384,1536]{2,1,0:T(8,128)(2,1)S(1)}, bf16[2,2,2,48,1536]{4,3,2,1,0:T(8,128)(2,1)S(1)}) custom-call(f32[2,2,4,2,72,128]{5,4,3,2,1,0:T(8,128)S(1)} %bitcast.248, bf16[384,1536]{1,0:T(8,128)(2,1)S(1)} %fusion.23.cot_hbm, bf16[2,2,2,48,1536]{4,3,2,1,0:T(8,128)(2,1)S(1)} %bitcast.259), custom_call_target="tpu_custom_call" | custom-call | flops 1048576 | bytes 1048576 | tf_op jit(solution)/shard_map/pallas_call | solution.py:1007
  114.4 17.9 %collective-permute-done.12.refs_5_.refs_2_ = bf16[4,3,48,768]{3,2,1,0:T(8,128)(2,1)S(1)} collective-permute-done((bf16[4,3,48,768]{3,2,1,0:T(8,128)(2,1)}, bf16[4,3,48,768]{3,2,1,0:T(8,128)(2,1)S(1)}, u32[]{:S(2)}, u32[]{:S(2)}) %collective-permute-start.12) | collective-permute-done | bytes 884768 | tf_op jit(solution)/shard_map/ppermute | solution.py:1573
  135.2 5.9 collective-permute-start.31
  141.1 10.8 %collective-permute-done.13.refs_6_ = bf16[4,3,48,768]{3,2,1,0:T(8,128)(2,1)} collective-permute-done((bf16[4,3,48,768]{3,2,1,0:T(8,128)(2,1)}, bf16[4,3,48,768]{3,2,1,0:T(8,128)(2,1)}, u32[]{:S(2)}, u32[]{:S(2)}) %collective-permute-start.13) | collective-permute-done | bytes 884768 | tf_op jit(solution)/shard_map/ppermute | solution.py:1573
  151.9 10.1 %collective-permute-done.9.refs_1_ = bf16[4,3,48,768]{3,2,1,0:T(8,128)(2,1)} collective-permute-done((bf16[4,3,48,768]{3,2,1,0:T(8,128)(2,1)}, bf16[4,3,48,768]{3,2,1,0:T(8,128)(2,1)}, u32[]{:S(2)}, u32[]{:S(2)}) %collective-permute-start.9) | collective-permute-done | bytes 884768 | tf_op jit(solution)/shard_map/ppermute | solution.py:1573
  162.1 7.3 collective-permute-done.14.refs_7_
  169.3 10.3 %collective-permute-done.11.refs_3_ = bf16[4,3,48,768]{3,2,1,0:T(8,128)(2,1)} collective-permute-done((bf16[4,3,48,768]{3,2,1,0:T(8,128)(2,1)S(1)}, bf16[4,3,48,768]{3,2,1,0:T(8,128)(2,1)}, u32[]{:S(2)}, u32[]{:S(2)}) %collective-permute-start.11) | collective-permute-done | bytes 884768 | tf_op jit(solution)/shard_map/ppermute | solution.py:1573
  201.4 11.5 %collective-permute-done.18.refs_5_.refs_2_ = bf16[4,2,48,768]{3,2,1,0:T(8,128)(2,1)S(1)} collective-permute-done((bf16[4,2,48,768]{3,2,1,0:T(8,128)(2,1)S(1)}, bf16[4,2,48,768]{3,2,1,0:T(8,128)(2,1)S(1)}, u32[]{:S(2)}, u32[]{:S(2)}) %collective-permute-start.18) | collective-permute-done | bytes 589856 | tf_op jit(solution)/shard_map/ppermute | solution.py:1573
  218.8 9.3 %shard_map.454.query_ref.key_ref.value_ref = bf16[768,2304]{1,0:T(8,128)(2,1)S(1)} custom-call(bf16[384,1536]{1,0:T(8,128)(2,1)S(1)} %copy-done.8, bf16[384,1536]{1,0:T(8,128)(2,1)S(1)} %collective-permute-done.8.other_ref.refs_13_, bf16[1536,2304]{1,0:T(8,128)(2,1)} %bitcast.235), custom_call_target="tpu_custom_call" | custom-call | flops 1048576 | bytes 1048576 | tf_op jit(solution)/shard_map/pallas_call | solution.py:811
  228.1 14.4 %shard_map.455.refs_0_.refs_9_ = bf16[768,768]{1,0:T(8,128)(2,1)S(1)} custom-call(s32[2]{0:T(128)S(1)} %pad_add_fusion.1.valid_ref, bf16[768,2304]{1,0:T(8,128)(2,1)S(1)} %shard_map.454.query_ref.key_ref.value_ref, bf16[768,2304]{1,0:T(8,128)(2,1)S(1)} %shard_map.454.query_ref.key_ref.value_ref, bf16[768,2304]{1,0:T(8,128)(2,1)S(1)} %shard_map.454.query_ref.key_ref.value_ref), custom_call_target="tpu_custom_call" | custom-call | flops 1048576 | bytes 1048576 | tf_op jit(solution)/shard_map/pallas_call | solution.py:140
  246.5 4.1 shard_map.458
  263.2 7.3 collective-permute-done.27.refs_5_
  278.4 5.4 collective-permute-done.28.refs_6_
  283.8 12.0 %collective-permute-done.29.refs_7_ = bf16[4,2,48,768]{3,2,1,0:T(8,128)(2,1)} collective-permute-done((bf16[4,2,48,768]{3,2,1,0:T(8,128)(2,1)}, bf16[4,2,48,768]{3,2,1,0:T(8,128)(2,1)}, u32[]{:S(2)}, u32[]{:S(2)}) %collective-permute-start.29) | collective-permute-done | bytes 589856 | tf_op jit(solution)/shard_map/ppermute | solution.py:1573
  303.6 11.9 %shard_map.462.refs_0_ = bf16[768,768]{1,0:T(8,128)(2,1)S(1)} custom-call(s32[2]{0:T(128)S(1)} %broadcast_13_valid_ref.2.valid_ref, bf16[768,768]{1,0:T(8,128)(2,1)S(1)} %shard_map.459.query_ref, bf16[512,768]{1,0:T(8,128)(2,1)S(1)} %convolution_convert_fusion.key_ref.value_ref, bf16[512,768]{1,0:T(8,128)(2,1)S(1)} %convolution_convert_fusion.key_ref.value_ref), custom_call_target="tpu_custom_call" | custom-call | flops 1048576 | bytes 1048576 | tf_op jit(solution)/shard_map/pallas_call | solution.py:140
  316.6 4.5 shard_map.463
  339.5 189.3 %shard_map.467 = (f32[384,1536]{1,0:T(8,128)}, bf16[768,1536]{1,0:T(8,128)(2,1)}, bf16[4,4,96,1536]{3,2,1,0:T(8,128)(2,1)}, f32[384,1536]{1,0:T(8,128)}, bf16[38...) custom-call(bf16[384,1536]{1,0:T(8,128)(2,1)} %add_convert_fusion.en, ...), custom_call_target="tpu_custom_call" | custom-call | flops 1048576 | bytes 1048576 | tf_op jit(solution)/shard_map/pallas_call | solution.py:1316
  530.5 7.6 fusion.17
  544.6 11.4 %shard_map.469 = (bf16[768,768]{1,0:T(8,128)(2,1)S(1)}, bf16[256,768]{1,0:T(8,128)(2,1)S(1)}, bf16[256,768]{1,0:T(8,128)(2,1)S(1)}) custom-call(s32[2]{0:T(128)S(1)} %broadcast_13_valid_ref.2.valid_ref, bf16[768,768]{1,0:T(8,128)(2,1)S(1)} %copy-done.16, bf16[512,768]{1,0:T(8,128)(2,1)S(1)} %convolution_convert_fusion.key_ref.value_ref, ...), custom_call_target="tpu_custom_call" | custom-call | flops 1048576 | bytes 1048576 | tf_op jit(solution)/shard_map/pallas_call | solution.py:154
  556.0 4.9 shard_map.470
  565.5 4.0 fusion.18
  575.1 19.4 %shard_map.472 = (bf16[768,768]{1,0:T(8,128)(2,1)S(1)}, bf16[768,768]{1,0:T(8,128)(2,1)S(1)}, bf16[768,768]{1,0:T(8,128)(2,1)S(1)}) custom-call(s32[2]{0:T(128)S(1)} %pad_add_fusion.1.valid_ref, bf16[768,2304]{1,0:T(8,128)(2,1)} %copy-done, bf16[768,2304]{1,0:T(8,128)(2,1)} %copy-done, bf16[768,2304]{1,0:T(8,128)(2,1)} %copy-done, ...), custom_call_target="tpu_custom_call" | custom-call | flops 1048576 | bytes 1048576 | tf_op jit(solution)/shard_map/pallas_call | solution.py:154
  594.6 11.8 %shard_map.473 = (f32[384,1536]{1,0:T(8,128)}, bf16[384,1536]{1,0:T(8,128)(2,1)S(1)}) custom-call(bf16[768,768]{1,0:T(8,128)(2,1)S(1)} %get-tuple-element.114.refs_0_.refs_14_, bf16[768,768]{1,0:T(8,128)(2,1)S(1)} %get-tuple-element.115.refs_1_.refs_15_, bf16[768,768]{1,0:T(8,128)(2,1)S(1)} %get-tuple-element.116.refs_2_.refs_16_, bf16[1536,2304]{1,0:T(8,128)(2,1)} %bitcast.236), custom_call_target="tpu_custom_call" | custom-call | flops 1048576 | bytes 1048576 | tf_op jit(solution)/shard_map/pallas_call | solution.py:847
  612.1 5.3 multiply_reduce_fusion.2
  618.9 4.4 fusion.29
  623.2 204.2 %shard_map.475 = (bf16[7,2,48,768]{3,2,1,0:T(8,128)(2,1)}, bf16[2,2,4,2,112,128]{5,4,3,2,1,0:T(8,128)(2,1)}, bf16[48,12288]{1,0:T(8,128)(2,1)}, bf16[192,1536]{1,0:T(8,128)(2,1)}, bf16[3,192,1536]{2,1,0:T(8,128)(2,1)}) custom-call(bf16[768,768]{1,0:T(8,128)(2,1)} %copy-done.10, bf16[384,1536]{1,0:T(8,128)(2,1)} %copy-done.9, bf16[384,1536]{1,0:T(8,128)(2,1)} %copy-done.39, ...), custom_call_target="tpu_custom_call" | custom-call | flops 1048576 | bytes 1048576 | tf_op jit(solution)/shard_map/pallas_call | solution.py:745
  846.3 5.5 shard_map.477
  852.8 4.6 shard_map.476
  858.6 6.9 shard_map.480
  871.7 17.9 %shard_map.482 = f32[16,128]{1,0:T(8,128)} custom-call(f32[16,128]{1,0:T(8,128)} %pad.7.sums_ref), custom_call_target="tpu_custom_call" | custom-call | flops 1048576 | bytes 1048576 | tf_op jit(solution)/shard_map/pallas_call | solution.py:1435
  892.6 8.4 shard_map.483
  (445 shorter events, 179.2 us)
Async XLA Ops:
  7.2 99.4 %all-gather.9.cloned.1.call-start = ((), (), s32[]{:S(2)}) async-start(), calls=%async_computation.2 | async-start | bytes 2211840 | tf_op jit(solution)/shard_map/all_gather | solution.py:1627
  16.8 177.5 %all-gather.11.cloned.1.call-start = ((), (), s32[]{:S(2)}) async-start(), calls=%async_computation.3 | async-start | bytes 1474560 | tf_op jit(solution)/shard_map/all_gather | solution.py:1627
  17.8 233.7 %all-gather.13.cloned.1.call-start = ((), (), s32[]{:S(2)}) async-start(), calls=%async_computation.4 | async-start | bytes 1474560 | tf_op jit(solution)/shard_map/all_gather | solution.py:1627
  23.8 5.9 collective-permute-start.4
  28.0 5.1 collective-permute-start.3
  28.0 5.5 collective-permute-start.2
  109.5 22.8 %collective-permute-start.12 = (bf16[4,3,48,768]{3,2,1,0:T(8,128)(2,1)}, bf16[4,3,48,768]{3,2,1,0:T(8,128)(2,1)S(1)}, u32[]{:S(2)}, u32[]{:S(2)}) collective-permute-start(bf16[4,3,48,768]{3,2,1,0:T(8,128)(2,1)} %get-tuple-element.199.refs_4_), channel_id=1, source_target_pairs={{0,1},{1,0},{2,3},{3,2},{4,5},{5,4},{6,7},{7,6},{8,9},{9,8},{10,11... | collective-permute-start | bytes 2654216 | tf_op jit(solution)/shard_map/ppermute | solution.py:1573
  110.1 23.8 %collective-permute-start.10 = (bf16[4,3,48,768]{3,2,1,0:T(8,128)(2,1)}, bf16[4,3,48,768]{3,2,1,0:T(8,128)(2,1)S(1)}, u32[]{:S(2)}, u32[]{:S(2)}) collective-permute-start(bf16[4,3,48,768]{3,2,1,0:T(8,128)(2,1)} %get-tuple-element.200.refs_0_), channel_id=1, source_target_pairs={{0,16},{16,0},{1,17},{17,1},{2,18},{18,2},{3,19},{19,3},{4,20},{20... | collective-permute-start | bytes 2654216 | tf_op jit(solution)/shard_map/ppermute | solution.py:1573
  112.3 219.2 %all-gather.15.cloned.1.call-start = ((), (), s32[]{:S(2)}) async-start(), calls=%async_computation.5 | async-start | bytes 8847360 | tf_op jit(solution)/shard_map/all_gather | solution.py:1689
  112.3 39.6 %collective-permute-start.13 = (bf16[4,3,48,768]{3,2,1,0:T(8,128)(2,1)}, bf16[4,3,48,768]{3,2,1,0:T(8,128)(2,1)}, u32[]{:S(2)}, u32[]{:S(2)}) collective-permute-start(bf16[4,3,48,768]{3,2,1,0:T(8,128)(2,1)} %get-tuple-element.199.refs_4_), channel_id=1, source_target_pairs={{0,16},{16,0},{1,17},{17,1},{2,18},{18,2},{3,19},{19,3},{4,20},{20... | collective-permute-start | bytes 2654216 | tf_op jit(solution)/shard_map/ppermute | solution.py:1573
  113.0 49.1 %collective-permute-start.9 = (bf16[4,3,48,768]{3,2,1,0:T(8,128)(2,1)}, bf16[4,3,48,768]{3,2,1,0:T(8,128)(2,1)}, u32[]{:S(2)}, u32[]{:S(2)}) collective-permute-start(bf16[4,3,48,768]{3,2,1,0:T(8,128)(2,1)} %get-tuple-element.200.refs_0_), channel_id=1, source_target_pairs={{0,1},{1,0},{2,3},{3,2},{4,5},{5,4},{6,7},{7,6},{8,9},{9,8},{10,11... | collective-permute-start | bytes 2654216 | tf_op jit(solution)/shard_map/ppermute | solution.py:1573
  132.3 37.0 %collective-permute-start.14 = (bf16[4,3,48,768]{3,2,1,0:T(8,128)(2,1)S(1)}, bf16[4,3,48,768]{3,2,1,0:T(8,128)(2,1)}, u32[]{:S(2)}, u32[]{:S(2)}) collective-permute-start(bf16[4,3,48,768]{3,2,1,0:T(8,128)(2,1)S(1)} %collective-permute-done.12.refs_5_.refs_2_), channel_id=1, source_target_pairs={{0,16},{16,0},{1,17},{17,1},{2,18},{18,2},{3,19},{19,3},{4,20},{20... | collective-permute-start | bytes 2654216 | tf_op jit(solution)/shard_map/ppermute | solution.py:1573
  133.9 45.8 %collective-permute-start.11 = (bf16[4,3,48,768]{3,2,1,0:T(8,128)(2,1)S(1)}, bf16[4,3,48,768]{3,2,1,0:T(8,128)(2,1)}, u32[]{:S(2)}, u32[]{:S(2)}) collective-permute-start(bf16[4,3,48,768]{3,2,1,0:T(8,128)(2,1)S(1)} %collective-permute-done.10.refs_2_.refs_1_), channel_id=1, source_target_pairs={{0,1},{1,0},{2,3},{3,2},{4,5},{5,4},{6,7},{7,6},{8,9},{9,8},{10,11... | collective-permute-start | bytes 2654216 | tf_op jit(solution)/shard_map/ppermute | solution.py:1573
  135.2 50.7 %collective-permute-start.31 = (bf16[192,1536]{1,0:T(8,128)(2,1)}, bf16[192,1536]{1,0:T(8,128)(2,1)}, u32[]{:S(2)}, u32[]{:S(2)}) collective-permute-start(bf16[192,1536]{1,0:T(8,128)(2,1)} %shard_map.464), channel_id=1, source_target_pairs={{0,0},{1,2},{2,4},{3,6},{4,1},{5,3},{6,5},{7,7},{8,8},{9,10},{10,1... | collective-permute-start | bytes 1769480 | tf_op jit(solution)/shard_map/ppermute | solution.py:1749
  189.6 433.6 %reduce-scatter.2.cloned.1.call-start = ((), (), s32[]{:S(2)}) async-start(), calls=%async_computation.1 | async-start | bytes 5898240 | tf_op jit(solution)/shard_map/reduce_scatter | solution.py:1986
  194.2 22.8 %collective-permute-start.8 = (bf16[384,1536]{1,0:T(8,128)(2,1)S(1)}, bf16[384,1536]{1,0:T(8,128)(2,1)S(1)}, u32[]{:S(2)}, u32[]{:S(2)}) collective-permute-start(bf16[384,1536]{1,0:T(8,128)(2,1)S(1)} %fusion.10.own_ref.refs_12_), channel_id=1, source_target_pairs={{0,8},{8,0},{1,9},{9,1},{2,10},{10,2},{3,11},{11,3},{4,12},{12,4},... | collective-permute-start | bytes 3538952 | tf_op jit(solution)/shard_map/ppermute | solution.py:1573
  196.1 16.8 %collective-permute-start.18 = (bf16[4,2,48,768]{3,2,1,0:T(8,128)(2,1)S(1)}, bf16[4,2,48,768]{3,2,1,0:T(8,128)(2,1)S(1)}, u32[]{:S(2)}, u32[]{:S(2)}) collective-permute-start(bf16[4,2,48,768]{3,2,1,0:T(8,128)(2,1)S(1)} %get-tuple-element.203.refs_4_), channel_id=1, source_target_pairs={{0,1},{1,0},{2,3},{3,2},{4,5},{5,4},{6,7},{7,6},{8,9},{9,8},{10,11... | collective-permute-start | bytes 1769480 | tf_op jit(solution)/shard_map/ppermute | solution.py:1573
  198.8 16.2 %collective-permute-start.16 = (bf16[4,2,48,768]{3,2,1,0:T(8,128)(2,1)S(1)}, bf16[4,2,48,768]{3,2,1,0:T(8,128)(2,1)S(1)}, u32[]{:S(2)}, u32[]{:S(2)}) collective-permute-start(bf16[4,2,48,768]{3,2,1,0:T(8,128)(2,1)S(1)} %get-tuple-element.204.refs_0_), channel_id=1, source_target_pairs={{0,16},{16,0},{1,17},{17,1},{2,18},{18,2},{3,19},{19,3},{4,20},{20... | collective-permute-start | bytes 1769480 | tf_op jit(solution)/shard_map/ppermute | solution.py:1573
  200.1 42.4 %collective-permute-start.19 = (bf16[4,2,48,768]{3,2,1,0:T(8,128)(2,1)S(1)}, bf16[4,2,48,768]{3,2,1,0:T(8,128)(2,1)S(1)}, u32[]{:S(2)}, u32[]{:S(2)}) collective-permute-start(bf16[4,2,48,768]{3,2,1,0:T(8,128)(2,1)S(1)} %get-tuple-element.203.refs_4_), channel_id=1, source_target_pairs={{0,16},{16,0},{1,17},{17,1},{2,18},{18,2},{3,19},{19,3},{4,20},{20... | collective-permute-start | bytes 1769480 | tf_op jit(solution)/shard_map/ppermute | solution.py:1573
  201.4 41.2 %collective-permute-start.15 = (bf16[4,2,48,768]{3,2,1,0:T(8,128)(2,1)S(1)}, bf16[4,2,48,768]{3,2,1,0:T(8,128)(2,1)S(1)}, u32[]{:S(2)}, u32[]{:S(2)}) collective-permute-start(bf16[4,2,48,768]{3,2,1,0:T(8,128)(2,1)S(1)} %get-tuple-element.204.refs_0_), channel_id=1, source_target_pairs={{0,1},{1,0},{2,3},{3,2},{4,5},{5,4},{6,7},{7,6},{8,9},{9,8},{10,11... | collective-permute-start | bytes 1769480 | tf_op jit(solution)/shard_map/ppermute | solution.py:1573
  212.9 29.6 %collective-permute-start.20 = (bf16[4,2,48,768]{3,2,1,0:T(8,128)(2,1)S(1)}, bf16[4,2,48,768]{3,2,1,0:T(8,128)(2,1)S(1)}, u32[]{:S(2)}, u32[]{:S(2)}) collective-permute-start(bf16[4,2,48,768]{3,2,1,0:T(8,128)(2,1)S(1)} %collective-permute-done.18.refs_5_.refs_2_), channel_id=1, source_target_pairs={{0,16},{16,0},{1,17},{17,1},{2,18},{18,2},{3,19},{19,3},{4,20},{20... | collective-permute-start | bytes 1769480 | tf_op jit(solution)/shard_map/ppermute | solution.py:1573
  215.0 27.5 %collective-permute-start.17 = (bf16[4,2,48,768]{3,2,1,0:T(8,128)(2,1)S(1)}, bf16[4,2,48,768]{3,2,1,0:T(8,128)(2,1)S(1)}, u32[]{:S(2)}, u32[]{:S(2)}) collective-permute-start(bf16[4,2,48,768]{3,2,1,0:T(8,128)(2,1)S(1)} %collective-permute-done.16.refs_2_.refs_1_), channel_id=1, source_target_pairs={{0,1},{1,0},{2,3},{3,2},{4,5},{5,4},{6,7},{7,6},{8,9},{9,8},{10,11... | collective-permute-start | bytes 1769480 | tf_op jit(solution)/shard_map/ppermute | solution.py:1573
  250.6 5.5 collective-permute-start.21
  254.0 16.4 %collective-permute-start.27 = (bf16[4,2,48,768]{3,2,1,0:T(8,128)(2,1)}, bf16[4,2,48,768]{3,2,1,0:T(8,128)(2,1)}, u32[]{:S(2)}, u32[]{:S(2)}) collective-permute-start(bf16[4,2,48,768]{3,2,1,0:T(8,128)(2,1)} %get-tuple-element.201.refs_4_), channel_id=1, source_target_pairs={{0,1},{1,0},{2,3},{3,2},{4,5},{5,4},{6,7},{7,6},{8,9},{9,8},{10,11... | collective-permute-start | bytes 1769480 | tf_op jit(solution)/shard_map/ppermute | solution.py:1573
  254.7 16.5 %collective-permute-start.25 = (bf16[4,2,48,768]{3,2,1,0:T(8,128)(2,1)}, bf16[4,2,48,768]{3,2,1,0:T(8,128)(2,1)}, u32[]{:S(2)}, u32[]{:S(2)}) collective-permute-start(bf16[4,2,48,768]{3,2,1,0:T(8,128)(2,1)} %get-tuple-element.202.refs_0_), channel_id=1, source_target_pairs={{0,16},{16,0},{1,17},{17,1},{2,18},{18,2},{3,19},{19,3},{4,20},{20... | collective-permute-start | bytes 1769480 | tf_op jit(solution)/shard_map/ppermute | solution.py:1573
  259.3 40.7 %collective-permute-start.22 = (bf16[384,1536]{1,0:T(8,128)(2,1)S(1)}, bf16[384,1536]{1,0:T(8,128)(2,1)S(1)}, u32[]{:S(2)}, u32[]{:S(2)}) collective-permute-start(bf16[384,1536]{1,0:T(8,128)(2,1)S(1)} %multiply_convert_fusion.1.own_ref.refs_3_), channel_id=1, source_target_pairs={{0,8},{8,0},{1,9},{9,1},{2,10},{10,2},{3,11},{11,3},{4,12},{12,4},... | collective-permute-start | bytes 3538952 | tf_op jit(solution)/shard_map/ppermute | solution.py:1573
  260.1 23.7 %collective-permute-start.28 = (bf16[4,2,48,768]{3,2,1,0:T(8,128)(2,1)}, bf16[4,2,48,768]{3,2,1,0:T(8,128)(2,1)S(1)}, u32[]{:S(2)}, u32[]{:S(2)}) collective-permute-start(bf16[4,2,48,768]{3,2,1,0:T(8,128)(2,1)} %get-tuple-element.201.refs_4_), channel_id=1, source_target_pairs={{0,16},{16,0},{1,17},{17,1},{2,18},{18,2},{3,19},{19,3},{4,20},{20... | collective-permute-start | bytes 1769480 | tf_op jit(solution)/shard_map/ppermute | solution.py:1573
  262.5 21.3 %collective-permute-start.24 = (bf16[4,2,48,768]{3,2,1,0:T(8,128)(2,1)}, bf16[4,2,48,768]{3,2,1,0:T(8,128)(2,1)}, u32[]{:S(2)}, u32[]{:S(2)}) collective-permute-start(bf16[4,2,48,768]{3,2,1,0:T(8,128)(2,1)} %get-tuple-element.202.refs_0_), channel_id=1, source_target_pairs={{0,1},{1,0},{2,3},{3,2},{4,5},{5,4},{6,7},{7,6},{8,9},{9,8},{10,11... | collective-permute-start | bytes 1769480 | tf_op jit(solution)/shard_map/ppermute | solution.py:1573
  270.4 25.3 %collective-permute-start.29 = (bf16[4,2,48,768]{3,2,1,0:T(8,128)(2,1)}, bf16[4,2,48,768]{3,2,1,0:T(8,128)(2,1)}, u32[]{:S(2)}, u32[]{:S(2)}) collective-permute-start(bf16[4,2,48,768]{3,2,1,0:T(8,128)(2,1)} %collective-permute-done.27.refs_5_), channel_id=1, source_target_pairs={{0,16},{16,0},{1,17},{17,1},{2,18},{18,2},{3,19},{19,3},{4,20},{20... | collective-permute-start | bytes 1769480 | tf_op jit(solution)/shard_map/ppermute | solution.py:1573
  271.2 24.5 %collective-permute-start.26 = (bf16[4,2,48,768]{3,2,1,0:T(8,128)(2,1)}, bf16[4,2,48,768]{3,2,1,0:T(8,128)(2,1)}, u32[]{:S(2)}, u32[]{:S(2)}) collective-permute-start(bf16[4,2,48,768]{3,2,1,0:T(8,128)(2,1)} %collective-permute-done.25.refs_2_), channel_id=1, source_target_pairs={{0,1},{1,0},{2,3},{3,2},{4,5},{5,4},{6,7},{7,6},{8,9},{9,8},{10,11... | collective-permute-start | bytes 1769480 | tf_op jit(solution)/shard_map/ppermute | solution.py:1573
  606.5 5.6 collective-permute-start.35
  832.4 33.6 %collective-permute-start.36 = (bf16[192,1536]{1,0:T(8,128)(2,1)}, bf16[192,1536]{1,0:T(8,128)(2,1)S(1)}, u32[]{:S(2)}, u32[]{:S(2)}) collective-permute-start(bf16[192,1536]{1,0:T(8,128)(2,1)} %get-tuple-element.131), channel_id=1, source_target_pairs={{0,0},{2,1},{4,2},{6,3},{1,4},{3,5},{5,6},{7,7},{8,8},{10,9},{12,1... | collective-permute-start | bytes 1769480 | tf_op jit(solution)/shard_map/ppermute | solution.py:1749
  (128 other events, 869.7 us)
Sparse Core Ops, SparseCore 0:
  16.9 55.4 all-gather.8
  74.6 29.5 all-gather.10
  112.4 27.8 all-gather.12
  189.7 127.5 all-gather.14
  528.9 83.4 reduce-scatter.1

commit v3 on v2

--- a/solution.py
+++ b/solution.py
@@ -93,9 +93,7 @@
     return jnp.where(lane < HEAD_DIM, first, second)
 
 
-def attend_kernel(valid_ref, query_ref, key_ref, value_ref, out_ref):
-    valid = valid_ref[pl.program_id(0)]
-    query, key, value = query_ref[...], key_ref[...], value_ref[...]
+def attend_heads(valid, query, key, value):
     mixed = []
     for head in range(2):
         scores = dot_back(only(query, head), key) * SCALE
@@ -104,7 +102,12 @@
         powers = jnp.exp(scores - jnp.max(scores, axis=-1, keepdims=True))
         chances = (powers / jnp.sum(powers, axis=-1, keepdims=True)).astype(BF16)
         mixed.append(dot(chances, value))
-    out_ref[...] = both_heads(*mixed).astype(BF16)
+    return both_heads(*mixed).astype(BF16)
+
+
+def attend_kernel(valid_ref, query_ref, key_ref, value_ref, out_ref):
+    valid = valid_ref[pl.program_id(0)]
+    out_ref[...] = attend_heads(valid, query_ref[...], key_ref[...], value_ref[...])
 
 
 def attend_back_kernel(
@@ -176,7 +179,8 @@
 def place_pieces(spot_ref, *refs, plan, sizes):
     ny, nb = sizes
     count = len(plan["offsets"]) * len(plan["parts"])
-    pieces, outs, sem = refs[:count], refs[count:-1], refs[-1]
+    pieces, sem = refs[:count], refs[-1]
+    outs = refs[-1 - plan["outs"] : -1]
     y, x = spot_ref[0], spot_ref[3]
     copies = []
     for part, blocks in enumerate(plan["parts"]):
@@ -246,7 +250,7 @@
     spot_ref, qkv_ref, square_ref, ctx_ref, in_ref, own_ref, other_ref, wide_ref, block_ref,
     *, offsets, sizes
 ):
-    ny, nb = sizes
+    ny, na, nb = sizes
     y, c, x = spot_ref[0], spot_ref[1], spot_ref[3]
     part = D // (2 * ny)
     for out_ref, which in ((own_ref, c), (other_ref, 1 - c)):
@@ -270,13 +274,153 @@
             values = square_ref[matrix, :, side * HALF : (side + 1) * HALF]
             wide_ref[2 * k + side] = values.astype(BF16)
     width = FF // len(offsets)
+    share = width // na
     for k, (dy, dc, dx) in enumerate(offsets):
-        rank = (lax.rem(y + dy, ny) * 2 + lax.rem(c + dc, 2)) * nb + lax.rem(x + dx, nb)
+        rank = lax.rem(y + dy, ny) * 2 + lax.rem(c + dc, 2)
+        first = lax.rem(x + dx, nb) == 0
         for side in range(2):
-            start = pl.multiple_of(side * FF + rank * width, width)
-            block_ref[k, :, side * width : (side + 1) * width] = in_ref[
-                :, pl.ds(start, width)
-            ].astype(BF16)
+            for z in range(na):
+                start = pl.multiple_of(side * FF + (rank * na + z) * nb * share, 128)
+                values = in_ref[:, pl.ds(start, nb * share)].astype(BF16)
+                values = jnp.where(first, values[:, :share], values[:, share:])
+                at = side * width + z * share
+                block_ref[k, :, at : at + share] = values
+
+
+BLOCKS = [(0, lane, k * HALF) for k in range(3) for lane in range(2)]
+BLOCKS += [(1, None, 0), (1, None, HALF), (2, 0, 0), (2, 1, 0)]
+BLOCKS += [(3, 0, 0), (3, 1, 0), (4, None, 0), (4, None, HALF)]
+ACROSS = (0, 1, 2, 6, 7, 10, 11)
+
+
+def gather_kernel(
+    valid_ref, own_hbm, other_hbm, lines_hbm,
+    mixture_ref, qkv_ref, *refs,
+):
+    outs, arrays = refs[:5], refs[5:10]
+    entry, x_send, x_recv, y_send, y_recv, on_send, on_recv, own_sem, load_sem, out_sem = refs[10:]
+    y, x = lax.axis_index("y"), lax.axis_index("x")
+    far_y, far_x = 1 - y, 1 - x
+    frames = entry.shape[1]
+
+    def place_of(block, at_y, at_x):
+        array, lane, column = BLOCKS[block]
+        columns = pl.ds(column, HALF)
+        if lane is None:
+            return arrays[array].at[at_y, :, at_x, :, columns]
+        return arrays[array].at[at_y, lane, :, at_x, :, columns]
+
+    def remote(source, target, send, recv, device):
+        return pltpu.make_async_remote_copy(
+            src_ref=source,
+            dst_ref=target,
+            send_sem=send,
+            recv_sem=recv,
+            device_id=device,
+            device_id_type=pl.DeviceIdType.MESH,
+        )
+
+    barrier = pltpu.get_barrier_semaphore()
+    for device in ({"y": far_y}, {"x": far_x}):
+        pl.semaphore_signal(
+            barrier, inc=1, device_id=device, device_id_type=pl.DeviceIdType.MESH
+        )
+    pl.semaphore_wait(barrier, 2)
+    count = len(BLOCKS)
+    to_x, to_y, onward, own = [], [], [], []
+    for b in range(count):
+        here = place_of(b, y, x)
+        to_x.append(remote(lines_hbm.at[:, b], here, x_send.at[b], x_recv.at[b], {"x": far_x}))
+        to_y.append(remote(lines_hbm.at[:, b], here, y_send.at[b], y_recv.at[b], {"y": far_y}))
+        if b in ACROSS:
+            there, device = place_of(b, y, far_x), {"y": far_y}
+        else:
+            there, device = place_of(b, far_y, x), {"x": far_x}
+        onward.append(remote(there, there, on_send.at[b], on_recv.at[b], device))
+        own.append(pltpu.make_async_copy(lines_hbm.at[:, b], here, own_sem.at[b]))
+
+    def send(blocks):
+        for b in blocks:
+            to_x[b].start()
+            to_y[b].start()
+            own[b].start()
+
+    def hand_on(blocks):
+        for b in blocks:
+            (to_x if b in ACROSS else to_y)[b].wait_recv()
+            onward[b].start()
+
+    def arrive(blocks):
+        for b in blocks:
+            own[b].wait()
+            (to_y if b in ACROSS else to_x)[b].wait_recv()
+            onward[b].wait_recv()
+
+    send(range(6))
+    loads = [
+        pltpu.make_async_copy(source, entry.at[k], load_sem.at[k])
+        for k, source in enumerate((own_hbm, other_hbm))
+    ]
+    for load in loads:
+        load.start()
+    hand_on(range(6))
+    send(range(6, count))
+    for load in loads:
+        load.wait()
+    arrive(range(6))
+    copies = [pltpu.make_async_copy(arrays[0], outs[0], out_sem.at[0])]
+    copies[0].start()
+    for k in range(2):
+        weights = arrays[0][...].reshape(D, 3 * HALF)
+        qkv_ref[k * frames : (k + 1) * frames, :] = dot(entry[k], weights).astype(BF16)
+    pairs = HALF // PAIR
+
+    @pl.loop(0, 2 * pairs)
+    def _(step):
+        clip, j = step // pairs, step % pairs
+        rows = pl.ds(pl.multiple_of(clip * frames, frames), frames)
+        lanes = [pl.ds(pl.multiple_of(k * HALF + j * PAIR, PAIR), PAIR) for k in range(3)]
+        query, key, value = (qkv_ref[rows, lane] for lane in lanes)
+        mixture_ref[rows, lanes[0]] = attend_heads(valid_ref[clip], query, key, value)
+
+    hand_on(range(6, count))
+    arrive(range(6, count))
+    for k in range(1, 5):
+        copies.append(pltpu.make_async_copy(arrays[k], outs[k], out_sem.at[k]))
+        copies[k].start()
+    for copy in copies:
+        copy.wait()
+    for b in range(count):
+        to_x[b].wait_send()
+        to_y[b].wait_send()
+        onward[b].wait_send()
+
+
+def gather_group(valid, own, other, lines):
+    na, count, rows, _ = lines.shape
+    frames = own.shape[0]
+    tall = lambda cols: (2, 2, na, 2, rows, cols)
+    wide = (2, na, 2, rows, D)
+    shapes = [tall(3 * HALF), wide, tall(HALF), tall(HALF), wide]
+    sem = lambda size: pltpu.SemaphoreType.DMA((size,))
+    return pl.pallas_call(
+        gather_kernel,
+        out_shape=[
+            jax.ShapeDtypeStruct((2 * frames, HALF), BF16),
+            jax.ShapeDtypeStruct((2 * frames, 3 * HALF), BF16),
+        ]
+        + [jax.ShapeDtypeStruct(shape, BF16) for shape in shapes],
+        in_specs=[SCALARS] + [ANY] * 3,
+        out_specs=[WHOLE] * 2 + [ANY] * 5,
+        scratch_shapes=[pltpu.VMEM(shape, BF16) for shape in shapes]
+        + [pltpu.VMEM((2, frames, D), BF16)]
+        + [sem(count)] * 7
+        + [sem(2), sem(5)],
+        compiler_params=pltpu.CompilerParams(
+            vmem_limit_bytes=56 * 2**20, collective_id=4, has_side_effects=True
+        ),
+        cost_estimate=LIGHT,
+    )(valid, own, other, lines)
 
 
 def ffn_kernel(
@@ -685,19 +829,24 @@
     for copy in in_hops[2]:
         copy.wait_recv()
     width = in_own.shape[-1] // 2
+    share = width // na
     for at_y in range(2):
         for at_c in range(2):
             if at_y:
                 near = in_y[at_c, x]
             else:
                 near = in_core[y, x] if at_c else in_own[y, c, x]
-            for at_x, piece in ((0, near), (1, in_x[at_y * 2 + at_c])):
-                rank = (
-                    lax.rem(y + at_y, 2) * 2 + lax.rem(c + at_c, 2)
-                ) * 2 + lax.rem(x + at_x, 2)
-                for half in range(2):
-                    start = pl.multiple_of(half * FF + rank * width, 128)
-                    in_ref[:, pl.ds(start, width)] = piece[:, half * width : (half + 1) * width]
+            across = in_x[at_y * 2 + at_c]
+            low = jnp.where(x == 0, near, across)
+            high = jnp.where(x == 0, across, near)
+            rank = lax.rem(y + at_y, 2) * 2 + lax.rem(c + at_c, 2)
+            for half in range(2):
+                for k in range(na):
+                    at = half * width + k * share
+                    start = pl.multiple_of(half * FF + (rank * na + k) * 2 * share, 128)
+                    in_ref[:, pl.ds(start, 2 * share)] = jnp.concatenate(
+                        [low[:, at : at + share], high[:, at : at + share]], axis=1
+                    )
     depth = down_ref.shape[0]
     sums = None
     for k in range(na):
@@ -859,6 +1008,64 @@
     )(*parts, weight)
 
 
+def notes_kernel(own_ref, out_ref, notes, send, recv):
+    y, c, z, x = (lax.axis_index(axis) for axis in AXES)
+    na = notes.shape[2]
+    far_y, far_c, far_x = {"y": 1 - y}, {"c": 1 - c}, {"x": 1 - x}
+    lines = [{"z": lax.rem(z + k, na)} for k in range(1, na)]
+    barrier = pltpu.get_barrier_semaphore()
+    for device in [far_y, far_c, far_x] + lines:
+        pl.semaphore_signal(
+            barrier, inc=1, device_id=device, device_id_type=pl.DeviceIdType.MESH
+        )
+    pl.semaphore_wait(barrier, 3 + len(lines))
+    notes[0, 0, 0, 0] = own_ref[...]
+    hops = [
+        [(notes.at[0, 0, 0, 0], notes.at[0, 0, 0, 1], far_x)],
+        [(notes.at[0, 0, 0], notes.at[0, 0, k + 1], line) for k, line in enumerate(lines)],
+        [(notes.at[0, 0], notes.at[0, 1], far_c)],
+        [(notes.at[0], notes.at[1], far_y)],
+    ]
+    at = 0
+    copies = []
+    for hop in hops:
+        group = []
+        for source, target, device in hop:
+            group.append(
+                pltpu.make_async_remote_copy(
+                    src_ref=source,
+                    dst_ref=target,
+                    send_sem=send.at[at],
+                    recv_sem=recv.at[at],
+                    device_id=device,
+                    device_id_type=pl.DeviceIdType.MESH,
+                )
+            )
+            at += 1
+        for copy in group:
+            copy.start()
+        for copy in group:
+            copy.wait_recv()
+        copies += group
+    for copy in copies:
+        copy.wait_send()
+    out_ref[...] = notes[...]
+
+
+def gather_notes(notes, na):
+    all_notes = (2, 2, na, 2) + notes.shape
+    sem = pltpu.SemaphoreType.DMA((na + 2,))
+    return pl.pallas_call(
+        notes_kernel,
+        out_shape=jax.ShapeDtypeStruct(all_notes, BF16),
+        in_specs=[WHOLE],
+        out_specs=WHOLE,
+        scratch_shapes=[pltpu.VMEM(all_notes, BF16), sem, sem],
+        compiler_params=pltpu.CompilerParams(collective_id=5, has_side_effects=True),
+        cost_estimate=LIGHT,
+    )(notes)
+
+
 def shift_kernel(
     terms_ref, cot_hbm, in_ref, shifts_ref, cots_hbm, parts_ref,
     from_core, line_out, line_in, y_out, y_in, x_out, x_in,
@@ -1048,20 +1255,23 @@
 
 
 def ffn_group_kernel(
-    entry_hbm, notes_hbm, cot_hbm, cots_hbm, in_hbm, down_hbm,
+    entry_hbm, notes_hbm, cot_hbm, cots_hbm, lines_hbm, down_hbm,
     d_entry_hbm, grad_down_hbm, grad_in_hbm, branch_hbm, own_hbm, other_hbm, pair_hbm, back_hbm,
     sum_hbm, branch_back_hbm,
-    entry, d_branch, hidden, d_gate_up, in_ref, down_ref, partial, away, branch, loaded, sums,
+    entry, d_branch, hidden, d_gate_up, in_lines, down_lines, partial, away, branch, loaded, sums,
     local_sem, entry_send, entry_recv, cot_sem,
     pair_send, pair_recv, back_send, back_recv, branch_sem, out_sem,
     relay_send, relay_recv, branch_pair_send, branch_pair_recv, branch_send, branch_recv,
-    *, chips, sizes,
+    *, chips, peers, sizes,
 ):
     ny, nb = sizes
     y, c, x = lax.axis_index("y"), lax.axis_index("c"), lax.axis_index("x")
     frames = cot_hbm.shape[0]
     rows = frames // 2
-    width = down_ref.shape[0]
+    own_rows = in_lines.shape[-2]
+    width = down_lines.shape[0] * down_lines.shape[1]
+    in_all = lambda: in_lines[...].reshape(D, 2 * width)
+    down_all = lambda: down_lines[...].reshape(width, D)
     count = len(chips)
     sibling = {"c": 1 - c}
     ahead = [{"y": lax.rem(y + dy, ny), "x": lax.rem(x + dx, nb)} for dy, dx in chips]
@@ -1092,11 +1302,16 @@
             [
                 (entry_hbm, entry.at[0, pl.ds(0, frames)]),
                 (notes_hbm, entry.at[0, pl.ds(frames, NOTE_ROWS)]),
-                (in_hbm, in_ref),
-                (down_hbm, down_ref),
+                (down_hbm, down_lines),
             ]
         )
     ]
+    for k, (dy, dc, dx) in enumerate(peers):
+        target = in_lines.at[
+            lax.rem(y + dy, ny), lax.rem(c + dc, 2), :, lax.rem(x + dx, nb)
+        ]
+        source = lines_hbm.at[:, pl.ds(k * own_rows, own_rows)]
+        loads.append(pltpu.make_async_copy(source, target, local_sem.at[3 + k]))
     for load in loads:
         load.start()
     cot_loads = [
@@ -1157,9 +1372,12 @@
             behind[k],
         )
 
+    order = (0, 3, 1, 2)
+    turn = {k: order.index(k) % 2 for k in order}
+
     def pair_copy(k):
         return remote(
-            away.at[k % 2], pair_hbm.at[k], pair_send.at[k], pair_recv.at[k], sibling
+            away.at[turn[k]], pair_hbm.at[k], pair_send.at[k], pair_recv.at[k], sibling
         )
 
     def back_copy(k):
@@ -1176,22 +1394,22 @@
             gate_row = notes[0:1] + notes[1:2] + notes[2:3]
             d_here = (d_branch[slot, here, :].astype(F32) * gate_row).astype(BF16)
             d_branch[slot, here, :] = d_here
-            gate_up = dot(entry[slot, here, :], in_ref[...])
+            gate_up = dot(entry[slot, here, :], in_all())
             gate, up = gate_up[:, :width], gate_up[:, width:]
             logistic = jax.nn.sigmoid(gate)
             hidden_here = (gate * logistic * up).astype(BF16)
             hidden[slot, here, :] = hidden_here
-            d_hidden = dot_back(d_here, down_ref[...])
+            d_hidden = dot_back(d_here, down_all())
             d_gate = d_hidden * up * logistic * (1.0 + gate * (1.0 - logistic))
             d_gate_up[slot, here, :width] = d_gate.astype(BF16)
             d_gate_up[slot, here, width:] = (d_hidden * gate * logistic).astype(BF16)
-            d_entry = dot_back(d_gate_up[slot, here, :], in_ref[...]).astype(BF16)
-            branch[i, here, :] = dot(hidden_here, down_ref[...]).astype(BF16)
+            d_entry = dot_back(d_gate_up[slot, here, :], in_all()).astype(BF16)
+            branch[i, here, :] = dot(hidden_here, down_all()).astype(BF16)
 
             if i == 0:
                 partial[k, here, :] = d_entry
             else:
-                away[k % 2, here, :] = d_entry
+                away[turn[k], here, :] = d_entry
 
     def move(source, target):
         copy = pltpu.make_async_copy(source, target, out_sem.at[0])
@@ -1213,34 +1431,34 @@
         if k:
             back_copy(k).start()
             pair_copy(k).wait_send()
-            away[k % 2] = branch_terms(k).astype(BF16)
-            move(away.at[k % 2], sum_hbm.at[k - 1])
+            away[turn[k]] = branch_terms(k).astype(BF16)
+            move(away.at[turn[k]], sum_hbm.at[k - 1])
             branch_copy(k).start()
         else:
             pair_copy(k).wait_send()
 
-    for k in range(count):
+    before = None
+    for k in order:
         if k == 0:
             for load in loads[2:]:
                 load.wait()
-        elif k < 3:
-            if k == 1:
-                entry_copies[2].wait_recv()
-                entry_copies[4].wait_recv()
-                for copy in relays:
-                    copy.start()
-            entry_copies[2 * k + 1].start()
-        else:
+        elif k == 3:
+            entry_copies[2].wait_recv()
+            entry_copies[4].wait_recv()
+            for copy in relays:
+                copy.start()
+            for near in (3, 5):
+                entry_copies[near].start()
             for copy in relays:
                 copy.wait_recv()
-            entry_copies[2 * k + 1].start()
+            entry_copies[7].start()
         entry_copies[2 * k + 1].wait_recv()
         cot_loads[2 * k].wait()
         cot_loads[2 * k + 1].wait()
-        if k:
-            branch_wait(k - 1)
+        if before is not None:
+            branch_wait(before)
         compute(k, 0)
-        if k == 1:
+        if before == 0:
             finish(0)
         compute(k, 1)
         pair_copy(k).start()
@@ -1248,7 +1466,8 @@
             copy.start()
         if k:
             finish(k)
-    branch_wait(count - 1)
+        before = k
+    branch_wait(before)
 
     down_rows = 256 if width % 256 == 0 else 128
 
@@ -1306,15 +1525,18 @@
         branch_copy(k).wait_send()
 
 
-def ffn_group(entry, notes, cotangent, cotangents, rank_in, rank_down, chips, sizes, na, lanes):
+def ffn_group(entry, notes, cotangent, cotangents, lines, down, chips, peers, sizes):
     frames = cotangent.shape[0]
-    width = rank_down.shape[0]
+    na, depth = down.shape[:2]
+    width = na * depth
+    rows = lines.shape[1] // len(peers)
+    lanes = sizes[1] * rows
     count = len(chips)
     low = lambda *shape: jax.ShapeDtypeStruct(shape, BF16)
     sem = lambda size: pltpu.SemaphoreType.DMA((size,))
     clip = (frames, D)
     return pl.pallas_call(
-        functools.partial(ffn_group_kernel, chips=chips, sizes=sizes),
+        functools.partial(ffn_group_kernel, chips=chips, peers=peers, sizes=sizes),
         out_shape=[
             jax.ShapeDtypeStruct(clip, F32),
             low(width, D),
@@ -1334,14 +1556,14 @@
             pltpu.VMEM((2 * count, frames, D), BF16),
             pltpu.VMEM((2 * count, frames, width), BF16),
             pltpu.VMEM((2 * count, frames, 2 * width), BF16),
-            pltpu.VMEM((D, 2 * width), BF16),
-            pltpu.VMEM((width, D), BF16),
+            pltpu.VMEM((sizes[0], 2, na, sizes[1], rows, 2 * width), BF16),
+            pltpu.VMEM((na, depth, D), BF16),
             pltpu.VMEM((count, frames, D), BF16),
             pltpu.VMEM((2, frames, D), BF16),
             pltpu.VMEM((2, frames, D), BF16),
             pltpu.VMEM(clip, BF16),
             pltpu.VMEM(clip, F32),
-            sem(4),
+            sem(3 + len(peers)),
             sem(2 * count),
             sem(2 * count),
             sem(2 * count),
@@ -1362,7 +1584,7 @@
             vmem_limit_bytes=60 * 2**20, collective_id=0, has_side_effects=True
         ),
         cost_estimate=LIGHT,
-    )(entry, notes, cotangent, cotangents, rank_in, rank_down)
+    )(entry, notes, cotangent, cotangents, lines, down)
 
 
 def stack_kernel(*refs):
@@ -1610,7 +1832,7 @@
             bit *= 2
         return array
 
-    def spread(self, lines, turn):
+    def spread(self, lines, turn, between):
         held, marks = {(0, 0): lines}, []
         for axis in ("x", "y") if turn else ("y", "x"):
             for (y, x), piece in list(held.items()):
@@ -1618,20 +1840,23 @@
                     step = dict(y=y, x=x)
                     step[axis] = k
                     held[(step["y"], step["x"])] = self.move(piece, **{axis: k})
-            marks = marks or list(held.values())[1:]
+            if not marks:
+                marks = list(held.values())[1:]
+                if between:
+                    held.update(zip(list(held)[1:], after(marks, between)))
         return held, marks
 
-    def gather_weights(self, parts, shapes, mine, spot, first):
+    def gather_weights(self, parts, shapes, mine, spot, first, between=(), behind=()):
         rows = parts[0][0][0].shape[0]
         mixed = jnp.stack([shard for part in parts for shard, *_ in part])
         lines = lax.all_gather(mixed, "z")
         if first:
             (lines,) = after([lines], first)
         start = 0
-        held, marks, plan = [], [], dict(parts=[])
+        held, marks, plan = [], [], dict(parts=[], outs=len(shapes))
         for turn, part in enumerate(parts):
             end = start + len(part)
-            pieces, arrived = self.spread(lines[:, start:end], turn)
+            pieces, arrived = self.spread(lines[:, start:end], turn, between)
             held.append(pieces)
             marks += arrived
             start = end
@@ -1641,6 +1866,7 @@
         plan["offsets"] = sorted(held[0])
         if rows % 16 == 0:
             arrays = [pieces[offset] for pieces in held for offset in plan["offsets"]]
+            arrays += behind
             copies = len(plan["offsets"]) * sum(len(part) for part in parts)
             kernel = functools.partial(place_pieces, plan=plan, sizes=(self.ny, self.nb))
             return place(kernel, spot, arrays, shapes, copies), marks
@@ -1803,8 +2029,9 @@
     keep_rows = (jnp.arange(frames) < valid).astype(F32)[:, None]
 
     width = FF // ranks
-    if rows % 16 == 0 and D // (2 * grid.ny) % 128 == 0:
-        prepare = functools.partial(prepare_kernel, offsets=grid.peers, sizes=(grid.ny, grid.nb))
+    grouped = rows % 16 == 0 and grid.ny == 2 and grid.nb == 2
+    if grouped:
+        prepare = functools.partial(prepare_kernel, offsets=grid.peers, sizes=(grid.ny, grid.na, grid.nb))
         five = (5, rows, HALF)
         five_own, five_other, wide_low, in_blocks = pl.pallas_call(
             prepare,
@@ -1839,8 +2066,12 @@
     five_high = jnp.where(core == 0, five_other, five_own)
     lifted = jax.nn.silu(timestep[0].astype(F32)).astype(BF16)
     notes = jnp.concatenate([lifted, norm_gains.astype(BF16).reshape(-1)])
-    (notes,) = after([notes], (five_other,))
-    notes = grid.gather_small(notes)
+    if grouped:
+        size = notes.shape[0]
+        notes = jnp.pad(notes, (0, -size % 2048)).reshape(-1, 128)
+        notes = gather_notes(notes, grid.na).reshape(count, -1)[:, :size]
+    else:
+        notes = grid.gather_small(notes)
     origin = []
     for spot_of in grid.spots:
         source = [
@@ -1853,7 +2084,12 @@
     gain_rows = gain_rows.reshape(count, 3, rows).transpose(1, 0, 2).reshape(3, D)
     lifted_own = lax.dynamic_slice(notes, (0, device * rows), (count, rows))
     shift_terms = dot(lifted_own, mod_matrix.astype(BF16))
-    grouped = rows % 16 == 0 and grid.ny == 2 and grid.nb == 2
+    text = jnp.concatenate([context[0], grid.swap(context[0])])
+    blank = jnp.zeros((2 * words, count, rows // 2), BF16)
+    text_cut = text.reshape(2 * words, count, rows // 2)
+    text_key = jnp.concatenate([text_cut, blank], axis=-1).reshape(2 * words, -1)
+    text_value = jnp.concatenate([blank, text_cut], axis=-1).reshape(2 * words, -1)
+    text_both = jnp.concatenate([text_key, text_value])
     cotangent_own = (cotangent[0].astype(F32) * keep_rows).astype(BF16)
     if grouped:
         shift_terms = shift_terms.reshape(grid.ny, 2, grid.na, grid.nb, 6 * D // 128, 128)
@@ -1872,38 +2108,46 @@
         (wide_low[2 * k], out, None, 0),
         (wide_low[2 * k + 1], out, None, HALF),
     ]
-    first = both(0, 0, 0) + both(1, 0, HALF) + both(2, 0, 2 * HALF)
-    (down_low,) = after([ff_down.astype(BF16)], (shifts,))
-    down_part = grid.to_rank(down_low)
-    (matrix_qkv,), marks = grid.gather_weights(
-        [first[:3], first[3:]], [tall + (3 * HALF,)], mine, spot, (shifts,)
-    )
-    (down_part,) = after([down_part], (*marks, matrix_qkv))
-    matrix_qkv = matrix_qkv.reshape(D, 3 * HALF)
-    (matrix_out, matrix_query), marks = grid.gather_weights(
-        [sides(0, 0), both(3, 1, 0)], [wide, tall + (HALF,)], mine, spot, marks
-    )
-    (matrix_ctx, matrix_cross), marks = grid.gather_weights(
-        [both(4, 0, 0), sides(1, 1)], [tall + (HALF,), wide], mine, spot, marks
-    )
-    matrix_out, matrix_cross = matrix_out.reshape(HALF, D), matrix_cross.reshape(HALF, D)
-    matrix_query, matrix_ctx = matrix_query.reshape(D, HALF), matrix_ctx.reshape(D, HALF)
-
-    rank_in, rank_down = grid.gather_ranks(in_parts, down_part, mine, spot)
-
-    pair_lengths = jnp.concatenate([lengths, grid.swap(lengths)])
-    all_words = jnp.full((2,), words, jnp.int32)
-    text = jnp.concatenate([context[0], grid.swap(context[0])])
     stream = latents[0].astype(F32)
     normed_one, inverse_one = norm_rows(stream)
     entry_attn = (normed_one * gain_rows[0] * (1.0 + shifts[1]) + shifts[0]).astype(BF16)
+    entry_pair = [entry_attn, grid.swap(entry_attn)]
+    pair_lengths = jnp.concatenate([lengths, grid.swap(lengths)])
+    columns = HALF // PAIR
+    if grouped:
+        blocks = [(five_low, five_high)[lane][k] for k in range(3) for lane in range(2)]
+        blocks += [wide_low[0], wide_low[1], five_low[3], five_high[3]]
+        blocks += [five_low[4], five_high[4], wide_low[2], wide_low[3]]
+        lines = lax.all_gather(jnp.stack(blocks), "z")
+        in_lines = lax.all_gather(in_parts.reshape(-1, D), "z")
+        down_lines = lax.all_gather(ff_down.astype(BF16), "z")
+        mixture_attn, qkv, matrix_qkv, matrix_out, matrix_query, matrix_ctx, matrix_cross = (
+            gather_group(pair_lengths, *entry_pair, lines)
+        )
+        matrix_qkv = matrix_qkv.reshape(D, 3 * HALF)
+    else:
+        first = both(0, 0, 0) + both(1, 0, HALF) + both(2, 0, 2 * HALF)
+        (matrix_qkv,), _ = grid.gather_weights(
+            [first[:3], first[3:]], [tall + (3 * HALF,)], mine, spot, ()
+        )
+        matrix_qkv = matrix_qkv.reshape(D, 3 * HALF)
+        (matrix_out, matrix_query), _ = grid.gather_weights(
+            [sides(0, 0), both(3, 1, 0)], [wide, tall + (HALF,)], mine, spot, ()
+        )
+        (matrix_ctx, matrix_cross), _ = grid.gather_weights(
+            [both(4, 0, 0), sides(1, 1)], [tall + (HALF,), wide], mine, spot, ()
+        )
+        down_part = grid.to_rank(ff_down.astype(BF16))
+        rank_in, rank_down = grid.gather_ranks(in_parts, down_part, mine, spot)
+        qkv = pair_in(*entry_pair, matrix_qkv, dot)
+        mixture_attn = attend(pair_lengths, *((qkv, frames, 0, k * columns) for k in range(3)))
+    matrix_out, matrix_cross = matrix_out.reshape(HALF, D), matrix_cross.reshape(HALF, D)
+    matrix_query, matrix_ctx = matrix_query.reshape(D, HALF), matrix_ctx.reshape(D, HALF)
+
+    all_words = jnp.full((2,), words, jnp.int32)
     d_result = cotangent[0].astype(F32) * keep_rows
 
-    columns = HALF // PAIR
-    entry_pair = [entry_attn, grid.swap(entry_attn)]
-    qkv = pair_in(*entry_pair, matrix_qkv, dot)
     self_parts = tuple((qkv, frames, 0, k * columns) for k in range(3))
-    mixture_attn = attend(pair_lengths, *self_parts)
     own, away = pair_out([mixture_attn], matrix_out, dot)
     branch_attn = own + grid.swap(away).astype(F32)
     after_attn = stream + shifts[2] * branch_attn
@@ -1911,11 +2155,6 @@
     entry_cross = (normed_two * gain_rows[1]).astype(BF16)
     cross_pair = [entry_cross, grid.swap(entry_cross)]
     query_cross = pair_in(*cross_pair, matrix_query, dot)
-    blank = jnp.zeros((2 * words, count, rows // 2), BF16)
-    text_cut = text.reshape(2 * words, count, rows // 2)
-    text_key = jnp.concatenate([text_cut, blank], axis=-1).reshape(2 * words, -1)
-    text_value = jnp.concatenate([blank, text_cut], axis=-1).reshape(2 * words, -1)
-    text_both = jnp.concatenate([text_key, text_value])
     kv_cross = dot(text_both, matrix_ctx).astype(BF16)
     cross_parts = ((query_cross, frames, 0, 0), (kv_cross, words, 0, 0), (kv_cross, words, 2, 0))
     mixture_cross = attend(all_words, *cross_parts)
@@ -1930,8 +2169,8 @@
     chips = grid.chips
     if grouped:
         d_entry_ffn, grad_down, grad_in, branch_ffn, *_ = ffn_group(
-            entry_ffn, notes, cotangent_own, cotangents, rank_in, rank_down,
-            chips, (grid.ny, grid.nb), grid.na, grid.nb * rows,
+            entry_ffn, notes, cotangent_own, cotangents, in_lines, down_lines,
+            chips, grid.peers, (grid.ny, grid.nb),
         )
         grad_in = grad_in.reshape(-1, 2 * width)
     else:
@@ -2064,6 +2303,7 @@
         turn_width = D // (2 * grid.ny)
     else:
         grad_down = lax.psum_scatter(grad_down, "z", tiled=True)
+        grad_down = grid.to_rank(grad_down, back=True)
         grad_in = grid.swap_back(grad_in.reshape(grid.ny, 2, grid.nb, rows, 2 * width), mine)
         grad_in = grid.join_columns(grad_in, mine, spot)
         small = grid.gather_small(small[: 9 * D // 128].reshape(9, D))
@@ -2095,8 +2335,6 @@
     grad_mod = jnp.einsum("nd,nkm->kdm", lifted_own, small[:, :6], preferred_element_type=F32)
     gain_sums = jnp.sum(small[:, 6:].astype(F32), axis=0)
     grad_gains = lax.dynamic_slice(gain_sums, (0, device * rows), (3, rows))
-    grad_down = grid.to_rank(grad_down, back=True)
-
     lamb = functools.partial(lamb_terms, spot)
     done = {}
     done["qkv"] = lamb(qkv_matrix, qkv_first, qkv_second, qkv_parts, turn_width)

time: 916 us -> 899 us (0.981)
  Pallas kernels: 615 us -> 740 us
  waiting for transfers between devices: 115 us -> 18.2 us
  starting transfers between devices: 38.4 us -> 2.64 us
  local copies, waits for them, and re-layouts: 63.4 us -> 51.9 us
    pallas_call x11 -> x3, Pallas kernels: 198 us -> 338 us  [the longest x1 179 us: ffn_group(): pl.pallas_call(functools.partial(ffn_group_kernel, chips=chips, peers=pee...]
    ppermute x35 -> x11, waiting for transfers between devices: 115 us -> 18.2 us  [move(): return lax.ppermute(array, names, pairs)]
    ppermute x35 -> x11, starting transfers between devices: 30.4 us -> 2.47 us  [move(): return lax.ppermute(array, names, pairs)]
    pallas_call x2 -> x1, Pallas kernels: 26.3 us -> 11.7 us  [attend(): pl.pallas_call(attend_kernel, out_shape=jax.ShapeDtypeStruct((2 * frames,...]
    pallas_call x4 -> x3, Pallas kernels: 16.2 us -> 6.71 us  [pair_in(): pl.pallas_call(functools.partial(pair_in_kernel, product=product), out_sh...]
    unnamed x243 -> x219, local copies, waits for them, and re-layouts: 41.9 us -> 34.3 us
  transfers between devices with their start and end apart: 42 -> 15, of which waited for: 23 -> 8; matrix products, arithmetic and copies ran while one was open for 8% -> 7% of each run, Pallas kernels for 21% -> 34%
where the time goes in v3:
time: 899 us; the launch traced here: 890 us
  Pallas kernels  740 us (82%)
  other arithmetic  54.4 us (6%)
  local copies, waits for them, and re-layouts  51.9 us (6%)
  waiting for transfers between devices  18.2 us (2%)
  between operations  16.4 us (2%)
    pallas_call x1, Pallas kernels, reduce_group(): pl.pallas_call(functools.partial(reduce_kernel, plan=plan, inputs=len(arr...  207 us
    pallas_call x1, Pallas kernels, ffn_group(): pl.pallas_call(functools.partial(ffn_group_kernel, chips=chips, peers=pee...  179 us
    pallas_call x1, Pallas kernels, gather_group(): pl.pallas_call(gather_kernel, out_shape=[jax.ShapeDtypeStruct((2 * frames...  143 us
    pallas_call x1, Pallas kernels, sum_shifts(): pl.pallas_call(shift_kernel, out_shape=[jax.ShapeDtypeStruct((rows, 128),...  63.9 us
    unnamed x219, local copies, waits for them, and re-layouts  34.3 us
    pallas_call x2, Pallas kernels, attend_back(): pl.pallas_call(attend_back_kernel, out_shape=[jax.ShapeDtypeStruct((2 * r...  30.9 us
    pallas_call x6, Pallas kernels, lamb_terms(): pl.pallas_call(lamb_kernel, out_shape=[full, full, full, jax.ShapeDtypeSt...  26.1 us
    pallas_call x4, Pallas kernels, pair_out(): pl.pallas_call(functools.partial(pair_out_kernel, product=product), out_s...  25.6 us
  transfers between devices with their start and end apart: 15, of which 8 were waited for; matrix products, arithmetic and copies ran while one was open for 7% of the time, Pallas kernels for 34%

profile of v3, /device:TPU:0, one launch (start us, length us, event | category | flops | bytes accessed | tf_op | source)
XLA Modules:
  0.0 889.7 jit_solution(8148267843024381964)
XLA Ops:
  12.3 2.9 shard_map.450
  28.3 15.8 %shard_map.449 = bf16[2,2,4,2,16,128]{5,4,3,2,1,0:T(8,128)(2,1)} custom-call(bf16[16,128]{1,0:T(8,128)(2,1)} %fusion.42.own_ref), custom_call_target="tpu_custom_call" | custom-call | flops 1048576 | bytes 1048576 | tf_op jit(solution)/shard_map/pallas_call | solution.py:1058
  48.9 63.9 %shard_map.451 = (f32[72,128]{1,0:T(8,128)S(1)}, bf16[8,384,1536]{2,1,0:T(8,128)(2,1)S(1)}, bf16[2,2,2,48,1536]{4,3,2,1,0:T(8,128)(2,1)}) custom-call(f32[2,2,4,2,72,128]{5,4,3,2,1,0:T(8,128)S(1)} %bitcast.248, bf16[384,1536]{1,0:T(8,128)(2,1)S(1)} %fusion.23.cot_hbm, bf16[2,2,2,48,1536]{4,3,2,1,0:T(8,128)(2,1)S(1)} %bitcast.257), custom_call_target="tpu_custom_call" | custom-call | flops 1048576 | bytes 1048576 | tf_op jit(solution)/shard_map/pallas_call | solution.py:1214
  112.8 3.6 copy-done.17
  124.1 143.4 %shard_map.452 = (bf16[768,768]{1,0:T(8,128)(2,1)}, bf16[768,2304]{1,0:T(8,128)(2,1)}, bf16[2,2,4,2,48,2304]{5,4,3,2,1,0:T(8,128)(2,1)}, bf16[2,4,2,48,1536]{4,3...) custom-call(s32[2]{0:T(128)} %pad_add_fusion.1.valid_ref, ...), custom_call_target="tpu_custom_call" | custom-call | flops 1048576 | bytes 1048576 | tf_op jit(solution)/shard_map/pallas_call | solution.py:406
  268.8 4.1 shard_map.453
  287.1 3.7 convolution_convert_fusion.key_ref.value_ref
  293.1 11.7 %shard_map.455.refs_0_ = bf16[768,768]{1,0:T(8,128)(2,1)S(1)} custom-call(s32[2]{0:T(128)S(1)} %broadcast_10_valid_ref.2.valid_ref, bf16[768,768]{1,0:T(8,128)(2,1)S(1)} %shard_map.454.query_ref, bf16[512,768]{1,0:T(8,128)(2,1)S(1)} %convolution_convert_fusion.key_ref.value_ref, bf16[512,768]{1,0:T(8,128)(2,1)S(1)} %convolution_convert_fusion.key_ref.value_ref), custom_call_target="tpu_custom_call" | custom-call | flops 1048576 | bytes 1048576 | tf_op jit(solution)/shard_map/pallas_call | solution.py:143
  305.9 4.5 shard_map.456
  314.7 3.1 fusion.51
  320.8 179.0 %shard_map.457 = (f32[384,1536]{1,0:T(8,128)}, bf16[768,1536]{1,0:T(8,128)(2,1)}, bf16[4,4,96,1536]{3,2,1,0:T(8,128)(2,1)}, f32[384,1536]{1,0:T(8,128)}, bf16[38...) custom-call(bf16[384,1536]{1,0:T(8,128)(2,1)} %add_convert_fusion.en, ...), custom_call_target="tpu_custom_call" | custom-call | flops 1048576 | bytes 1048576 | tf_op jit(solution)/shard_map/pallas_call | solution.py:1538
  501.6 6.9 fusion.17
  509.8 2.8 collective-permute-done.7.other_ref.refs_2_
  514.9 11.4 %shard_map.459 = (bf16[768,768]{1,0:T(8,128)(2,1)S(1)}, bf16[256,768]{1,0:T(8,128)(2,1)S(1)}, bf16[256,768]{1,0:T(8,128)(2,1)S(1)}) custom-call(s32[2]{0:T(128)S(1)} %broadcast_10_valid_ref.2.valid_ref, bf16[768,768]{1,0:T(8,128)(2,1)S(1)} %copy-done.11, bf16[512,768]{1,0:T(8,128)(2,1)S(1)} %convolution_convert_fusion.key_ref.value_ref, ...), custom_call_target="tpu_custom_call" | custom-call | flops 1048576 | bytes 1048576 | tf_op jit(solution)/shard_map/pallas_call | solution.py:157
  526.4 4.9 shard_map.460
  531.4 2.7 collective-permute-done.8
  535.8 4.0 fusion.18
  540.2 2.7 collective-permute-done.9.other_ref.refs_11_
  545.3 19.5 %shard_map.462 = (bf16[768,768]{1,0:T(8,128)(2,1)S(1)}, bf16[768,768]{1,0:T(8,128)(2,1)S(1)}, bf16[768,768]{1,0:T(8,128)(2,1)S(1)}) custom-call(s32[2]{0:T(128)S(1)} %copy-done.59, bf16[768,2304]{1,0:T(8,128)(2,1)} %get-tuple-element.114.query_ref.key_ref.value_ref, bf16[768,2304]{1,0:T(8,128)(2,1)} %get-tuple-element.114.query_ref.key_ref.value_ref, ...), custom_call_target="tpu_custom_call" | custom-call | flops 1048576 | bytes 1048576 | tf_op jit(solution)/shard_map/pallas_call | solution.py:157
  564.8 12.2 %shard_map.463 = (f32[384,1536]{1,0:T(8,128)}, bf16[384,1536]{1,0:T(8,128)(2,1)}) custom-call(bf16[768,768]{1,0:T(8,128)(2,1)S(1)} %get-tuple-element.115.refs_0_.refs_14_, bf16[768,768]{1,0:T(8,128)(2,1)S(1)} %get-tuple-element.116.refs_1_.refs_15_, bf16[768,768]{1,0:T(8,128)(2,1)S(1)} %get-tuple-element.117.refs_2_.refs_16_, bf16[1536,2304]{1,0:T(8,128)(2,1)} %bitcast.268), custom_call_target="tpu_custom_call" | custom-call | flops 1048576 | bytes 1048576 | tf_op jit(solution)/shard_map/pallas_call | solution.py:996
  579.9 3.3 maximum_bitcast_fusion.4
  585.7 5.3 multiply_reduce_fusion.2
  593.9 3.6 fusion.29
  597.5 206.8 %shard_map.465 = (bf16[7,2,48,768]{3,2,1,0:T(8,128)(2,1)}, bf16[2,2,4,2,112,128]{5,4,3,2,1,0:T(8,128)(2,1)}, bf16[48,12288]{1,0:T(8,128)(2,1)}, bf16[192,1536]{1,0:T(8,128)(2,1)}, bf16[3,192,1536]{2,1,0:T(8,128)(2,1)}) custom-call(bf16[768,768]{1,0:T(8,128)(2,1)} %copy-done.5, bf16[384,1536]{1,0:T(8,128)(2,1)} %copy-done.4, bf16[384,1536]{1,0:T(8,128)(2,1)} %copy-done.28, ...), custom_call_target="tpu_custom_call" | custom-call | flops 1048576 | bytes 1048576 | tf_op jit(solution)/shard_map/pallas_call | solution.py:894
  807.2 2.8 reshape.525
  821.7 5.4 shard_map.467
  828.0 3.6 shard_map.468
  831.7 3.9 shard_map.471
  835.8 4.6 shard_map.466
  841.8 6.9 shard_map.470
  853.5 17.8 %shard_map.472 = f32[16,128]{1,0:T(8,128)} custom-call(f32[16,128]{1,0:T(8,128)} %pad.12.sums_ref), custom_call_target="tpu_custom_call" | custom-call | flops 1048576 | bytes 1048576 | tf_op jit(solution)/shard_map/pallas_call | solution.py:1657
  874.3 8.4 shard_map.473
  (343 shorter events, 98.1 us)
Async XLA Ops:
  7.2 115.8 %all-gather.8.cloned.1.call-start = ((), (), s32[]{:S(2)}) async-start(), calls=%async_computation.3 | async-start | bytes 5160960 | tf_op jit(solution)/shard_map/all_gather | solution.py:2121
  16.2 9.6 %copy-start.7 = (f32[192,1536]{1,0:T(8,128)S(1)}, f32[192,1536]{1,0:T(8,128)}, u32[]{:S(2)}) copy-start(f32[192,1536]{1,0:T(8,128)} %refs_5_.1) | copy-start | bytes 3538948
  16.2 1.8 collective-permute-start.2
  25.8 21.2 %copy-start.2 = (f32[48,9216]{1,0:T(8,128)S(1)}, f32[48,9216]{1,0:T(8,128)}, u32[]{:S(2)}) copy-start(f32[48,9216]{1,0:T(8,128)} %refs_0_.1) | copy-start | bytes 5308420
  25.8 295.0 %all-gather.10.cloned.1.call-start = ((), (), s32[]{:S(2)}) async-start(), calls=%async_computation.4 | async-start | bytes 2949120 | tf_op jit(solution)/shard_map/all_gather | solution.py:2123
  26.8 294.1 %all-gather.6.cloned.1.call-start = ((), (), s32[]{:S(2)}) async-start(), calls=%async_computation.1 | async-start | bytes 5898240 | tf_op jit(solution)/shard_map/all_gather | solution.py:2122
  47.0 70.8 %copy-start.79 = (f32[1536]{0:T(1024)}, f32[1536]{0:T(1024)S(1)}, u32[]{:S(2)}) copy-start(f32[1536]{0:T(1024)S(1)} %mul.251) | copy-start | bytes 18436
  48.6 68.1 %copy-start.12 = (bf16[384,1536]{1,0:T(8,128)(2,1)}, bf16[384,1536]{1,0:T(8,128)(2,1)S(1)}, u32[]{:S(2)}) copy-start(bf16[384,1536]{1,0:T(8,128)(2,1)S(1)} %fusion.23.cot_hbm) | copy-start | bytes 3538948
  48.6 67.9 %copy-start.64 = (bf16[1,384,1536]{2,1,0:T(8,128)(2,1)S(1)}, bf16[1,384,1536]{2,1,0:T(8,128)(2,1)}, u32[]{:S(2)}) copy-start(bf16[1,384,1536]{2,1,0:T(8,128)(2,1)} %param.26) | copy-start | bytes 3538948
  119.0 4.0 collective-permute-start.1
  119.1 478.4 %reduce-scatter.2.cloned.1.call-start = ((), (), s32[]{:S(2)}) async-start(), calls=%async_computation.2 | async-start | bytes 5898240 | tf_op jit(solution)/shard_map/reduce_scatter | solution.py:2225
  119.2 2.7 collective-permute-start
  272.8 3.0 collective-permute-start.3
  278.5 255.6 %copy-start.90 = (f32[384]{0:T(512)}, f32[384]{0:T(512)S(1)}, u32[]{:S(2)}) copy-start(f32[384]{0:T(512)S(1)} %add_rsqrt_fusion.1) | copy-start | bytes 4612
  279.5 11.3 %copy-start.9 = (bf16[384,1536]{1,0:T(8,128)(2,1)}, bf16[384,1536]{1,0:T(8,128)(2,1)S(1)}, u32[]{:S(2)}) copy-start(bf16[384,1536]{1,0:T(8,128)(2,1)S(1)} %multiply_convert_fusion.1.own_ref.refs_3_) | copy-start | bytes 3538948
  279.5 11.3 %collective-permute-start.4 = (bf16[384,1536]{1,0:T(8,128)(2,1)S(1)}, bf16[384,1536]{1,0:T(8,128)(2,1)S(1)}, u32[]{:S(2)}, u32[]{:S(2)}) collective-permute-start(bf16[384,1536]{1,0:T(8,128)(2,1)S(1)} %multiply_convert_fusion.1.own_ref.refs_3_), channel_id=1, source_target_pairs={{0,8},{8,0},{1,9},{9,1},{2,10},{10,2},{3,11},{11,3},{4,12},{12,4},... | collective-permute-start | bytes 3538952 | tf_op jit(solution)/shard_map/ppermute | solution.py:1795
  279.8 2.8 collective-permute-start.5
  305.8 12.0 %copy-start.5 = (bf16[768,768]{1,0:T(8,128)(2,1)}, bf16[768,768]{1,0:T(8,128)(2,1)S(1)}, u32[]{:S(2)}) copy-start(bf16[768,768]{1,0:T(8,128)(2,1)S(1)} %shard_map.455.refs_0_) | copy-start | bytes 3538948
  311.8 3.0 collective-permute-start.6
  509.7 2.9 collective-permute-start.7
  531.2 2.9 collective-permute-start.8
  540.0 2.9 collective-permute-start.9
  564.7 12.3 %copy-start.30 = (bf16[768,768]{1,0:T(8,128)(2,1)}, bf16[768,768]{1,0:T(8,128)(2,1)S(1)}, u32[]{:S(2)}) copy-start(bf16[768,768]{1,0:T(8,128)(2,1)S(1)} %get-tuple-element.115.refs_0_.refs_14_) | copy-start | bytes 3538948
  564.8 12.2 %copy-start.31 = (bf16[768,768]{1,0:T(8,128)(2,1)}, bf16[768,768]{1,0:T(8,128)(2,1)S(1)}, u32[]{:S(2)}) copy-start(bf16[768,768]{1,0:T(8,128)(2,1)S(1)} %get-tuple-element.116.refs_1_.refs_15_) | copy-start | bytes 3538948
  564.8 12.2 %copy-start.32 = (bf16[768,768]{1,0:T(8,128)(2,1)}, bf16[768,768]{1,0:T(8,128)(2,1)S(1)}, u32[]{:S(2)}) copy-start(bf16[768,768]{1,0:T(8,128)(2,1)S(1)} %get-tuple-element.117.refs_2_.refs_16_) | copy-start | bytes 3538948
  577.0 8.7 collective-permute-start.10
  817.8 9.4 %copy-start.72 = (bf16[48,768]{1,0:T(8,128)(2,1)S(1)}, bf16[48,768]{1,0:T(8,128)(2,1)}, u32[]{:S(2)}) copy-start(bf16[48,768]{1,0:T(8,128)(2,1)} %get-tuple-element.204) | copy-start | bytes 221188
  817.8 10.2 %copy-start.49 = (f32[3,48,1536]{2,1,0:T(8,128)S(1)}, f32[3,48,1536]{2,1,0:T(8,128)}, u32[]{:S(2)}) copy-start(f32[3,48,1536]{2,1,0:T(8,128)} %first_ref.1) | copy-start | bytes 2654212
  817.9 10.2 %copy-start.50 = (f32[3,48,1536]{2,1,0:T(8,128)S(1)}, f32[3,48,1536]{2,1,0:T(8,128)}, u32[]{:S(2)}) copy-start(f32[3,48,1536]{2,1,0:T(8,128)} %second_ref.1) | copy-start | bytes 2654212
  821.7 10.0 %copy-start.45 = (f32[192,1536]{1,0:T(8,128)S(1)}, f32[192,1536]{1,0:T(8,128)}, u32[]{:S(2)}) copy-start(f32[192,1536]{1,0:T(8,128)} %param.48) | copy-start | bytes 3538948
  821.7 20.0 %copy-start.46 = (bf16[48,12288]{1,0:T(8,128)(2,1)S(1)}, bf16[48,12288]{1,0:T(8,128)(2,1)}, u32[]{:S(2)}) copy-start(bf16[48,12288]{1,0:T(8,128)(2,1)} %get-tuple-element.131) | copy-start | bytes 3538948
  841.8 11.1 %copy-start.96 = (f32[4,2]{1,0:T(4,128)S(1)}, f32[4,2]{1,0:T(4,128)}, u32[]{:S(2)}) copy-start(f32[4,2]{1,0:T(4,128)} %pad_bitcast_fusion) | copy-start | bytes 100
  (86 other events, 368.1 us)
Sparse Core Ops, SparseCore 0:
  25.9 94.8 all-gather.7
  123.0 48.8 all-gather.9
  173.4 88.2 all-gather.5
  500.0 85.7 reduce-scatter.1

commit v4 on v3

--- a/solution.py
+++ b/solution.py
@@ -247,7 +247,7 @@
 
 
 def prepare_kernel(
-    spot_ref, qkv_ref, square_ref, ctx_ref, in_ref, own_ref, other_ref, wide_ref, block_ref,
+    spot_ref, qkv_ref, square_ref, ctx_ref, in_ref, own_ref, other_ref, block_ref,
     *, offsets, sizes
 ):
     ny, na, nb = sizes
@@ -272,7 +272,7 @@
     for k, matrix in enumerate((0, 2)):
         for side in range(2):
             values = square_ref[matrix, :, side * HALF : (side + 1) * HALF]
-            wide_ref[2 * k + side] = values.astype(BF16)
+            own_ref[5 + 2 * k + side] = values.astype(BF16)
     width = FF // len(offsets)
     share = width // na
     for k, (dy, dc, dx) in enumerate(offsets):
@@ -287,28 +287,28 @@
                 block_ref[k, :, at : at + share] = values
 
 
-BLOCKS = [(0, lane, k * HALF) for k in range(3) for lane in range(2)]
-BLOCKS += [(1, None, 0), (1, None, HALF), (2, 0, 0), (2, 1, 0)]
-BLOCKS += [(3, 0, 0), (3, 1, 0), (4, None, 0), (4, None, HALF)]
+BLOCKS = [(0, lane, k * HALF, lane, k) for k in range(3) for lane in range(2)]
+BLOCKS += [(1, None, 0, 0, 5), (1, None, HALF, 0, 6), (2, 0, 0, 0, 3), (2, 1, 0, 1, 3)]
+BLOCKS += [(3, 0, 0, 0, 4), (3, 1, 0, 1, 4), (4, None, 0, 0, 7), (4, None, HALF, 0, 8)]
 ACROSS = (0, 1, 2, 6, 7, 10, 11)
 
 
 def gather_kernel(
-    valid_ref, own_hbm, other_hbm, lines_hbm,
-    mixture_ref, qkv_ref, *refs,
+    valid_ref, own_hbm, other_hbm, lines_hbm, more_lines_hbm, words_ref, more_words_ref,
+    mixture_ref, qkv_ref, text_ref, kv_ref, *refs,
 ):
     outs, arrays = refs[:5], refs[5:10]
     entry, x_send, x_recv, y_send, y_recv, on_send, on_recv, own_sem, load_sem, out_sem = refs[10:]
-    y, x = lax.axis_index("y"), lax.axis_index("x")
+    y, c, x = (lax.axis_index(axis) for axis in "ycx")
     far_y, far_x = 1 - y, 1 - x
     frames = entry.shape[1]
 
     def place_of(block, at_y, at_x):
-        array, lane, column = BLOCKS[block]
+        array, lane, column, _, _ = BLOCKS[block]
         columns = pl.ds(column, HALF)
         if lane is None:
             return arrays[array].at[at_y, :, at_x, :, columns]
-        return arrays[array].at[at_y, lane, :, at_x, :, columns]
+        return arrays[array].at[at_y, 1 - c if lane else c, :, at_x, :, columns]
 
     def remote(source, target, send, recv, device):
         return pltpu.make_async_remote_copy(
@@ -330,14 +330,15 @@
     to_x, to_y, onward, own = [], [], [], []
     for b in range(count):
         here = place_of(b, y, x)
-        to_x.append(remote(lines_hbm.at[:, b], here, x_send.at[b], x_recv.at[b], {"x": far_x}))
-        to_y.append(remote(lines_hbm.at[:, b], here, y_send.at[b], y_recv.at[b], {"y": far_y}))
+        source = (lines_hbm, more_lines_hbm)[BLOCKS[b][3]].at[:, BLOCKS[b][4]]
+        to_x.append(remote(source, here, x_send.at[b], x_recv.at[b], {"x": far_x}))
+        to_y.append(remote(source, here, y_send.at[b], y_recv.at[b], {"y": far_y}))
         if b in ACROSS:
             there, device = place_of(b, y, far_x), {"y": far_y}
         else:
             there, device = place_of(b, far_y, x), {"x": far_x}
         onward.append(remote(there, there, on_send.at[b], on_recv.at[b], device))
-        own.append(pltpu.make_async_copy(lines_hbm.at[:, b], here, own_sem.at[b]))
+        own.append(pltpu.make_async_copy(source, here, own_sem.at[b]))
 
     def send(blocks):
         for b in blocks:
@@ -363,6 +364,16 @@
     ]
     for load in loads:
         load.start()
+    text_ref[...] = jnp.zeros_like(text_ref)
+    share = arrays[3].shape[-2] // 2
+    for k, ref in enumerate((words_ref, more_words_ref)):
+        height = ref.shape[0]
+        words = ref[...]
+        for device in range(D // (2 * share)):
+            part = words[:, device * share : (device + 1) * share]
+            for side in range(2):
+                at, column = (2 * side + k) * height, (2 * device + side) * share
+                text_ref[at : at + height, column : column + share] = part
     hand_on(range(6))
     send(range(6, count))
     for load in loads:
@@ -385,6 +396,7 @@
 
     hand_on(range(6, count))
     arrive(range(6, count))
+    kv_ref[...] = dot(text_ref[...], arrays[3][...].reshape(D, HALF)).astype(BF16)
     for k in range(1, 5):
         copies.append(pltpu.make_async_copy(arrays[k], outs[k], out_sem.at[k]))
         copies[k].start()
@@ -396,8 +408,9 @@
         onward[b].wait_send()
 
 
-def gather_group(valid, own, other, lines):
-    na, count, rows, _ = lines.shape
+def gather_group(valid, own, other, lines, more_lines, words, more_words):
+    na, _, rows, _ = lines.shape
+    count = len(BLOCKS)
     frames = own.shape[0]
     tall = lambda cols: (2, 2, na, 2, rows, cols)
     wide = (2, na, 2, rows, D)
@@ -408,10 +421,12 @@
         out_shape=[
             jax.ShapeDtypeStruct((2 * frames, HALF), BF16),
             jax.ShapeDtypeStruct((2 * frames, 3 * HALF), BF16),
+            jax.ShapeDtypeStruct((4 * words.shape[0], D), BF16),
+            jax.ShapeDtypeStruct((4 * words.shape[0], HALF), BF16),
         ]
         + [jax.ShapeDtypeStruct(shape, BF16) for shape in shapes],
-        in_specs=[SCALARS] + [ANY] * 3,
-        out_specs=[WHOLE] * 2 + [ANY] * 5,
+        in_specs=[SCALARS] + [ANY] * 4 + [WHOLE] * 2,
+        out_specs=[WHOLE] * 4 + [ANY] * 5,
         scratch_shapes=[pltpu.VMEM(shape, BF16) for shape in shapes]
         + [pltpu.VMEM((2, frames, D), BF16)]
         + [sem(count)] * 7
@@ -420,7 +435,7 @@
             vmem_limit_bytes=56 * 2**20, collective_id=4, has_side_effects=True
         ),
         cost_estimate=LIGHT,
-    )(valid, own, other, lines)
+    )(valid, own, other, lines, more_lines, words, more_words)
 
 
 def ffn_kernel(
@@ -2032,15 +2047,14 @@
     grouped = rows % 16 == 0 and grid.ny == 2 and grid.nb == 2
     if grouped:
         prepare = functools.partial(prepare_kernel, offsets=grid.peers, sizes=(grid.ny, grid.na, grid.nb))
-        five = (5, rows, HALF)
-        five_own, five_other, wide_low, in_blocks = pl.pallas_call(
+        low_own, five_other, in_blocks = pl.pallas_call(
             prepare,
             out_shape=[
                 jax.ShapeDtypeStruct(shape, BF16)
-                for shape in (five, five, (4, rows, HALF), (ranks, rows, 2 * width))
+                for shape in ((9, rows, HALF), (5, rows, HALF), (ranks, rows, 2 * width))
             ],
             in_specs=[SCALARS] + [WHOLE] * 4,
-            out_specs=[WHOLE] * 4,
+            out_specs=[WHOLE] * 3,
             compiler_params=pltpu.CompilerParams(vmem_limit_bytes=40 * 2**20),
         )(spot, qkv_matrix, square_set, ctx_matrix, ff_in)
     else:
@@ -2062,8 +2076,9 @@
             ]
         ).astype(BF16).reshape(ranks, rows, 2 * width)
     five_other = grid.swap(five_other)
-    five_low = jnp.where(core == 0, five_own, five_other)
-    five_high = jnp.where(core == 0, five_other, five_own)
+    if not grouped:
+        five_low = jnp.where(core == 0, five_own, five_other)
+        five_high = jnp.where(core == 0, five_other, five_own)
     lifted = jax.nn.silu(timestep[0].astype(F32)).astype(BF16)
     notes = jnp.concatenate([lifted, norm_gains.astype(BF16).reshape(-1)])
     if grouped:
@@ -2084,12 +2099,6 @@
     gain_rows = gain_rows.reshape(count, 3, rows).transpose(1, 0, 2).reshape(3, D)
     lifted_own = lax.dynamic_slice(notes, (0, device * rows), (count, rows))
     shift_terms = dot(lifted_own, mod_matrix.astype(BF16))
-    text = jnp.concatenate([context[0], grid.swap(context[0])])
-    blank = jnp.zeros((2 * words, count, rows // 2), BF16)
-    text_cut = text.reshape(2 * words, count, rows // 2)
-    text_key = jnp.concatenate([text_cut, blank], axis=-1).reshape(2 * words, -1)
-    text_value = jnp.concatenate([blank, text_cut], axis=-1).reshape(2 * words, -1)
-    text_both = jnp.concatenate([text_key, text_value])
     cotangent_own = (cotangent[0].astype(F32) * keep_rows).astype(BF16)
     if grouped:
         shift_terms = shift_terms.reshape(grid.ny, 2, grid.na, grid.nb, 6 * D // 128, 128)
@@ -2115,15 +2124,13 @@
     pair_lengths = jnp.concatenate([lengths, grid.swap(lengths)])
     columns = HALF // PAIR
     if grouped:
-        blocks = [(five_low, five_high)[lane][k] for k in range(3) for lane in range(2)]
-        blocks += [wide_low[0], wide_low[1], five_low[3], five_high[3]]
-        blocks += [five_low[4], five_high[4], wide_low[2], wide_low[3]]
-        lines = lax.all_gather(jnp.stack(blocks), "z")
+        lines = [lax.all_gather(low_own, "z"), lax.all_gather(five_other, "z")]
         in_lines = lax.all_gather(in_parts.reshape(-1, D), "z")
         down_lines = lax.all_gather(ff_down.astype(BF16), "z")
-        mixture_attn, qkv, matrix_qkv, matrix_out, matrix_query, matrix_ctx, matrix_cross = (
-            gather_group(pair_lengths, *entry_pair, lines)
-        )
+        (
+            mixture_attn, qkv, text_both, kv_cross,
+            matrix_qkv, matrix_out, matrix_query, matrix_ctx, matrix_cross,
+        ) = gather_group(pair_lengths, *entry_pair, *lines, context[0], grid.swap(context[0]))
         matrix_qkv = matrix_qkv.reshape(D, 3 * HALF)
     else:
         first = both(0, 0, 0) + both(1, 0, HALF) + both(2, 0, 2 * HALF)
@@ -2141,6 +2148,13 @@
         rank_in, rank_down = grid.gather_ranks(in_parts, down_part, mine, spot)
         qkv = pair_in(*entry_pair, matrix_qkv, dot)
         mixture_attn = attend(pair_lengths, *((qkv, frames, 0, k * columns) for k in range(3)))
+        text = jnp.concatenate([context[0], grid.swap(context[0])])
+        blank = jnp.zeros((2 * words, count, rows // 2), BF16)
+        text_cut = text.reshape(2 * words, count, rows // 2)
+        text_key = jnp.concatenate([text_cut, blank], axis=-1).reshape(2 * words, -1)
+        text_value = jnp.concatenate([blank, text_cut], axis=-1).reshape(2 * words, -1)
+        text_both = jnp.concatenate([text_key, text_value])
+        kv_cross = dot(text_both, matrix_ctx.reshape(D, HALF)).astype(BF16)
     matrix_out, matrix_cross = matrix_out.reshape(HALF, D), matrix_cross.reshape(HALF, D)
     matrix_query, matrix_ctx = matrix_query.reshape(D, HALF), matrix_ctx.reshape(D, HALF)
 
@@ -2155,7 +2169,6 @@
     entry_cross = (normed_two * gain_rows[1]).astype(BF16)
     cross_pair = [entry_cross, grid.swap(entry_cross)]
     query_cross = pair_in(*cross_pair, matrix_query, dot)
-    kv_cross = dot(text_both, matrix_ctx).astype(BF16)
     cross_parts = ((query_cross, frames, 0, 0), (kv_cross, words, 0, 0), (kv_cross, words, 2, 0))
     mixture_cross = attend(all_words, *cross_parts)
     own, away = pair_out([mixture_cross], matrix_cross, dot)

time: 899 us -> 886 us (0.986)
  local copies, waits for them, and re-layouts: 51.9 us -> 42.2 us
  waiting for transfers between devices: 18.2 us -> 27.7 us
    unnamed x219 -> x209, local copies, waits for them, and re-layouts: 34.3 us -> 30.6 us
  transfers between devices with their start and end apart: 15 -> 16, of which waited for: 8 -> 9; matrix products, arithmetic and copies ran while one was open for 7% -> 5% of each run, Pallas kernels for 34% -> 34%
where the time goes in v4:
time: 886 us; the launch traced here: 877 us
  Pallas kernels  737 us (83%)
  other arithmetic  48.8 us (6%)
  local copies, waits for them, and re-layouts  42.2 us (5%)
  waiting for transfers between devices  27.7 us (3%)
  between operations  16.4 us (2%)
    pallas_call x1, Pallas kernels, reduce_group(): pl.pallas_call(functools.partial(reduce_kernel, plan=plan, inputs=len(arr...  206 us
    pallas_call x1, Pallas kernels, ffn_group(): pl.pallas_call(functools.partial(ffn_group_kernel, chips=chips, peers=pee...  178 us
    pallas_call x1, Pallas kernels, gather_group(): pl.pallas_call(gather_kernel, out_shape=[jax.ShapeDtypeStruct((2 * frames...  145 us
    pallas_call x1, Pallas kernels, sum_shifts(): pl.pallas_call(shift_kernel, out_shape=[jax.ShapeDtypeStruct((rows, 128),...  61.6 us
    pallas_call x2, Pallas kernels, attend_back(): pl.pallas_call(attend_back_kernel, out_shape=[jax.ShapeDtypeStruct((2 * r...  30.8 us
    unnamed x209, local copies, waits for them, and re-layouts  30.6 us
    pallas_call x4, Pallas kernels, pair_out(): pl.pallas_call(functools.partial(pair_out_kernel, product=product), out_s...  26.4 us
    pallas_call x6, Pallas kernels, lamb_terms(): pl.pallas_call(lamb_kernel, out_shape=[full, full, full, jax.ShapeDtypeSt...  26.1 us
  transfers between devices with their start and end apart: 16, of which 9 were waited for; matrix products, arithmetic and copies ran while one was open for 5% of the time, Pallas kernels for 34%

profile of v4, /device:TPU:0, one launch (start us, length us, event | category | flops | bytes accessed | tf_op | source)
XLA Modules:
  0.0 876.7 jit_solution(4672404908696845654)
XLA Ops:
  12.3 2.9 shard_map.450
  22.9 16.0 %shard_map.449 = bf16[2,2,4,2,16,128]{5,4,3,2,1,0:T(8,128)(2,1)} custom-call(bf16[16,128]{1,0:T(8,128)(2,1)} %fusion.42.own_ref), custom_call_target="tpu_custom_call" | custom-call | flops 1048576 | bytes 1048576 | tf_op jit(solution)/shard_map/pallas_call | solution.py:1073
  43.5 61.6 %shard_map.451 = (f32[72,128]{1,0:T(8,128)S(1)}, bf16[8,384,1536]{2,1,0:T(8,128)(2,1)S(1)}, bf16[2,2,2,48,1536]{4,3,2,1,0:T(8,128)(2,1)}) custom-call(f32[2,2,4,2,72,128]{5,4,3,2,1,0:T(8,128)S(1)} %bitcast.243, bf16[384,1536]{1,0:T(8,128)(2,1)S(1)} %fusion.23.cot_hbm, bf16[2,2,2,48,1536]{4,3,2,1,0:T(8,128)(2,1)S(1)} %bitcast.252), custom_call_target="tpu_custom_call" | custom-call | flops 1048576 | bytes 1048576 | tf_op jit(solution)/shard_map/pallas_call | solution.py:1229
  105.0 3.6 copy-done.18
  115.9 8.8 %all-gather.10.cloned.1.call-done = bf16[36,48,768]{2,1,0:T(8,128)(2,1)} async-done(((bf16[9,48,768]{2,1,0:T(8,128)(2,1)}), bf16[36,48,768]{2,1,0:T(8,128)(2,1)}) %all-gather.10.cloned.1.call-update) | async-done | bytes 2654224 | tf_op jit(solution)/shard_map/all_gather | solution.py:2127
  124.8 144.9 %shard_map.452 = (bf16[768,768]{1,0:T(8,128)(2,1)}, bf16[768,2304]{1,0:T(8,128)(2,1)}, bf16[512,1536]{1,0:T(8,128)(2,1)}, bf16[512,768]{1,0:T(8,128)(2,1)}, bf16...) custom-call(s32[2]{0:T(128)} %pad_add_fusion.1.valid_ref, ...), custom_call_target="tpu_custom_call" | custom-call | flops 1048576 | bytes 1048576 | tf_op jit(solution)/shard_map/pallas_call | solution.py:419
  270.9 5.1 shard_map.453
  283.0 2.7 collective-permute-done.5.other_ref.refs_4_
  288.0 11.7 %shard_map.455.refs_0_ = bf16[768,768]{1,0:T(8,128)(2,1)S(1)} custom-call(s32[2]{0:T(128)S(1)} %broadcast_10_valid_ref.2.valid_ref, bf16[768,768]{1,0:T(8,128)(2,1)S(1)} %shard_map.454.query_ref, bf16[512,768]{1,0:T(8,128)(2,1)S(1)} %copy-done.4, bf16[512,768]{1,0:T(8,128)(2,1)S(1)} %copy-done.4), custom_call_target="tpu_custom_call" | custom-call | flops 1048576 | bytes 1048576 | tf_op jit(solution)/shard_map/pallas_call | solution.py:143
  300.8 4.5 shard_map.456
  309.7 3.1 fusion.51
  315.7 177.8 %shard_map.457 = (f32[384,1536]{1,0:T(8,128)}, bf16[768,1536]{1,0:T(8,128)(2,1)}, bf16[4,4,96,1536]{3,2,1,0:T(8,128)(2,1)}, f32[384,1536]{1,0:T(8,128)}, bf16[38...) custom-call(bf16[384,1536]{1,0:T(8,128)(2,1)} %add_convert_fusion.en, ...), custom_call_target="tpu_custom_call" | custom-call | flops 1048576 | bytes 1048576 | tf_op jit(solution)/shard_map/pallas_call | solution.py:1553
  495.3 7.6 fusion.17
  504.3 2.8 collective-permute-done.7.other_ref.refs_2_
  509.4 11.4 %shard_map.459 = (bf16[768,768]{1,0:T(8,128)(2,1)S(1)}, bf16[256,768]{1,0:T(8,128)(2,1)S(1)}, bf16[256,768]{1,0:T(8,128)(2,1)S(1)}) custom-call(s32[2]{0:T(128)S(1)} %broadcast_10_valid_ref.2.valid_ref, bf16[768,768]{1,0:T(8,128)(2,1)S(1)} %copy-done.12, bf16[512,768]{1,0:T(8,128)(2,1)S(1)} %copy-done.4, bf16[512,768]{1,0:T(8,128)(2,1)S(1)} %copy-done.4, ...), custom_call_target="tpu_custom_call" | custom-call | flops 1048576 | bytes 1048576 | tf_op jit(solution)/shard_map/pallas_call | solution.py:157
  522.3 4.6 shard_map.460
  527.1 2.7 collective-permute-done.8
  531.5 3.9 fusion.18
  540.9 19.4 %shard_map.462 = (bf16[768,768]{1,0:T(8,128)(2,1)S(1)}, bf16[768,768]{1,0:T(8,128)(2,1)S(1)}, bf16[768,768]{1,0:T(8,128)(2,1)S(1)}) custom-call(s32[2]{0:T(128)S(1)} %copy-done.61, bf16[768,2304]{1,0:T(8,128)(2,1)} %get-tuple-element.113.query_ref.key_ref.value_ref, bf16[768,2304]{1,0:T(8,128)(2,1)} %get-tuple-element.113.query_ref.key_ref.value_ref, ...), custom_call_target="tpu_custom_call" | custom-call | flops 1048576 | bytes 1048576 | tf_op jit(solution)/shard_map/pallas_call | solution.py:157
  560.4 12.2 %shard_map.463 = (f32[384,1536]{1,0:T(8,128)}, bf16[384,1536]{1,0:T(8,128)(2,1)S(1)}) custom-call(bf16[768,768]{1,0:T(8,128)(2,1)S(1)} %get-tuple-element.114.refs_0_.refs_14_, bf16[768,768]{1,0:T(8,128)(2,1)S(1)} %get-tuple-element.115.refs_1_.refs_15_, bf16[768,768]{1,0:T(8,128)(2,1)S(1)} %get-tuple-element.116.refs_2_.refs_16_, bf16[1536,2304]{1,0:T(8,128)(2,1)} %bitcast.263), custom_call_target="tpu_custom_call" | custom-call | flops 1048576 | bytes 1048576 | tf_op jit(solution)/shard_map/pallas_call | solution.py:1011
  572.9 3.1 maximum_bitcast_fusion.4
  578.6 5.0 multiply_reduce_fusion.2
  585.1 4.4 fusion.29
  589.4 205.8 %shard_map.465 = (bf16[7,2,48,768]{3,2,1,0:T(8,128)(2,1)}, bf16[2,2,4,2,112,128]{5,4,3,2,1,0:T(8,128)(2,1)}, bf16[48,12288]{1,0:T(8,128)(2,1)}, bf16[192,1536]{1,0:T(8,128)(2,1)}, bf16[3,192,1536]{2,1,0:T(8,128)(2,1)}) custom-call(bf16[768,768]{1,0:T(8,128)(2,1)} %copy-done.6, bf16[384,1536]{1,0:T(8,128)(2,1)} %copy-done.5, bf16[384,1536]{1,0:T(8,128)(2,1)} %copy-done.29, ...), custom_call_target="tpu_custom_call" | custom-call | flops 1048576 | bytes 1048576 | tf_op jit(solution)/shard_map/pallas_call | solution.py:909
  795.2 2.8 reshape.509
  810.0 5.4 shard_map.467
  816.4 3.6 shard_map.468
  820.1 3.9 shard_map.471
  824.1 4.6 shard_map.466
  830.2 6.9 shard_map.470
  841.9 16.5 %shard_map.472 = f32[16,128]{1,0:T(8,128)} custom-call(f32[16,128]{1,0:T(8,128)} %pad.10.sums_ref), custom_call_target="tpu_custom_call" | custom-call | flops 1048576 | bytes 1048576 | tf_op jit(solution)/shard_map/pallas_call | solution.py:1672
  861.3 8.4 shard_map.473
  (328 shorter events, 82.7 us)
Async XLA Ops:
  7.2 108.7 %all-gather.12.cloned.1.call-start = ((), (), s32[]{:S(2)}) async-start(), calls=%async_computation.4 | async-start | bytes 1843200 | tf_op jit(solution)/shard_map/all_gather | solution.py:2127
  17.1 1.8 collective-permute-start.2
  18.8 22.8 %copy-start.2 = (f32[48,9216]{1,0:T(8,128)S(1)}, f32[48,9216]{1,0:T(8,128)}, u32[]{:S(2)}) copy-start(f32[48,9216]{1,0:T(8,128)} %refs_0_.1) | copy-start | bytes 5308420
  19.6 105.2 %all-gather.10.cloned.1.call-start = ((), (), s32[]{:S(2)}) async-start(), calls=%async_computation.3 | async-start | bytes 3317760 | tf_op jit(solution)/shard_map/all_gather | solution.py:2127
  20.4 295.4 %all-gather.14.cloned.1.call-start = ((), (), s32[]{:S(2)}) async-start(), calls=%async_computation.5 | async-start | bytes 2949120 | tf_op jit(solution)/shard_map/all_gather | solution.py:2129
  21.3 294.4 %all-gather.8.cloned.1.call-start = ((), (), s32[]{:S(2)}) async-start(), calls=%async_computation.1 | async-start | bytes 5898240 | tf_op jit(solution)/shard_map/all_gather | solution.py:2128
  41.7 68.3 %copy-start.82 = (f32[1536]{0:T(1024)}, f32[1536]{0:T(1024)S(1)}, u32[]{:S(2)}) copy-start(f32[1536]{0:T(1024)S(1)} %mul.251) | copy-start | bytes 18436
  43.2 65.7 %copy-start.13 = (bf16[384,1536]{1,0:T(8,128)(2,1)}, bf16[384,1536]{1,0:T(8,128)(2,1)S(1)}, u32[]{:S(2)}) copy-start(bf16[384,1536]{1,0:T(8,128)(2,1)S(1)} %fusion.23.cot_hbm) | copy-start | bytes 3538948
  43.2 65.4 %copy-start.66 = (bf16[1,384,1536]{2,1,0:T(8,128)(2,1)S(1)}, bf16[1,384,1536]{2,1,0:T(8,128)(2,1)}, u32[]{:S(2)}) copy-start(bf16[1,384,1536]{2,1,0:T(8,128)(2,1)} %param.26) | copy-start | bytes 3538948
  109.4 160.3 %copy-start.93 = (f32[384]{0:T(512)}, f32[384]{0:T(512)S(1)}, u32[]{:S(2)}) copy-start(f32[384]{0:T(512)S(1)} %add_rsqrt_fusion.2) | copy-start | bytes 4612
  111.2 13.6 %copy-start.71 = (bf16[384,1536]{1,0:T(8,128)(2,1)}, bf16[384,1536]{1,0:T(8,128)(2,1)S(1)}, u32[]{:S(2)}) copy-start(bf16[384,1536]{1,0:T(8,128)(2,1)S(1)} %fusion.10.own_hbm.refs_12_) | copy-start | bytes 3538948
  111.2 4.7 collective-permute-start.1
  111.7 477.7 %reduce-scatter.2.cloned.1.call-start = ((), (), s32[]{:S(2)}) async-start(), calls=%async_computation.2 | async-start | bytes 5898240 | tf_op jit(solution)/shard_map/reduce_scatter | solution.py:2238
  111.7 4.1 collective-permute-start.3
  112.0 2.8 collective-permute-start
  276.0 3.2 collective-permute-start.4
  282.8 2.9 collective-permute-start.5
  300.8 12.0 %copy-start.6 = (bf16[768,768]{1,0:T(8,128)(2,1)}, bf16[768,768]{1,0:T(8,128)(2,1)S(1)}, u32[]{:S(2)}) copy-start(bf16[768,768]{1,0:T(8,128)(2,1)S(1)} %shard_map.455.refs_0_) | copy-start | bytes 3538948
  306.7 3.0 collective-permute-start.6
  504.2 2.9 collective-permute-start.7
  526.9 2.9 collective-permute-start.8
  535.7 2.9 collective-permute-start.9
  560.4 12.3 %copy-start.31 = (bf16[768,768]{1,0:T(8,128)(2,1)}, bf16[768,768]{1,0:T(8,128)(2,1)S(1)}, u32[]{:S(2)}) copy-start(bf16[768,768]{1,0:T(8,128)(2,1)S(1)} %get-tuple-element.114.refs_0_.refs_14_) | copy-start | bytes 3538948
  560.4 12.3 %copy-start.32 = (bf16[768,768]{1,0:T(8,128)(2,1)}, bf16[768,768]{1,0:T(8,128)(2,1)S(1)}, u32[]{:S(2)}) copy-start(bf16[768,768]{1,0:T(8,128)(2,1)S(1)} %get-tuple-element.115.refs_1_.refs_15_) | copy-start | bytes 3538948
  560.4 12.3 %copy-start.33 = (bf16[768,768]{1,0:T(8,128)(2,1)}, bf16[768,768]{1,0:T(8,128)(2,1)S(1)}, u32[]{:S(2)}) copy-start(bf16[768,768]{1,0:T(8,128)(2,1)S(1)} %get-tuple-element.116.refs_2_.refs_16_) | copy-start | bytes 3538948
  560.4 18.1 %copy-start.67 = (bf16[1,384,1536]{2,1,0:T(8,128)(2,1)S(1)}, bf16[1,384,1536]{2,1,0:T(8,128)(2,1)}, u32[]{:S(2)}) copy-start(bf16[1,384,1536]{2,1,0:T(8,128)(2,1)} %param.26) | copy-start | bytes 3538948
  560.4 18.1 %copy-start.83 = (f32[1536]{0:T(1024)S(1)}, f32[1536]{0:T(1024)}, u32[]{:S(2)}) copy-start(f32[1536]{0:T(1024)} %copy-done.82) | copy-start | bytes 18436
  560.4 18.1 %copy-start.90 = (f32[384]{0:T(512)S(1)}, f32[384]{0:T(512)}, u32[]{:S(2)}) copy-start(f32[384]{0:T(512)} %copy-done.89) | copy-start | bytes 4612
  572.6 5.9 collective-permute-start.10
  806.2 10.2 %copy-start.50 = (f32[3,48,1536]{2,1,0:T(8,128)S(1)}, f32[3,48,1536]{2,1,0:T(8,128)}, u32[]{:S(2)}) copy-start(f32[3,48,1536]{2,1,0:T(8,128)} %first_ref.1) | copy-start | bytes 2654212
  810.0 20.0 %copy-start.47 = (bf16[48,12288]{1,0:T(8,128)(2,1)S(1)}, bf16[48,12288]{1,0:T(8,128)(2,1)}, u32[]{:S(2)}) copy-start(bf16[48,12288]{1,0:T(8,128)(2,1)} %get-tuple-element.131) | copy-start | bytes 3538948
  830.1 11.1 %copy-start.97 = (f32[4,2]{1,0:T(4,128)S(1)}, f32[4,2]{1,0:T(4,128)}, u32[]{:S(2)}) copy-start(f32[4,2]{1,0:T(4,128)} %pad_bitcast_fusion) | copy-start | bytes 100
  (88 other events, 380.2 us)
Sparse Core Ops, SparseCore 0:
  19.7 44.5 all-gather.11
  66.5 58.2 all-gather.9
  126.9 49.2 all-gather.13
  177.6 88.2 all-gather.7
  493.8 83.2 reduce-scatter.1

commit v5 on v4

--- a/solution.py
+++ b/solution.py
@@ -806,6 +806,41 @@
         if plan[m][0] == "tall":
             core_copy(m).start()
 
+    def rows_back():
+        for copy in in_hops[2]:
+            copy.wait_recv()
+        width = in_own.shape[-1] // 2
+        share = width // na
+        for at_y in range(2):
+            for at_c in range(2):
+                if at_y:
+                    near = in_y[at_c, x]
+                else:
+                    near = in_core[y, x] if at_c else in_own[y, c, x]
+                across = in_x[at_y * 2 + at_c]
+                low = jnp.where(x == 0, near, across)
+                high = jnp.where(x == 0, across, near)
+                rank = lax.rem(y + at_y, 2) * 2 + lax.rem(c + at_c, 2)
+                for half in range(2):
+                    for k in range(na):
+                        at = half * width + k * share
+                        start = pl.multiple_of(half * FF + (rank * na + k) * 2 * share, 128)
+                        in_ref[:, pl.ds(start, 2 * share)] = jnp.concatenate(
+                            [low[:, at : at + share], high[:, at : at + share]], axis=1
+                        )
+        depth = down_ref.shape[0]
+        sums = None
+        for k in range(na):
+            if k:
+                down_copies[k - 1].wait_recv()
+            source = down_in.at[k - 1] if k else down_hbm.at[z]
+            copy = pltpu.make_async_copy(source, left_ref.at[0, pl.ds(0, depth)], down_sem.at[0])
+            copy.start()
+            copy.wait()
+            term = left_ref[0, :depth, :].astype(F32)
+            sums = term if sums is None else sums + term
+        down_ref[...] = sums.astype(BF16)
+
     for m in range(count + 6):
         if m < count:
             for copy in loads(m):
@@ -829,6 +864,8 @@
         for behind, step in ((2, second_step), (4, line_step), (6, last_step)):
             if 0 <= m - behind < count:
                 step(m - behind)
+        if m == count - 1:
+            rows_back()
     order = range(count)
     for m in order:
         if plan[m][0] == "tall":
@@ -841,39 +878,6 @@
         copy.wait_recv()
     small_ref[...] = notes[...]
 
-    for copy in in_hops[2]:
-        copy.wait_recv()
-    width = in_own.shape[-1] // 2
-    share = width // na
-    for at_y in range(2):
-        for at_c in range(2):
-            if at_y:
-                near = in_y[at_c, x]
-            else:
-                near = in_core[y, x] if at_c else in_own[y, c, x]
-            across = in_x[at_y * 2 + at_c]
-            low = jnp.where(x == 0, near, across)
-            high = jnp.where(x == 0, across, near)
-            rank = lax.rem(y + at_y, 2) * 2 + lax.rem(c + at_c, 2)
-            for half in range(2):
-                for k in range(na):
-                    at = half * width + k * share
-                    start = pl.multiple_of(half * FF + (rank * na + k) * 2 * share, 128)
-                    in_ref[:, pl.ds(start, 2 * share)] = jnp.concatenate(
-                        [low[:, at : at + share], high[:, at : at + share]], axis=1
-                    )
-    depth = down_ref.shape[0]
-    sums = None
-    for k in range(na):
-        if k:
-            down_copies[k - 1].wait_recv()
-        source = down_in.at[k - 1] if k else down_hbm.at[z]
-        copy = pltpu.make_async_copy(source, left_ref.at[0, pl.ds(0, depth)], down_sem.at[0])
-        copy.start()
-        copy.wait()
-        term = left_ref[0, :depth, :].astype(F32)
-        sums = term if sums is None else sums + term
-    down_ref[...] = sums.astype(BF16)
 
     for hop in hops + in_hops + [down_copies]:
         for copy in hop:

time: 886 us -> 881 us (level)
  no operation moved by 1% of the time
where the time goes in v5:
time: 881 us; the launch traced here: 872 us
  Pallas kernels  732 us (83%)
  other arithmetic  48.8 us (6%)
  local copies, waits for them, and re-layouts  42.2 us (5%)
  waiting for transfers between devices  27.7 us (3%)
  between operations  16.4 us (2%)
    pallas_call x1, Pallas kernels, reduce_group(): pl.pallas_call(functools.partial(reduce_kernel, plan=plan, inputs=len(arr...  201 us
    pallas_call x1, Pallas kernels, ffn_group(): pl.pallas_call(functools.partial(ffn_group_kernel, chips=chips, peers=pee...  178 us
    pallas_call x1, Pallas kernels, gather_group(): pl.pallas_call(gather_kernel, out_shape=[jax.ShapeDtypeStruct((2 * frames...  145 us
    pallas_call x1, Pallas kernels, sum_shifts(): pl.pallas_call(shift_kernel, out_shape=[jax.ShapeDtypeStruct((rows, 128),...  61.6 us
    pallas_call x2, Pallas kernels, attend_back(): pl.pallas_call(attend_back_kernel, out_shape=[jax.ShapeDtypeStruct((2 * r...  30.8 us
    unnamed x209, local copies, waits for them, and re-layouts  30.6 us
    pallas_call x4, Pallas kernels, pair_out(): pl.pallas_call(functools.partial(pair_out_kernel, product=product), out_s...  26.4 us
    pallas_call x6, Pallas kernels, lamb_terms(): pl.pallas_call(lamb_kernel, out_shape=[full, full, full, jax.ShapeDtypeSt...  26.1 us
  transfers between devices with their start and end apart: 16, of which 9 were waited for; matrix products, arithmetic and copies ran while one was open for 5% of the time, Pallas kernels for 34%

profile of v5, /device:TPU:0, one launch (start us, length us, event | category | flops | bytes accessed | tf_op | source)
XLA Modules:
  0.0 871.7 jit_solution(1517960654866736767)
XLA Ops:
  12.3 2.9 shard_map.450
  22.9 16.0 %shard_map.449 = bf16[2,2,4,2,16,128]{5,4,3,2,1,0:T(8,128)(2,1)} custom-call(bf16[16,128]{1,0:T(8,128)(2,1)} %fusion.42.own_ref), custom_call_target="tpu_custom_call" | custom-call | flops 1048576 | bytes 1048576 | tf_op jit(solution)/shard_map/pallas_call | solution.py:1077
  43.5 61.6 %shard_map.451 = (f32[72,128]{1,0:T(8,128)S(1)}, bf16[8,384,1536]{2,1,0:T(8,128)(2,1)S(1)}, bf16[2,2,2,48,1536]{4,3,2,1,0:T(8,128)(2,1)}) custom-call(f32[2,2,4,2,72,128]{5,4,3,2,1,0:T(8,128)S(1)} %bitcast.243, bf16[384,1536]{1,0:T(8,128)(2,1)S(1)} %fusion.23.cot_hbm, bf16[2,2,2,48,1536]{4,3,2,1,0:T(8,128)(2,1)S(1)} %bitcast.252), custom_call_target="tpu_custom_call" | custom-call | flops 1048576 | bytes 1048576 | tf_op jit(solution)/shard_map/pallas_call | solution.py:1233
  105.0 3.6 copy-done.18
  115.9 8.8 %all-gather.10.cloned.1.call-done = bf16[36,48,768]{2,1,0:T(8,128)(2,1)} async-done(((bf16[9,48,768]{2,1,0:T(8,128)(2,1)}), bf16[36,48,768]{2,1,0:T(8,128)(2,1)}) %all-gather.10.cloned.1.call-update) | async-done | bytes 2654224 | tf_op jit(solution)/shard_map/all_gather | solution.py:2131
  124.8 144.9 %shard_map.452 = (bf16[768,768]{1,0:T(8,128)(2,1)}, bf16[768,2304]{1,0:T(8,128)(2,1)}, bf16[512,1536]{1,0:T(8,128)(2,1)}, bf16[512,768]{1,0:T(8,128)(2,1)}, bf16...) custom-call(s32[2]{0:T(128)} %pad_add_fusion.1.valid_ref, ...), custom_call_target="tpu_custom_call" | custom-call | flops 1048576 | bytes 1048576 | tf_op jit(solution)/shard_map/pallas_call | solution.py:419
  270.9 5.1 shard_map.453
  283.0 2.7 collective-permute-done.5.other_ref.refs_4_
  288.0 11.7 %shard_map.455.refs_0_ = bf16[768,768]{1,0:T(8,128)(2,1)S(1)} custom-call(s32[2]{0:T(128)S(1)} %broadcast_10_valid_ref.2.valid_ref, bf16[768,768]{1,0:T(8,128)(2,1)S(1)} %shard_map.454.query_ref, bf16[512,768]{1,0:T(8,128)(2,1)S(1)} %copy-done.4, bf16[512,768]{1,0:T(8,128)(2,1)S(1)} %copy-done.4), custom_call_target="tpu_custom_call" | custom-call | flops 1048576 | bytes 1048576 | tf_op jit(solution)/shard_map/pallas_call | solution.py:143
  300.8 4.5 shard_map.456
  309.7 3.1 fusion.51
  315.7 177.8 %shard_map.457 = (f32[384,1536]{1,0:T(8,128)}, bf16[768,1536]{1,0:T(8,128)(2,1)}, bf16[4,4,96,1536]{3,2,1,0:T(8,128)(2,1)}, f32[384,1536]{1,0:T(8,128)}, bf16[38...) custom-call(bf16[384,1536]{1,0:T(8,128)(2,1)} %add_convert_fusion.en, ...), custom_call_target="tpu_custom_call" | custom-call | flops 1048576 | bytes 1048576 | tf_op jit(solution)/shard_map/pallas_call | solution.py:1557
  495.3 7.6 fusion.17
  504.3 2.8 collective-permute-done.7.other_ref.refs_2_
  509.4 11.4 %shard_map.459 = (bf16[768,768]{1,0:T(8,128)(2,1)S(1)}, bf16[256,768]{1,0:T(8,128)(2,1)S(1)}, bf16[256,768]{1,0:T(8,128)(2,1)S(1)}) custom-call(s32[2]{0:T(128)S(1)} %broadcast_10_valid_ref.2.valid_ref, bf16[768,768]{1,0:T(8,128)(2,1)S(1)} %copy-done.12, bf16[512,768]{1,0:T(8,128)(2,1)S(1)} %copy-done.4, bf16[512,768]{1,0:T(8,128)(2,1)S(1)} %copy-done.4, ...), custom_call_target="tpu_custom_call" | custom-call | flops 1048576 | bytes 1048576 | tf_op jit(solution)/shard_map/pallas_call | solution.py:157
  522.3 4.6 shard_map.460
  527.1 2.7 collective-permute-done.8
  531.5 3.9 fusion.18
  540.9 19.4 %shard_map.462 = (bf16[768,768]{1,0:T(8,128)(2,1)S(1)}, bf16[768,768]{1,0:T(8,128)(2,1)S(1)}, bf16[768,768]{1,0:T(8,128)(2,1)S(1)}) custom-call(s32[2]{0:T(128)S(1)} %copy-done.61, bf16[768,2304]{1,0:T(8,128)(2,1)} %get-tuple-element.113.query_ref.key_ref.value_ref, bf16[768,2304]{1,0:T(8,128)(2,1)} %get-tuple-element.113.query_ref.key_ref.value_ref, ...), custom_call_target="tpu_custom_call" | custom-call | flops 1048576 | bytes 1048576 | tf_op jit(solution)/shard_map/pallas_call | solution.py:157
  560.4 12.2 %shard_map.463 = (f32[384,1536]{1,0:T(8,128)}, bf16[384,1536]{1,0:T(8,128)(2,1)S(1)}) custom-call(bf16[768,768]{1,0:T(8,128)(2,1)S(1)} %get-tuple-element.114.refs_0_.refs_14_, bf16[768,768]{1,0:T(8,128)(2,1)S(1)} %get-tuple-element.115.refs_1_.refs_15_, bf16[768,768]{1,0:T(8,128)(2,1)S(1)} %get-tuple-element.116.refs_2_.refs_16_, bf16[1536,2304]{1,0:T(8,128)(2,1)} %bitcast.263), custom_call_target="tpu_custom_call" | custom-call | flops 1048576 | bytes 1048576 | tf_op jit(solution)/shard_map/pallas_call | solution.py:1015
  572.9 3.1 maximum_bitcast_fusion.4
  578.6 5.0 multiply_reduce_fusion.2
  585.1 4.4 fusion.29
  589.4 201.5 %shard_map.465 = (bf16[7,2,48,768]{3,2,1,0:T(8,128)(2,1)}, bf16[2,2,4,2,112,128]{5,4,3,2,1,0:T(8,128)(2,1)}, bf16[48,12288]{1,0:T(8,128)(2,1)}, bf16[192,1536]{1,0:T(8,128)(2,1)}, bf16[3,192,1536]{2,1,0:T(8,128)(2,1)}) custom-call(bf16[768,768]{1,0:T(8,128)(2,1)} %copy-done.6, bf16[384,1536]{1,0:T(8,128)(2,1)} %copy-done.5, bf16[384,1536]{1,0:T(8,128)(2,1)} %copy-done.29, ...), custom_call_target="tpu_custom_call" | custom-call | flops 1048576 | bytes 1048576 | tf_op jit(solution)/shard_map/pallas_call | solution.py:913
  790.9 2.8 reshape.509
  805.7 5.4 shard_map.467
  812.1 3.6 shard_map.468
  815.8 3.9 shard_map.471
  819.8 4.6 shard_map.466
  825.9 6.9 shard_map.470
  837.6 15.8 %shard_map.472 = f32[16,128]{1,0:T(8,128)} custom-call(f32[16,128]{1,0:T(8,128)} %pad.10.sums_ref), custom_call_target="tpu_custom_call" | custom-call | flops 1048576 | bytes 1048576 | tf_op jit(solution)/shard_map/pallas_call | solution.py:1676
  856.3 8.4 shard_map.473
  (328 shorter events, 82.7 us)
Async XLA Ops:
  7.2 108.7 %all-gather.12.cloned.1.call-start = ((), (), s32[]{:S(2)}) async-start(), calls=%async_computation.4 | async-start | bytes 1843200 | tf_op jit(solution)/shard_map/all_gather | solution.py:2131
  17.1 1.8 collective-permute-start.2
  18.8 22.8 %copy-start.2 = (f32[48,9216]{1,0:T(8,128)S(1)}, f32[48,9216]{1,0:T(8,128)}, u32[]{:S(2)}) copy-start(f32[48,9216]{1,0:T(8,128)} %refs_0_.1) | copy-start | bytes 5308420
  19.6 105.2 %all-gather.10.cloned.1.call-start = ((), (), s32[]{:S(2)}) async-start(), calls=%async_computation.3 | async-start | bytes 3317760 | tf_op jit(solution)/shard_map/all_gather | solution.py:2131
  20.4 295.4 %all-gather.14.cloned.1.call-start = ((), (), s32[]{:S(2)}) async-start(), calls=%async_computation.5 | async-start | bytes 2949120 | tf_op jit(solution)/shard_map/all_gather | solution.py:2133
  21.3 294.4 %all-gather.8.cloned.1.call-start = ((), (), s32[]{:S(2)}) async-start(), calls=%async_computation.1 | async-start | bytes 5898240 | tf_op jit(solution)/shard_map/all_gather | solution.py:2132
  41.7 68.3 %copy-start.82 = (f32[1536]{0:T(1024)}, f32[1536]{0:T(1024)S(1)}, u32[]{:S(2)}) copy-start(f32[1536]{0:T(1024)S(1)} %mul.251) | copy-start | bytes 18436
  43.2 65.7 %copy-start.13 = (bf16[384,1536]{1,0:T(8,128)(2,1)}, bf16[384,1536]{1,0:T(8,128)(2,1)S(1)}, u32[]{:S(2)}) copy-start(bf16[384,1536]{1,0:T(8,128)(2,1)S(1)} %fusion.23.cot_hbm) | copy-start | bytes 3538948
  43.2 65.4 %copy-start.66 = (bf16[1,384,1536]{2,1,0:T(8,128)(2,1)S(1)}, bf16[1,384,1536]{2,1,0:T(8,128)(2,1)}, u32[]{:S(2)}) copy-start(bf16[1,384,1536]{2,1,0:T(8,128)(2,1)} %param.26) | copy-start | bytes 3538948
  109.4 160.3 %copy-start.93 = (f32[384]{0:T(512)}, f32[384]{0:T(512)S(1)}, u32[]{:S(2)}) copy-start(f32[384]{0:T(512)S(1)} %add_rsqrt_fusion.2) | copy-start | bytes 4612
  111.2 13.6 %copy-start.71 = (bf16[384,1536]{1,0:T(8,128)(2,1)}, bf16[384,1536]{1,0:T(8,128)(2,1)S(1)}, u32[]{:S(2)}) copy-start(bf16[384,1536]{1,0:T(8,128)(2,1)S(1)} %fusion.10.own_hbm.refs_12_) | copy-start | bytes 3538948
  111.2 4.7 collective-permute-start.1
  111.7 477.7 %reduce-scatter.2.cloned.1.call-start = ((), (), s32[]{:S(2)}) async-start(), calls=%async_computation.2 | async-start | bytes 5898240 | tf_op jit(solution)/shard_map/reduce_scatter | solution.py:2242
  111.7 4.1 collective-permute-start.3
  112.0 2.8 collective-permute-start
  276.0 3.2 collective-permute-start.4
  282.8 2.9 collective-permute-start.5
  300.8 12.0 %copy-start.6 = (bf16[768,768]{1,0:T(8,128)(2,1)}, bf16[768,768]{1,0:T(8,128)(2,1)S(1)}, u32[]{:S(2)}) copy-start(bf16[768,768]{1,0:T(8,128)(2,1)S(1)} %shard_map.455.refs_0_) | copy-start | bytes 3538948
  306.7 3.0 collective-permute-start.6
  504.2 2.9 collective-permute-start.7
  526.9 2.9 collective-permute-start.8
  535.7 2.9 collective-permute-start.9
  560.4 12.3 %copy-start.31 = (bf16[768,768]{1,0:T(8,128)(2,1)}, bf16[768,768]{1,0:T(8,128)(2,1)S(1)}, u32[]{:S(2)}) copy-start(bf16[768,768]{1,0:T(8,128)(2,1)S(1)} %get-tuple-element.114.refs_0_.refs_14_) | copy-start | bytes 3538948
  560.4 12.3 %copy-start.32 = (bf16[768,768]{1,0:T(8,128)(2,1)}, bf16[768,768]{1,0:T(8,128)(2,1)S(1)}, u32[]{:S(2)}) copy-start(bf16[768,768]{1,0:T(8,128)(2,1)S(1)} %get-tuple-element.115.refs_1_.refs_15_) | copy-start | bytes 3538948
  560.4 12.3 %copy-start.33 = (bf16[768,768]{1,0:T(8,128)(2,1)}, bf16[768,768]{1,0:T(8,128)(2,1)S(1)}, u32[]{:S(2)}) copy-start(bf16[768,768]{1,0:T(8,128)(2,1)S(1)} %get-tuple-element.116.refs_2_.refs_16_) | copy-start | bytes 3538948
  560.4 18.1 %copy-start.67 = (bf16[1,384,1536]{2,1,0:T(8,128)(2,1)S(1)}, bf16[1,384,1536]{2,1,0:T(8,128)(2,1)}, u32[]{:S(2)}) copy-start(bf16[1,384,1536]{2,1,0:T(8,128)(2,1)} %param.26) | copy-start | bytes 3538948
  560.4 18.1 %copy-start.83 = (f32[1536]{0:T(1024)S(1)}, f32[1536]{0:T(1024)}, u32[]{:S(2)}) copy-start(f32[1536]{0:T(1024)} %copy-done.82) | copy-start | bytes 18436
  560.4 18.1 %copy-start.90 = (f32[384]{0:T(512)S(1)}, f32[384]{0:T(512)}, u32[]{:S(2)}) copy-start(f32[384]{0:T(512)} %copy-done.89) | copy-start | bytes 4612
  572.6 5.9 collective-permute-start.10
  801.9 10.2 %copy-start.50 = (f32[3,48,1536]{2,1,0:T(8,128)S(1)}, f32[3,48,1536]{2,1,0:T(8,128)}, u32[]{:S(2)}) copy-start(f32[3,48,1536]{2,1,0:T(8,128)} %first_ref.1) | copy-start | bytes 2654212
  805.7 20.0 %copy-start.47 = (bf16[48,12288]{1,0:T(8,128)(2,1)S(1)}, bf16[48,12288]{1,0:T(8,128)(2,1)}, u32[]{:S(2)}) copy-start(bf16[48,12288]{1,0:T(8,128)(2,1)} %get-tuple-element.131) | copy-start | bytes 3538948
  825.8 11.1 %copy-start.97 = (f32[4,2]{1,0:T(4,128)S(1)}, f32[4,2]{1,0:T(4,128)}, u32[]{:S(2)}) copy-start(f32[4,2]{1,0:T(4,128)} %pad_bitcast_fusion) | copy-start | bytes 100
  (88 other events, 380.2 us)
Sparse Core Ops, SparseCore 0:
  19.7 44.5 all-gather.11
  66.5 58.2 all-gather.9
  126.9 49.2 all-gather.13
  177.6 88.2 all-gather.7
  493.8 83.2 reduce-scatter.1
